TPU v7x, 256 devices: a whole 4x4x8 slice. The times are simulated.
256 devices in a mesh: lat: 8 (over x_hi, y), lon: 32 (over z, x_lo, core).
Axes of the slice: x: 4 (x_hi: 2, x_lo: 2; x = x_hi * 2 + x_lo), y: 4, z: 8, core: 2. Of those that a mesh axis runs over, the one named last changes fastest.
Arguments:
- tokens: bfloat16 [4, 48, 384, 512], P(None, 'lat', 'lon'), may hold values from -6 to 6
- weights: bfloat16 [2048, 512], replicated, may hold values from -1 to 1, as said below
- out_grad: bfloat16 [4, 48, 384, 512], P(None, 'lat', 'lon'), may hold values from -6 to 6
Outputs:
- mixed: bfloat16 [4, 48, 384, 512], P(None, 'lat', 'lon')
- token_grads: bfloat16 [4, 48, 384, 512], P(None, 'lat', 'lon')
- weight_grads: float32 [2048, 512], P(('lat', 'lon'))
Inputs may be any that keep to these rules, and one draw needn't show every extreme that they name: Rows 0 to 511 of weights give queries, the next 512 keys, the next 512 values, the last 512 the output projection.
All inputs are finite; a program needn't handle non-finite values.
Results may differ from a plain program's by a relative error of at most 0.0091.
Values may be sent and summed in bfloat16 or wider, within the bound.
No kernel may reach another device: no remote copies, remote signals or barrier semaphores. Data moves between devices by JAX's collectives and lax.ppermute only.
A program may use at most 128 MiB of HBM per device.

v0:
```python
import jax
import jax.numpy as jnp
from jax import lax
from jax.sharding import PartitionSpec as P

HEADS = 8
WIN_LEV = 2
WIN_LAT = 6
WIN_LON = 12


epsilon = 1e-05
masked_score = -1e30


def padded(cells, sides, width, closed):
    for axis, dim in sides:
        count = lax.axis_size(axis)
        ends = count if closed else count - 1
        head = lax.slice_in_dim(cells, 0, width, axis=dim)
        tail = lax.slice_in_dim(cells, cells.shape[dim] - width, cells.shape[dim], axis=dim)
        cells = jnp.concatenate(
            [
                lax.ppermute(tail, axis, [(i, (i + 1) % count) for i in range(ends)]),
                cells,
                lax.ppermute(head, axis, [((i + 1) % count, i) for i in range(ends)]),
            ],
            axis=dim,
        )
    return cells


def normalize(values):
    average = jnp.mean(values, axis=-1, keepdims=True)
    centred = values - average
    inverse = lax.rsqrt(jnp.mean(centred * centred, axis=-1, keepdims=True) + epsilon)
    return (centred * inverse, inverse)


def product(form, left, right):
    return jnp.einsum(form, left, right, preferred_element_type=jnp.float32)


def window_pass(query, keys, values, ctx_grad, key_valid):
    score_scale = query.shape[-1] ** (-0.5)
    scores = product("whqe,whke->whqk", query, keys) * score_scale
    scores = jnp.where(key_valid[:, None, None, :], scores, masked_score)
    peak = jnp.max(scores, axis=-1, keepdims=True)
    raised = jnp.exp(scores - peak)
    probs = raised / jnp.sum(raised, axis=-1, keepdims=True)
    prob_weights = probs.astype(jnp.bfloat16)
    context = product("whqk,whke->whqe", prob_weights, values).astype(jnp.bfloat16)
    prob_grad = product("whqe,whke->whqk", ctx_grad, values)
    value_grad = product("whqk,whqe->whke", prob_weights, ctx_grad)
    score_grad = (
        probs * (prob_grad - jnp.sum(prob_grad * probs, axis=-1, keepdims=True)) * score_scale
    ).astype(jnp.bfloat16)
    query_grad = product("whqk,whke->whqe", score_grad, keys)
    key_grad = product("whqk,whqe->whke", score_grad, query)
    return (context, query_grad, key_grad, value_grad)


def grouped_pass(query_w, keys_w, values_w, ctx_w, key_valid, groups):

    def regroup(block):
        return block.reshape((groups, block.shape[0] // groups) + block.shape[1:])

    def window_step(packed):
        return window_pass(packed[0], packed[1], packed[2], packed[3], packed[4])

    results = lax.map(
        window_step,
        (regroup(query_w), regroup(keys_w), regroup(values_w), regroup(ctx_w), regroup(key_valid)),
    )
    return tuple((part.reshape((-1,) + part.shape[2:]) for part in results))


def windows_of(field, head_count, lev_win):
    level_num, lat_num, lon_num, feat_num = field.shape
    shaped = field.reshape(
        level_num // lev_win,
        lev_win,
        lat_num // WIN_LAT,
        WIN_LAT,
        lon_num // WIN_LON,
        WIN_LON,
        head_count,
        feat_num // head_count,
    )
    shaped = shaped.transpose(0, 2, 4, 6, 1, 3, 5, 7)
    return shaped.reshape(-1, head_count, lev_win * WIN_LAT * WIN_LON, feat_num // head_count)


def field_of(blocks, level_num, lat_num, lon_num, lev_win):
    head_count = blocks.shape[1]
    head_size = blocks.shape[3]
    shaped = blocks.reshape(
        level_num // lev_win,
        lat_num // WIN_LAT,
        lon_num // WIN_LON,
        head_count,
        lev_win,
        WIN_LAT,
        WIN_LON,
        head_size,
    )
    shaped = shaped.transpose(0, 4, 1, 5, 2, 6, 3, 7)
    return shaped.reshape(level_num, lat_num, lon_num, head_count * head_size)


def spread(field):
    beside_all = padded(field, (("lon", 2),), WIN_LON // 2, True)
    return padded(beside_all, (("lat", 1),), WIN_LAT // 2, False)


def gather_back(wide):
    lat_rim = WIN_LAT // 2
    lon_rim = WIN_LON // 2
    strips = jnp.concatenate([wide[:, :lat_rim], wide[:, -lat_rim:]], axis=1)
    returned = padded(strips.astype(jnp.bfloat16), (("lat", 1),), lat_rim, False).astype(
        strips.dtype
    )
    middle = wide[:, lat_rim:-lat_rim]
    inner_rows = middle.shape[1]
    middle = middle + jnp.pad(
        returned[:, :lat_rim], ((0, 0), (0, inner_rows - lat_rim), (0, 0), (0, 0))
    )
    middle = middle + jnp.pad(
        returned[:, -lat_rim:], ((0, 0), (inner_rows - lat_rim, 0), (0, 0), (0, 0))
    )
    side_strips = jnp.concatenate([middle[:, :, :lon_rim], middle[:, :, -lon_rim:]], axis=2)
    side_returned = padded(side_strips.astype(jnp.bfloat16), (("lon", 2),), lon_rim, True).astype(
        side_strips.dtype
    )
    inner = middle[:, :, lon_rim:-lon_rim]
    inner_cols = inner.shape[2]
    inner = inner + jnp.pad(
        side_returned[:, :, :lon_rim], ((0, 0), (0, 0), (0, inner_cols - lon_rim), (0, 0))
    )
    inner = inner + jnp.pad(
        side_returned[:, :, -lon_rim:], ((0, 0), (0, 0), (inner_cols - lon_rim, 0), (0, 0))
    )
    return inner


def body(tokens, weights, out_grad):
    level_num, lat_num, lon_num, feat_num = tokens.shape
    lev_pad = WIN_LEV // 2
    lat_rim = WIN_LAT // 2
    lon_rim = WIN_LON // 2
    wide_lat = lat_num + 2 * lat_rim
    wide_lon = lon_num + 2 * lon_rim
    x_float = tokens.astype(jnp.float32)
    normed_exact, inverse = normalize(x_float)
    normed = normed_exact.astype(jnp.bfloat16)
    flat_normed = normed.reshape(-1, feat_num)
    w_query = weights[:feat_num]
    w_keyval = weights[feat_num : 3 * feat_num]
    w_proj = weights[: 3 * feat_num]
    w_out = weights[3 * feat_num :]
    flat_grad = out_grad.reshape(-1, feat_num)
    rim_pads = ((0, 0), (lat_rim, lat_rim), (lon_rim, lon_rim), (0, 0))
    query = jnp.dot(flat_normed, w_query.T, preferred_element_type=jnp.float32).astype(jnp.bfloat16)
    query = query.reshape(level_num, lat_num, lon_num, feat_num)
    wide_normed = spread(normed)
    wide_keyval = jnp.dot(
        wide_normed.reshape(-1, feat_num), w_keyval.T, preferred_element_type=jnp.float32
    ).astype(jnp.bfloat16)
    wide_keyval = wide_keyval.reshape(level_num, wide_lat, wide_lon, 2 * feat_num)
    ctx_grad = jnp.dot(flat_grad, w_out, preferred_element_type=jnp.float32).astype(jnp.bfloat16)
    ctx_grad = ctx_grad.reshape(level_num, lat_num, lon_num, feat_num)
    wide_query = jnp.pad(query, rim_pads)
    wide_ctx = jnp.pad(ctx_grad, rim_pads)
    lat_index = lax.axis_index("lat") * lat_num - lat_rim + jnp.arange(wide_lat, dtype=jnp.int32)
    lat_ok = (lat_index >= 0) & (lat_index < lax.axis_size("lat") * lat_num)
    low_count = WIN_LEV - lev_pad
    spans = [
        (0, low_count, low_count),
        (low_count, level_num - lev_pad, WIN_LEV),
        (level_num - lev_pad, level_num, lev_pad),
    ]
    context_parts = []
    query_parts = []
    keyval_parts = []
    for start, finish, lev_win in spans:
        count = finish - start
        valid = lat_ok[None, :, None] & jnp.ones((count, 1, wide_lon), dtype=jnp.bool_)
        key_valid = windows_of(valid[..., None], 1, lev_win)[:, 0, :, 0]
        piece_kv = wide_keyval[start:finish]
        context_w, query_grad_w, key_grad_w, value_grad_w = grouped_pass(
            windows_of(wide_query[start:finish], HEADS, lev_win),
            windows_of(piece_kv[..., :feat_num], HEADS, lev_win),
            windows_of(piece_kv[..., feat_num:], HEADS, lev_win),
            windows_of(wide_ctx[start:finish], HEADS, lev_win),
            key_valid,
            count // lev_win,
        )
        context_parts.append(field_of(context_w, count, wide_lat, wide_lon, lev_win))
        query_parts.append(field_of(query_grad_w, count, wide_lat, wide_lon, lev_win))
        keyval_parts.append(
            jnp.concatenate(
                [
                    field_of(key_grad_w, count, wide_lat, wide_lon, lev_win),
                    field_of(value_grad_w, count, wide_lat, wide_lon, lev_win),
                ],
                axis=-1,
            )
        )
    own_part = (slice(None), slice(lat_rim, lat_rim + lat_num), slice(lon_rim, lon_rim + lon_num))
    context = jnp.concatenate(context_parts, axis=0)[own_part]
    query_grad = jnp.concatenate(query_parts, axis=0)[own_part].astype(jnp.bfloat16)
    wide_kv_grad = jnp.concatenate(keyval_parts, axis=0)
    keyval_grad = gather_back(wide_kv_grad).astype(jnp.bfloat16)
    flat_context = context.reshape(-1, feat_num)
    mixed = (
        x_float
        + jnp.dot(flat_context, w_out.T, preferred_element_type=jnp.float32).reshape(tokens.shape)
    ).astype(jnp.bfloat16)
    proj_grad = jnp.concatenate([query_grad, keyval_grad], axis=-1).reshape(-1, 3 * feat_num)
    grad_term = jnp.concatenate(
        [
            jnp.einsum("tk,td->kd", proj_grad, flat_normed, preferred_element_type=jnp.float32),
            jnp.einsum("tk,td->kd", flat_grad, flat_context, preferred_element_type=jnp.float32),
        ],
        axis=0,
    )
    weight_grads = lax.psum_scatter(grad_term, ("lat", "lon"), scatter_dimension=0, tiled=True)
    normed_grad = jnp.dot(proj_grad, w_proj, preferred_element_type=jnp.float32).reshape(
        tokens.shape
    )
    correction = (
        normed_grad
        - jnp.mean(normed_grad, axis=-1, keepdims=True)
        - normed_exact * jnp.mean(normed_grad * normed_exact, axis=-1, keepdims=True)
    )
    token_grads = (out_grad.astype(jnp.float32) + inverse * correction).astype(jnp.bfloat16)
    return (mixed, token_grads, weight_grads)


def solution(mesh):
    return jax.shard_map(
        body,
        mesh=mesh,
        in_specs=(P(None, "lat", "lon", None), P(), P(None, "lat", "lon", None)),
        out_specs=(
            P(None, "lat", "lon", None),
            P(None, "lat", "lon", None),
            P(("lat", "lon"), None),
        ),
        check_vma=False,
    )
```

profile of v0, /device:TPU:2, one launch (start us, length us, event | category | flops | bytes accessed | tf_op | source)
XLA Modules:
  0.0 1474.6 jit_solution(10478440077561851676)
XLA Ops:
  10.9 1.7 collective-permute-start.1
  12.9 1.4 convolution_convert_fusion.7
  17.2 4.2 collective-permute-start.2
  27.9 1.6 copy.157
  33.5 1.8 copy.131
  35.3 1.5 pad_maximum_fusion.3
  37.0 1.4 convolution_convert_fusion
  41.7 1.6 fusion.132
  43.3 1.7 fusion.127
  45.0 3.8 convolution_convert_fusion.2
  48.8 3.9 fusion.53
  52.7 2.5 convolution_convert_fusion.4
  55.2 1.5 fusion.83
  58.8 1.5 fusion.130
  60.3 1.8 fusion.129
  62.1 2.5 convolution_convert_fusion.5
  64.5 1.4 fusion.86
  66.8 1.6 copy.132
  70.4 3.0 fusion.131
  73.5 5.4 fusion.128
  78.8 9.4 fusion.31
  88.2 9.4 fusion.11
  97.6 4.7 fusion.48
  105.6 3.0 fusion.59
  112.0 2.3 copy.184
  114.3 1.6 copy.185
  116.0 2.0 reshape.202
  118.0 2.3 copy.180
  120.3 1.6 copy.181
  122.0 2.4 reshape.201
  124.4 1.6 fusion.115
  126.6 4.7 collective-permute-start.4
  132.7 1.6 convolution_convert_fusion.1
  134.2 9.3 collective-permute-done.4
  143.6 4.7 collective-permute-done.5
  152.7 3.8 convolution_convert_fusion.3
  158.0 1.4 copy.168
  160.5 1.4 copy.127
  165.6 1.9 copy.136
  168.7 2.7 reshape.186
  171.3 1.8 copy.161
  174.3 2.8 reshape.196
  177.1 1.4 convolution_bitcast_fusion.1
  179.8 2.0 maximum_convert_fusion.1
  184.6 2.4 pad_maximum_fusion
  188.1 1.6 fusion.46
  190.7 2.3 fusion.116
  194.3 1273.3 %reduce-scatter.2.cloned.1.call-done = f32[8,512]{1,0:T(8,128)} async-done(((f32[2048,512]{1,0:T(8,128)}), f32[8,512]{1,0:T(8,128)}) %reduce-scatter.2.cloned.1.call-update) | async-done | bytes 16400 | tf_op jit(solution)/shard_map/reduce_scatter | solution.py:227
  (215 shorter events, 53.9 us)
Async XLA Ops:
  7.2 5.6 copy-start.9
  7.2 1460.4 %reduce-scatter.2.cloned.1.call-start = ((), (), s32[]{:S(2)}) async-start(), calls=%async_computation.1 | async-start | bytes 4210688 | tf_op jit(solution)/shard_map/reduce_scatter | solution.py:227
  9.6 3.1 copy-start.35
  10.8 5.2 collective-permute-start
  10.9 5.1 collective-permute-start.1
  17.2 18.1 %collective-permute-start.2 = (bf16[4,3,24,512]{3,2,1,0:T(8,128)(2,1)}, bf16[4,3,24,512]{3,2,1,0:T(8,128)(2,1)}, u32[]{:S(2)}, u32[]{:S(2)}) collective-permute-start(bf16[4,3,24,512]{3,2,1,0:T(8,128)(2,1)} %get-tuple-element.108), channel_id=1, source_target_pairs={{0,32},{32,64},{64,96},{96,128},{128,160},{160,192},{192,224},{1,3... | collective-permute-start | bytes 884744 | tf_op jit(solution)/shard_map/ppermute | solution.py:24
  21.4 13.9 collective-permute-start.3
  35.2 1.8 copy-start.42
  41.0 2.2 copy-start.30
  41.1 2.2 copy-start.41
  52.7 2.5 copy-start.44
  57.5 2.8 copy-start.26
  57.9 2.4 copy-start.28
  62.1 43.6 %copy-start.45 = (f32[4,8,72]{2,1,0:T(8,128)}, f32[4,8,72]{2,1,0:T(8,128)S(1)}, u32[]{:S(2)}) copy-start(f32[4,8,72]{2,1,0:T(8,128)S(1)} %get-tuple-element.130) | copy-start | bytes 27652
  62.1 2.5 copy-start.43
  70.4 3.0 copy-start.7
  70.4 3.0 copy-start.17
  70.4 3.0 copy-start.38
  78.8 18.7 %copy-start.47 = (f32[4,8,144]{2,1,0:T(8,128)}, f32[4,8,144]{2,1,0:T(8,128)S(1)}, u32[]{:S(2)}) copy-start(f32[4,8,144]{2,1,0:T(8,128)S(1)} %get-tuple-element.128) | copy-start | bytes 55300
  97.6 4.7 copy-start.19
  105.6 3.0 copy-start.20
  122.0 2.4 copy-start
  122.0 2.4 copy-start.1
  124.4 1.6 copy-start.2
  124.4 1.6 copy-start.3
  124.4 8.3 slice-start.1
  126.0 6.6 slice-start.2
  126.5 6.2 copy-start.8
  126.5 6.2 copy-start.48
  126.6 17.0 %collective-permute-start.4 = (bf16[4,3,24,1024]{3,2,1,0:T(8,128)(2,1)S(1)}, bf16[4,3,24,1024]{3,2,1,0:T(8,128)(2,1)S(1)}, u32[]{:S(2)}, u32[]{:S(2)}) collective-permute-start(bf16[4,3,24,1024]{3,2,1,0:T(8,128)(2,1)S(1)} %get-tuple-element.86), channel_id=1, source_target_pairs={{0,32},{32,64},{64,96},{96,128},{128,160},{160,192},{192,224},{1,3... | collective-permute-start | bytes 1769480 | tf_op jit(solution)/shard_map/ppermute | solution.py:24
  131.3 17.0 %collective-permute-start.5 = (bf16[4,3,24,1024]{3,2,1,0:T(8,128)(2,1)S(1)}, bf16[4,3,24,1024]{3,2,1,0:T(8,128)(2,1)S(1)}, u32[]{:S(2)}, u32[]{:S(2)}) collective-permute-start(bf16[4,3,24,1024]{3,2,1,0:T(8,128)(2,1)S(1)} %get-tuple-element.87), channel_id=1, source_target_pairs={{32,0},{64,32},{96,64},{128,96},{160,128},{192,160},{224,192},{33,... | collective-permute-start | bytes 1769480 | tf_op jit(solution)/shard_map/ppermute | solution.py:26
  149.9 2.8 copy-start.27
  149.9 2.8 copy-start.46
  151.0 27.5 %collective-permute-start.6 = (bf16[4,6,6,1024]{3,2,1,0:T(8,128)(2,1)}, bf16[4,6,6,1024]{3,2,1,0:T(8,128)(2,1)}, u32[]{:S(2)}, u32[]{:S(2)}) collective-permute-start(bf16[4,6,6,1024]{3,2,1,0:T(8,128)(2,1)} %get-tuple-element.100), channel_id=1, source_target_pairs={{0,1},{1,2},{2,3},{3,4},{4,5},{5,6},{6,7},{7,8},{8,9},{9,10},{10,1... | collective-permute-start | bytes 884744 | tf_op jit(solution)/shard_map/ppermute | solution.py:24
  151.9 4.7 copy-start.25
  151.9 26.6 %collective-permute-start.7 = (bf16[4,6,6,1024]{3,2,1,0:T(8,128)(2,1)}, bf16[4,6,6,1024]{3,2,1,0:T(8,128)(2,1)}, u32[]{:S(2)}, u32[]{:S(2)}) collective-permute-start(bf16[4,6,6,1024]{3,2,1,0:T(8,128)(2,1)} %get-tuple-element.101), channel_id=1, source_target_pairs={{1,0},{2,1},{3,2},{4,3},{5,4},{6,5},{7,6},{8,7},{9,8},{10,9},{11,1... | collective-permute-start | bytes 884744 | tf_op jit(solution)/shard_map/ppermute | solution.py:26
  174.3 2.8 copy-start.10
  174.3 2.8 copy-start.11
  174.3 2.8 copy-start.14
  179.8 2.0 copy-start.39
  181.9 1.6 copy-start.4
  181.9 1.6 copy-start.23
  181.9 1.6 copy-start.31
  188.1 2.6 copy-start.22
  188.1 2.6 copy-start.24
  188.1 2.6 copy-start.32
  188.1 2.6 copy-start.34
  188.1 2.6 copy-start.37
  (13 other events, 15.5 us)
Sparse Core Ops, SparseCore 0:
  187.2 1280.3 reduce-scatter.1
where the time goes:
time: 1490 us; the launch traced here: 1470 us
  waiting for transfers between devices  1290 us (87%)
  matrix products  73 us (5%)
  local copies, waits for them, and re-layouts  68.4 us (5%)
  other arithmetic  15.3 us (1%)
  between operations  15.3 us (1%)
  starting transfers between devices  15.1 us (1%)
    reduce_scatter x1, waiting for transfers between devices, body(): lax.psum_scatter(grad_term, ('lat', 'lon'), scatter_dimension=0, tiled=True)  1270 us
    dot_general x15, matrix products, product(): return jnp.einsum(form, left, right, preferred_element_type=jnp.float32)  53.5 us
  transfers between devices with their start and end apart: 9, of which 4 were waited for; matrix products, arithmetic and copies ran while one was open for 3% of the time, Pallas kernels for 0%

commit v1 on v0

v1 whole, which is shorter than its diff:
```python
import jax
import jax.numpy as jnp
from jax import lax
from jax.experimental import pallas as pl
from jax.experimental.pallas import tpu as pltpu
from jax.sharding import Mesh, PartitionSpec as P

HEADS = 8
FEAT = 512
HEAD = 64
WIN = 144
epsilon = 1e-05
masked_score = -1e30
LAT = ("xh", "y")
LON = ("zh", "zl", "xl", "c")
ALL = LAT + LON
VMEM = pl.BlockSpec(memory_space=pltpu.VMEM)
HBM = pl.BlockSpec(memory_space=pltpu.HBM)
ANY = pl.BlockSpec(memory_space=pl.ANY)
LOG2E = 1.4426950408889634
f32 = jnp.float32
bf16 = jnp.bfloat16


def nn(a, b):
    return lax.dot_general(a, b, (((1,), (0,)), ((), ())), preferred_element_type=f32)


def nt(a, b):
    return lax.dot_general(a, b, (((1,), (1,)), ((), ())), preferred_element_type=f32)


def call(kernel, outs, scratch, mib, args, kinds=None, out_kind=VMEM):
    return pl.pallas_call(
        kernel,
        out_shape=[jax.ShapeDtypeStruct(s, d) for s, d in outs],
        in_specs=[VMEM] * len(args) if kinds is None else kinds,
        out_specs=[out_kind] * len(outs),
        scratch_shapes=scratch,
        compiler_params=pltpu.CompilerParams(vmem_limit_bytes=mib * 2**20),
    )(*args)


def normalize(x):
    mean = jnp.mean(x, axis=-1, keepdims=True)
    centred = x - mean
    inverse = lax.rsqrt(jnp.mean(centred * centred, axis=-1, keepdims=True) + epsilon)
    return centred * inverse, inverse


QUAD = (2, 3, 6, 4, FEAT)


def quadrants():
    far = 3 - 3 * lax.axis_index("c")
    near = 3 - far
    return [
        (pl.ds(lat, 3), pl.ds(lon, 6)) for lat, lon in ((far, 6), (near, 0), (near, 6), (far, 0))
    ]


def pack_kernel(t_ref, g_ref, o0, o1, o2, o3, sems):
    copies = []
    for q, (out, (lat, lon)) in enumerate(zip((o0, o1, o2, o3), quadrants())):
        for i, field in enumerate((t_ref, g_ref)):
            copies.append(pltpu.make_async_copy(field.at[lat, lon], out.at[i], sems.at[q, i]))
    for copy in copies:
        copy.start()
    for copy in copies:
        copy.wait()


def unpack_kernel(p0, p1, p2, p3, mixed_ref, token_ref, sems):
    copies = []
    for q, (piece, (lat, lon)) in enumerate(zip((p0, p1, p2, p3), quadrants())):
        for i, field in enumerate((mixed_ref, token_ref)):
            copies.append(pltpu.make_async_copy(piece.at[i], field.at[lat, lon], sems.at[q, i]))
    for copy in copies:
        copy.start()
    for copy in copies:
        copy.wait()


def stage_kernel(w_ref, held_ref, turned_ref):
    held_ref[...] = w_ref[...]
    turned_ref[...] = w_ref[3 * FEAT :, :].T


def order_matrix(window_axis):
    shape = (2 * WIN, 2 * WIN)
    row = lax.broadcasted_iota(jnp.int32, shape, window_axis)
    col = lax.broadcasted_iota(jnp.int32, shape, 1 - window_axis)
    outer = row >= WIN
    j = jnp.where(outer, row - WIN, row)
    level = j & 1
    source = 4 * (j >> 1) + jnp.where(outer, 3 * level, 1 + level)
    return (source == col).astype(f32).astype(bf16)


def put_rows(core, block, part, kept_ref, sent_ref):
    for h in range(0, HEADS, 2):
        for xl in range(2):
            for zl in range(2):
                two = []
                for c in range(2):
                    at = h * HEAD + zl * 32 + xl * 16 + c * 8
                    pair = [block[at : at + 8], block[at + HEAD : at + HEAD + 8]]
                    two.append(jnp.concatenate(pair, axis=0))
                at = (part * 2 + h // 4) * 128 + xl * 64 + zl * 32 + (h % 4) * 8
                kept_ref[at : at + 16, :] = jnp.where(core == 0, two[0], two[1]).astype(bf16)
                sent_ref[at : at + 16, :] = jnp.where(core == 0, two[1], two[0]).astype(bf16)


def main_kernel(
    p0, p1, p2, p3, w_ref, wot_ref,
    x_ref, g_ref, dqt_ref, dkt_ref, dvt_ref, ctxt_ref, kept_ref, sent_ref,
    rows_ref, s_ref, dp_ref, pb_ref, ds_ref,
):
    core = lax.axis_index("c")
    last = lax.axis_size(LAT) - 1
    seam = lax.axis_index("xh") * 4 + lax.axis_index("y") == jnp.where(core == 0, last, 0)
    order = order_matrix(0)
    fields = []
    for i, ref in enumerate((x_ref, g_ref)):
        for q, piece in enumerate((p0, p1, p2, p3)):
            for a in range(3):
                for b in range(6):
                    at = ((q * 3 + a) * 6 + b) * 4
                    rows_ref[i, at : at + 4, :] = piece[i, a, b].astype(f32)
        field = nn(order, rows_ref[i].astype(bf16))
        fields.append(field)
        ref[...] = field.astype(bf16)
    normed = normalize(fields[0])[0].astype(bf16)
    grad = fields[1].astype(bf16)
    kvn = nt(normed, w_ref[FEAT : 3 * FEAT, :]).astype(bf16)
    key = lax.broadcasted_iota(jnp.int32, (WIN, WIN), 0)
    query = lax.broadcasted_iota(jnp.int32, (WIN, WIN), 1)
    apart = seam & ((key >= 72) != (query >= 72))
    levels = (key & 1) != (query & 1)
    halves = []
    zero = jnp.zeros((HEAD, WIN), bf16)
    for w in range(2):
        rows = slice(w * WIN, (w + 1) * WIN)
        nw = normed[rows]
        qkvt = nt(w_ref[: 3 * FEAT, :], nw).astype(bf16)
        cgt = nt(wot_ref[...], grad[rows]).astype(bf16)
        qt, kt, vt = qkvt[:FEAT], qkvt[FEAT : 2 * FEAT], qkvt[2 * FEAT :]
        halves.append((nw, qt, kt, vt, cgt))
        scaled_q = (qt.astype(f32) * 0.125).astype(bf16)
        scaled_c = (cgt.astype(f32) * 0.125).astype(bf16)
        for h in range(HEADS):
            pair = slice((h // 2) * 128, (h // 2) * 128 + 128)
            value = slice(FEAT + (h // 2) * 128, FEAT + (h // 2) * 128 + 128)
            mine = slice(h * HEAD, h * HEAD + HEAD)

            def padded(half):
                return jnp.concatenate([half, zero] if h % 2 == 0 else [zero, half], axis=0)

            s_ref[w, h] = nn(kvn[rows, pair], padded(scaled_q[mine]))
            dp_ref[w, h] = nn(kvn[rows, value], padded(scaled_c[mine]))
    for w in range(2):
        hidden = apart if w == 0 else apart | levels
        for h in range(HEADS):
            s = jnp.where(hidden, masked_score, s_ref[w, h] * LOG2E)
            e = jnp.exp2(s - jnp.max(s, axis=0, keepdims=True))
            p = e * (1.0 / jnp.sum(e, axis=0, keepdims=True))
            dp = dp_ref[w, h]
            pb_ref[w, h] = p.astype(bf16)
            ds_ref[w, h] = (p * (dp - jnp.sum(dp * p, axis=0, keepdims=True))).astype(bf16)
    for w in range(2):
        nw, qt, kt, vt, cgt = halves[w]
        for h in range(HEADS):
            mine = slice(h * HEAD, h * HEAD + HEAD)
            pb = pb_ref[w, h]
            ds = ds_ref[w, h]
            ctxt_ref[w, mine, :] = nn(vt[mine], pb).astype(bf16)
            dvt_ref[w, mine, :] = nt(cgt[mine], pb).astype(bf16)
            dqt_ref[w, mine, :] = nn(kt[mine], ds).astype(bf16)
            dkt_ref[w, mine, :] = nt(qt[mine], ds).astype(bf16)
    for part, ref in enumerate((dqt_ref, dkt_ref, dvt_ref)):
        block = nn(ref[0], halves[0][0]) + nn(ref[1], halves[1][0])
        put_rows(core, block, part, kept_ref, sent_ref)
    block = nt(grad[:WIN].T, ctxt_ref[0]) + nt(grad[WIN:].T, ctxt_ref[1])
    put_rows(core, block, 3, kept_ref, sent_ref)


def back_kernel(
    x_ref, g_ref, w_ref, dqt_ref, dkt_ref, dvt_ref, ctxt_ref, o0, o1, o2, o3, rows_ref, win_ref
):
    for w in range(2):
        rows = slice(w * WIN, (w + 1) * WIN)
        x = x_ref[rows, :].astype(f32)
        normed_exact, inverse = normalize(x)
        win_ref[0, rows, :] = (x + nt(ctxt_ref[w].T, w_ref[3 * FEAT :, :])).astype(bf16)
        normed_grad = (
            nn(dqt_ref[w].T, w_ref[:FEAT, :])
            + nn(dkt_ref[w].T, w_ref[FEAT : 2 * FEAT, :])
            + nn(dvt_ref[w].T, w_ref[2 * FEAT : 3 * FEAT, :])
        )
        correction = (
            normed_grad
            - jnp.mean(normed_grad, axis=-1, keepdims=True)
            - normed_exact * jnp.mean(normed_grad * normed_exact, axis=-1, keepdims=True)
        )
        win_ref[1, rows, :] = (g_ref[rows, :].astype(f32) + inverse * correction).astype(bf16)
    order = order_matrix(1)
    for i in range(2):
        rows_ref[...] = nn(order, win_ref[i])
        for q, piece in enumerate((o0, o1, o2, o3)):
            for a in range(3):
                for b in range(6):
                    at = ((q * 3 + a) * 6 + b) * 4
                    piece[i, a, b] = rows_ref[at : at + 4, :].astype(bf16)


def shift(piece, lat, lon, back):
    n_lat, n_lon = lax.axis_size(LAT), lax.axis_size(LON)
    pairs = []
    for i in range(n_lat):
        for j in range(n_lon):
            from_lat = (i + (lat if j % 2 == 0 else -lat)) % n_lat
            owner = from_lat * n_lon + (j + lon) % n_lon
            pairs.append((i * n_lon + j, owner) if back else (owner, i * n_lon + j))
    return lax.ppermute(piece, ALL, pairs)


def body(tokens, weights, out_grad):
    quads = [(QUAD, bf16)] * 4
    sems = [pltpu.SemaphoreType.DMA((4, 2))]
    moves = ((0, 1), (1, 0), (1, 1))
    sources = [
        pltpu.with_memory_space_constraint(a.transpose(1, 2, 0, 3), pltpu.HBM)
        for a in (tokens, out_grad)
    ]
    parts = call(pack_kernel, quads, sems, 4, sources, [HBM] * 2)
    parts = [parts[0]] + [shift(p, *m, False) for p, m in zip(parts[1:], moves)]
    wide = ((4 * FEAT, FEAT), bf16)
    held, turned = call(stage_kernel, [wide, ((FEAT, FEAT), bf16)], [], 8, (weights,))
    rows = ((2 * WIN, FEAT), bf16)
    square = ((2, FEAT, WIN), bf16)
    half = ((2 * FEAT, FEAT), bf16)

    def tiles(kind):
        return pltpu.VMEM((2, HEADS, WIN, WIN), kind)

    x, grad, dqt, dkt, dvt, ctxt, kept, sent = call(
        main_kernel,
        [rows] * 2 + [square] * 4 + [half] * 2,
        [pltpu.VMEM((2, 2 * WIN, FEAT), f32)] + [tiles(f32)] * 2 + [tiles(bf16)] * 2,
        20,
        (*parts, held, turned),
    )
    got = lax.ppermute(sent, "c", [(0, 1), (1, 0)])
    backs = call(
        back_kernel,
        quads,
        [pltpu.VMEM((2 * WIN, FEAT), f32), pltpu.VMEM((2, 2 * WIN, FEAT), bf16)],
        12,
        (x, grad, held, dqt, dkt, dvt, ctxt),
    )
    got, backs = lax.optimization_barrier((got, backs))
    total = (kept.astype(f32) + got.astype(f32)).astype(bf16).reshape(32, 32, FEAT)
    total = lax.all_to_all(total, ("xh", "y", "xl", "zl"), 0, 0, tiled=True)
    backs = [backs[0]] + [shift(p, *m, True) for p, m in zip(backs[1:], moves)]
    total = jnp.sum(total.astype(f32), axis=0)
    total, backs[1] = lax.optimization_barrier((total, backs[1]))
    at = lax.axis_index("zh")
    for bit in (2, 1):
        total = total.reshape(2, 8 * bit, FEAT)
        mine = (at // bit) % 2
        gone = lax.dynamic_index_in_dim(total, 1 - mine, 0, keepdims=False)
        held_back = lax.dynamic_index_in_dim(total, mine, 0, keepdims=False)
        total = held_back + lax.ppermute(gone, "zh", [(i, i ^ bit) for i in range(4)])
    weight_grads = total
    field = ((6, 12, 4, FEAT), bf16)
    results = call(unpack_kernel, [field] * 2, sems, 4, backs, [ANY] * 4, HBM)
    mixed, token_grads = (r.transpose(2, 0, 1, 3) for r in results)
    return mixed, token_grads, weight_grads


def solution(mesh):
    fine = Mesh(mesh.devices.reshape(2, 4, 4, 2, 2, 2), ALL)
    spread = P(None, LAT, LON, None)
    return jax.shard_map(
        body,
        mesh=fine,
        in_specs=(spread, P(), spread),
        out_specs=(spread, spread, P(ALL, None)),
        check_vma=False,
    )
```

time: 1490 us -> 71 us (0.05)
  the two profiles are of different devices: /device:TPU:2 before, /device:TPU:1 now
where the time goes in v1:
time: 71 us; the launch traced here: 70.8 us
  starting transfers between devices  36.2 us (51%)
  waiting for transfers between devices  20.3 us (29%)
  Pallas kernels  9.76 us (14%)
  other arithmetic  2.06 us (3%)
  local copies, waits for them, and re-layouts  1.61 us (2%)
  between operations  0.77 us (1%)
    ppermute x6, starting transfers between devices, shift(): return lax.ppermute(piece, ALL, pairs)  22.8 us
    all_to_all x1, waiting for transfers between devices, body(): total = lax.all_to_all(total, ('xh', 'y', 'xl', 'zl'), 0, 0, tiled=True)  15.1 us
    pallas_call x5, Pallas kernels, call(): pl.pallas_call(kernel, out_shape=[jax.ShapeDtypeStruct(s, d) for s, d in...  9.76 us
    all_to_all x1, starting transfers between devices, body(): total = lax.all_to_all(total, ('xh', 'y', 'xl', 'zl'), 0, 0, tiled=True)  7.15 us
    ppermute x2, starting transfers between devices, body(): lax.ppermute(gone, 'zh', [(i, i ^ bit) for i in range(4)])  5.46 us
    ppermute x6, waiting for transfers between devices, shift(): return lax.ppermute(piece, ALL, pairs)  4.5 us
    unnamed x2, local copies, waits for them, and re-layouts  1.59 us
  transfers between devices with their start and end apart: 10, of which 4 were waited for; matrix products, arithmetic and copies ran while one was open for 0% of the time, Pallas kernels for 4%

profile of v1, /device:TPU:1, one launch (start us, length us, event | category | flops | bytes accessed | tf_op | source)
XLA Modules:
  0.0 70.8 jit_solution(16844524335895312593)
XLA Ops:
  0.6 1.2 %shard_map.58 = (bf16[2,3,6,4,512]{4,3,2,1,0:T(4,128)(2,1)S(1)}, bf16[2,3,6,4,512]{4,3,2,1,0:T(4,128)(2,1)S(1)}, bf16[2,3,6,4,512]{4,3,2,1,0:T(4,128)(2,1)S(1)}, bf16[2,3,6,4,512]{4,3,2,1,0:T(4,128)(2,1)S(1)}) custom-call(bf16[6,12,4,512]{3,2,1,0:T(4,128)(2,1)} %bitcast.18, bf16[6,12,4,512]{3,2,1,0:T(4,128)(2,1)} %bitcast.19), custom_call_target="tpu_custom_call" | custom-call | tf_op jit(solution)/shard_map/pallas_call | solution.py:34
  1.9 3.3 %collective-permute-start = (bf16[2,3,6,4,512]{4,3,2,1,0:T(4,128)(2,1)S(1)}, bf16[2,3,6,4,512]{4,3,2,1,0:T(4,128)(2,1)S(1)}, u32[]{:S(2)}, u32[]{:S(2)}) collective-permute-start(bf16[2,3,6,4,512]{4,3,2,1,0:T(4,128)(2,1)S(1)} %get-tuple-element.31), channel_id=1, source_target_pairs={{1,0},{2,1},{3,2},{4,3},{5,4},{6,5},{7,6},{8,7},{9,8},{10,9},{11,1... | collective-permute-start | bytes 442376 | tf_op jit(solution)/shard_map/ppermute | solution.py:224
  5.2 0.0 collective-permute-start.1
  5.2 10.0 %collective-permute-start.2 = (bf16[2,3,6,4,512]{4,3,2,1,0:T(4,128)(2,1)S(1)}, bf16[2,3,6,4,512]{4,3,2,1,0:T(4,128)(2,1)S(1)}, u32[]{:S(2)}, u32[]{:S(2)}) collective-permute-start(bf16[2,3,6,4,512]{4,3,2,1,0:T(4,128)(2,1)S(1)} %get-tuple-element.33), channel_id=1, source_target_pairs={{33,0},{226,1},{35,2},{228,3},{37,4},{230,5},{39,6},{232,7},{41,8}... | collective-permute-start | bytes 442376 | tf_op jit(solution)/shard_map/ppermute | solution.py:224
  15.2 0.0 copy-start
  15.2 1.6 %copy-done = bf16[2048,512]{1,0:T(8,128)(2,1)S(1)} copy-done((bf16[2048,512]{1,0:T(8,128)(2,1)S(1)}, bf16[2048,512]{1,0:T(8,128)(2,1)}, u32[]{:S(2)}) %copy-start) | copy-done | bytes 2097176
  16.8 0.3 shard_map.59
  17.1 0.0 collective-permute-done.p1
  17.1 0.0 collective-permute-done.1.p2
  17.1 1.6 %collective-permute-done.2.p3 = bf16[2,3,6,4,512]{4,3,2,1,0:T(4,128)(2,1)S(1)} collective-permute-done((bf16[2,3,6,4,512]{4,3,2,1,0:T(4,128)(2,1)S(1)}, bf16[2,3,6,4,512]{4,3,2,1,0:T(4,128)(2,1)S(1)}, u32[]{:S(2)}, u32[]{:S(2)}) %collective-permute-start.2) | collective-permute-done | bytes 147488 | tf_op jit(solution)/shard_map/ppermute | solution.py:224
  18.7 5.8 %shard_map.60 = (bf16[288,512]{1,0:T(8,128)(2,1)S(1)}, bf16[288,512]{1,0:T(8,128)(2,1)S(1)}, bf16[2,512,144]{2,1,0:T(8,128)(2,1)S(1)}, bf16[2,512,144]{2,1,0:T(8...) custom-call(bf16[2,3,6,4,512]{4,3,2,1,0:T(4,128)(2,1)S(1)} %get-tupl, ...), custom_call_target="tpu_custom_call" | custom-call | tf_op jit(solution)/shard_map/pallas_call | solution.py:34
  24.5 0.8 %collective-permute-start.3 = (bf16[1024,512]{1,0:T(8,128)(2,1)S(1)}, bf16[1024,512]{1,0:T(8,128)(2,1)S(1)}, u32[]{:S(2)}, u32[]{:S(2)}) collective-permute-start(bf16[1024,512]{1,0:T(8,128)(2,1)S(1)} %get-tuple-element.36), channel_id=1, source_target_pairs={{0,1},{1,0},{2,3},{3,2},{4,5},{5,4},{6,7},{7,6},{8,9},{9,8},{10,11... | collective-permute-start | bytes 3145736 | tf_op jit(solution)/shard_map/ppermute | solution.py:253
  25.3 1.6 %shard_map.61 = (bf16[2,3,6,4,512]{4,3,2,1,0:T(4,128)(2,1)S(1)}, bf16[2,3,6,4,512]{4,3,2,1,0:T(4,128)(2,1)S(1)}, bf16[2,3,6,4,512]{4,3,2,1,0:T(4,128)(2,1)S(1)}, bf16[2,3,6,4,512]{4,3,2,1,0:T(4,128)(2,1)S(1)}) custom-call(bf16[288,512]{1,0:T(8,128)(2,1)S(1)} %get-tuple-element.37.x_ref, bf16[288,512]{1,0:T(8,128)(2,1)S(1)} %get-tuple-element.38.g_ref, ...), custom_call_target="tpu_custom_call" | custom-call | tf_op jit(solution)/shard_map/pallas_call | solution.py:34
  26.9 0.7 %collective-permute-done.3 = bf16[1024,512]{1,0:T(8,128)(2,1)S(1)} collective-permute-done((bf16[1024,512]{1,0:T(8,128)(2,1)S(1)}, bf16[1024,512]{1,0:T(8,128)(2,1)S(1)}, u32[]{:S(2)}, u32[]{:S(2)}) %collective-permute-start.3) | collective-permute-done | bytes 1048608 | tf_op jit(solution)/shard_map/ppermute | solution.py:253
  27.6 1.3 %add_convert_fusion = bf16[1024,512]{1,0:T(8,128)(2,1)} fusion(bf16[1024,512]{1,0:T(8,128)(2,1)S(1)} %collective-permute-done.3, bf16[1024,512]{1,0:T(8,128)(2,1)S(1)} %get-tuple-element.48), kind=kLoop, calls=%fused_computation.1 | loop fusion | flops 2097152 | bytes 3145728 | tf_op jit(solution)/shard_map/convert_element_type | solution.py:262
  28.9 7.2 %all-to-all-start = ((bf16[32,32,512]{2,1,0:T(8,128)(2,1)}), bf16[32,32,512]{2,1,0:T(8,128)(2,1)S(1)}, u32[]{:S(2)}, u32[]{:S(2)}) async-start(bf16[32,32,512]{2,1,0:T(8,128)(2,1)} %bitcast.2), calls=%async_computation | async-start | bytes 2097152 | tf_op jit(solution)/shard_map/all_to_all | solution.py:263
  36.1 2.1 %collective-permute-start.4 = (bf16[2,3,6,4,512]{4,3,2,1,0:T(4,128)(2,1)S(1)}, bf16[2,3,6,4,512]{4,3,2,1,0:T(4,128)(2,1)S(1)}, u32[]{:S(2)}, u32[]{:S(2)}) collective-permute-start(bf16[2,3,6,4,512]{4,3,2,1,0:T(4,128)(2,1)S(1)} %get-tuple-element.50), channel_id=1, source_target_pairs={{0,1},{1,2},{2,3},{3,4},{4,5},{5,6},{6,7},{7,8},{8,9},{9,10},{10,1... | collective-permute-start | bytes 442376 | tf_op jit(solution)/shard_map/ppermute | solution.py:224
  38.2 15.1 %all-to-all-done = bf16[32,32,512]{2,1,0:T(8,128)(2,1)S(1)} async-done(((bf16[32,32,512]{2,1,0:T(8,128)(2,1)}), bf16[32,32,512]{2,1,0:T(8,128)(2,1)S(1)}, u32[]{:S(2)}, u32[]{:S(2)}) %all-to-all-start) | async-done | bytes 1048608 | tf_op jit(solution)/shard_map/all_to_all | solution.py:263
  53.4 0.2 convert_reduce_fusion
  53.5 0.0 collective-permute-done.4.p1
  53.5 4.2 %collective-permute-start.7 = (f32[16,512]{1,0:T(8,128)S(1)}, f32[16,512]{1,0:T(8,128)S(1)}, u32[]{:S(2)}, u32[]{:S(2)}) collective-permute-start(f32[16,512]{1,0:T(8,128)S(1)} %dynamic-slice_bitcast_fusion), channel_id=1, source_target_pairs={{0,16},{8,24},{16,0},{24,8},{1,17},{9,25},{17,1},{25,9},{2,18},{10... | collective-permute-start | bytes 98312 | tf_op jit(solution)/shard_map/ppermute | solution.py:273
  57.7 0.9 %collective-permute-start.5 = (bf16[2,3,6,4,512]{4,3,2,1,0:T(4,128)(2,1)S(1)}, bf16[2,3,6,4,512]{4,3,2,1,0:T(4,128)(2,1)S(1)}, u32[]{:S(2)}, u32[]{:S(2)}) collective-permute-start(bf16[2,3,6,4,512]{4,3,2,1,0:T(4,128)(2,1)S(1)} %get-tuple-element.52), channel_id=1, source_target_pairs={{0,32},{1,225},{2,34},{3,227},{4,36},{5,229},{6,38},{7,231},{8,40}... | collective-permute-start | bytes 442376 | tf_op jit(solution)/shard_map/ppermute | solution.py:224
  58.6 6.5 %collective-permute-start.6 = (bf16[2,3,6,4,512]{4,3,2,1,0:T(4,128)(2,1)S(1)}, bf16[2,3,6,4,512]{4,3,2,1,0:T(4,128)(2,1)S(1)}, u32[]{:S(2)}, u32[]{:S(2)}) collective-permute-start(bf16[2,3,6,4,512]{4,3,2,1,0:T(4,128)(2,1)S(1)} %get-tuple-element.53), channel_id=1, source_target_pairs={{0,33},{1,226},{2,35},{3,228},{4,37},{5,230},{6,39},{7,232},{8,41}... | collective-permute-start | bytes 442376 | tf_op jit(solution)/shard_map/ppermute | solution.py:224
  65.1 0.0 collective-permute-done.7
  65.1 1.3 %collective-permute-start.8 = (f32[8,512]{1,0:T(8,128)S(1)}, f32[8,512]{1,0:T(8,128)S(1)}, u32[]{:S(2)}, u32[]{:S(2)}) collective-permute-start(f32[8,512]{1,0:T(8,128)S(1)} %dynamic-slice_bitcast_fusion.1), channel_id=1, source_target_pairs={{0,8},{8,0},{16,24},{24,16},{1,9},{9,1},{17,25},{25,17},{2,10},{10... | collective-permute-start | bytes 49160 | tf_op jit(solution)/shard_map/ppermute | solution.py:273
  66.4 0.0 collective-permute-done.5.p2
  66.4 2.9 %collective-permute-done.6.p3 = bf16[2,3,6,4,512]{4,3,2,1,0:T(4,128)(2,1)S(1)} collective-permute-done((bf16[2,3,6,4,512]{4,3,2,1,0:T(4,128)(2,1)S(1)}, bf16[2,3,6,4,512]{4,3,2,1,0:T(4,128)(2,1)S(1)}, u32[]{:S(2)}, u32[]{:S(2)}) %collective-permute-start.6) | collective-permute-done | bytes 147488 | tf_op jit(solution)/shard_map/ppermute | solution.py:224
  69.2 0.9 %shard_map.62 = (bf16[6,12,4,512]{3,2,1,0:T(4,128)(2,1)}, bf16[6,12,4,512]{3,2,1,0:T(4,128)(2,1)}) custom-call(bf16[2,3,6,4,512]{4,3,2,1,0:T(4,128)(2,1)S(1)} %get-tuple-element.47.p0, bf16[2,3,6,4,512]{4,3,2,1,0:T(4,128)(2,1)S(1)} %collective-permute-done.4.p1, bf16[2,3,6,4,512]{4,3,2,1,0:T(4,128)(2,1)S(1)} %collective-permute-done.5.p2, ...), custom_call_target="tpu_custom_call" | custom-call | tf_op jit(solution)/shard_map/pallas_call | solution.py:34
  70.1 0.0 collective-permute-done.8
  70.1 0.6 bitcast_add_fusion.1
  (3 shorter events, 0.0 us)
Async XLA Ops:
  1.9 15.2 %collective-permute-start = (bf16[2,3,6,4,512]{4,3,2,1,0:T(4,128)(2,1)S(1)}, bf16[2,3,6,4,512]{4,3,2,1,0:T(4,128)(2,1)S(1)}, u32[]{:S(2)}, u32[]{:S(2)}) collective-permute-start(bf16[2,3,6,4,512]{4,3,2,1,0:T(4,128)(2,1)S(1)} %get-tuple-element.31), channel_id=1, source_target_pairs={{1,0},{2,1},{3,2},{4,3},{5,4},{6,5},{7,6},{8,7},{9,8},{10,9},{11,1... | collective-permute-start | bytes 442376 | tf_op jit(solution)/shard_map/ppermute | solution.py:224
  5.2 11.9 %collective-permute-start.1 = (bf16[2,3,6,4,512]{4,3,2,1,0:T(4,128)(2,1)S(1)}, bf16[2,3,6,4,512]{4,3,2,1,0:T(4,128)(2,1)S(1)}, u32[]{:S(2)}, u32[]{:S(2)}) collective-permute-start(bf16[2,3,6,4,512]{4,3,2,1,0:T(4,128)(2,1)S(1)} %get-tuple-element.32), channel_id=1, source_target_pairs={{32,0},{225,1},{34,2},{227,3},{36,4},{229,5},{38,6},{231,7},{40,8}... | collective-permute-start | bytes 442376 | tf_op jit(solution)/shard_map/ppermute | solution.py:224
  5.2 13.5 %collective-permute-start.2 = (bf16[2,3,6,4,512]{4,3,2,1,0:T(4,128)(2,1)S(1)}, bf16[2,3,6,4,512]{4,3,2,1,0:T(4,128)(2,1)S(1)}, u32[]{:S(2)}, u32[]{:S(2)}) collective-permute-start(bf16[2,3,6,4,512]{4,3,2,1,0:T(4,128)(2,1)S(1)} %get-tuple-element.33), channel_id=1, source_target_pairs={{33,0},{226,1},{35,2},{228,3},{37,4},{230,5},{39,6},{232,7},{41,8}... | collective-permute-start | bytes 442376 | tf_op jit(solution)/shard_map/ppermute | solution.py:224
  15.2 1.6 %copy-start = (bf16[2048,512]{1,0:T(8,128)(2,1)S(1)}, bf16[2048,512]{1,0:T(8,128)(2,1)}, u32[]{:S(2)}) copy-start(bf16[2048,512]{1,0:T(8,128)(2,1)} %w_ref.1) | copy-start | bytes 6291460
  24.5 3.1 %collective-permute-start.3 = (bf16[1024,512]{1,0:T(8,128)(2,1)S(1)}, bf16[1024,512]{1,0:T(8,128)(2,1)S(1)}, u32[]{:S(2)}, u32[]{:S(2)}) collective-permute-start(bf16[1024,512]{1,0:T(8,128)(2,1)S(1)} %get-tuple-element.36), channel_id=1, source_target_pairs={{0,1},{1,0},{2,3},{3,2},{4,5},{5,4},{6,7},{7,6},{8,9},{9,8},{10,11... | collective-permute-start | bytes 3145736 | tf_op jit(solution)/shard_map/ppermute | solution.py:253
  28.9 24.4 %all-to-all-start = ((bf16[32,32,512]{2,1,0:T(8,128)(2,1)}), bf16[32,32,512]{2,1,0:T(8,128)(2,1)S(1)}, u32[]{:S(2)}, u32[]{:S(2)}) async-start(bf16[32,32,512]{2,1,0:T(8,128)(2,1)} %bitcast.2), calls=%async_computation | async-start | bytes 2097152 | tf_op jit(solution)/shard_map/all_to_all | solution.py:263
  36.1 17.4 %collective-permute-start.4 = (bf16[2,3,6,4,512]{4,3,2,1,0:T(4,128)(2,1)S(1)}, bf16[2,3,6,4,512]{4,3,2,1,0:T(4,128)(2,1)S(1)}, u32[]{:S(2)}, u32[]{:S(2)}) collective-permute-start(bf16[2,3,6,4,512]{4,3,2,1,0:T(4,128)(2,1)S(1)} %get-tuple-element.50), channel_id=1, source_target_pairs={{0,1},{1,2},{2,3},{3,4},{4,5},{5,6},{6,7},{7,8},{8,9},{9,10},{10,1... | collective-permute-start | bytes 442376 | tf_op jit(solution)/shard_map/ppermute | solution.py:224
  53.5 11.5 %collective-permute-start.7 = (f32[16,512]{1,0:T(8,128)S(1)}, f32[16,512]{1,0:T(8,128)S(1)}, u32[]{:S(2)}, u32[]{:S(2)}) collective-permute-start(f32[16,512]{1,0:T(8,128)S(1)} %dynamic-slice_bitcast_fusion), channel_id=1, source_target_pairs={{0,16},{8,24},{16,0},{24,8},{1,17},{9,25},{17,1},{25,9},{2,18},{10... | collective-permute-start | bytes 98312 | tf_op jit(solution)/shard_map/ppermute | solution.py:273
  57.7 8.7 %collective-permute-start.5 = (bf16[2,3,6,4,512]{4,3,2,1,0:T(4,128)(2,1)S(1)}, bf16[2,3,6,4,512]{4,3,2,1,0:T(4,128)(2,1)S(1)}, u32[]{:S(2)}, u32[]{:S(2)}) collective-permute-start(bf16[2,3,6,4,512]{4,3,2,1,0:T(4,128)(2,1)S(1)} %get-tuple-element.52), channel_id=1, source_target_pairs={{0,32},{1,225},{2,34},{3,227},{4,36},{5,229},{6,38},{7,231},{8,40}... | collective-permute-start | bytes 442376 | tf_op jit(solution)/shard_map/ppermute | solution.py:224
  58.6 10.6 %collective-permute-start.6 = (bf16[2,3,6,4,512]{4,3,2,1,0:T(4,128)(2,1)S(1)}, bf16[2,3,6,4,512]{4,3,2,1,0:T(4,128)(2,1)S(1)}, u32[]{:S(2)}, u32[]{:S(2)}) collective-permute-start(bf16[2,3,6,4,512]{4,3,2,1,0:T(4,128)(2,1)S(1)} %get-tuple-element.53), channel_id=1, source_target_pairs={{0,33},{1,226},{2,35},{3,228},{4,37},{5,230},{6,39},{7,232},{8,41}... | collective-permute-start | bytes 442376 | tf_op jit(solution)/shard_map/ppermute | solution.py:224
  65.1 5.0 %collective-permute-start.8 = (f32[8,512]{1,0:T(8,128)S(1)}, f32[8,512]{1,0:T(8,128)S(1)}, u32[]{:S(2)}, u32[]{:S(2)}) collective-permute-start(f32[8,512]{1,0:T(8,128)S(1)} %dynamic-slice_bitcast_fusion.1), channel_id=1, source_target_pairs={{0,8},{8,0},{16,24},{24,16},{1,9},{9,1},{17,25},{25,17},{2,10},{10... | collective-permute-start | bytes 49160 | tf_op jit(solution)/shard_map/ppermute | solution.py:273

commit v2 on v1

--- a/solution.py
+++ b/solution.py
@@ -52,10 +52,11 @@
 
 
 def quadrants():
-    far = 3 - 3 * lax.axis_index("c")
-    near = 3 - far
+    own = jnp.where(lax.axis_index("c") == lax.axis_index("xl"), 3, 0)
+    left = jnp.where(lax.axis_index("xl") == 0, 3, 0)
     return [
-        (pl.ds(lat, 3), pl.ds(lon, 6)) for lat, lon in ((far, 6), (near, 0), (near, 6), (far, 0))
+        (pl.ds(lat, 3), pl.ds(lon, 6))
+        for lat, lon in ((own, 6), (left, 0), (3 - own, 6), (3 - left, 0))
     ]
 
 
@@ -118,7 +119,8 @@
 ):
     core = lax.axis_index("c")
     last = lax.axis_size(LAT) - 1
-    seam = lax.axis_index("xh") * 4 + lax.axis_index("y") == jnp.where(core == 0, last, 0)
+    upper = core == lax.axis_index("xl")
+    seam = lax.axis_index("xh") * 4 + lax.axis_index("y") == jnp.where(upper, last, 0)
     order = order_matrix(0)
     fields = []
     for i, ref in enumerate((x_ref, g_ref)):
@@ -218,7 +220,7 @@
     pairs = []
     for i in range(n_lat):
         for j in range(n_lon):
-            from_lat = (i + (lat if j % 2 == 0 else -lat)) % n_lat
+            from_lat = (i + (lat if j % 4 in (0, 3) else -lat)) % n_lat
             owner = from_lat * n_lon + (j + lon) % n_lon
             pairs.append((i * n_lon + j, owner) if back else (owner, i * n_lon + j))
     return lax.ppermute(piece, ALL, pairs)
@@ -263,7 +265,7 @@
     total = lax.all_to_all(total, ("xh", "y", "xl", "zl"), 0, 0, tiled=True)
     backs = [backs[0]] + [shift(p, *m, True) for p, m in zip(backs[1:], moves)]
     total = jnp.sum(total.astype(f32), axis=0)
-    total, backs[1] = lax.optimization_barrier((total, backs[1]))
+    total, backs[1], backs[2] = lax.optimization_barrier((total, backs[1], backs[2]))
     at = lax.axis_index("zh")
     for bit in (2, 1):
         total = total.reshape(2, 8 * bit, FEAT)

time: 71 us -> 68.8 us (0.969)
  the two profiles are of different devices: /device:TPU:1 before, /device:TPU:32 now
where the time goes in v2:
time: 68.8 us; the launch traced here: 68.5 us
  waiting for transfers between devices  31 us (45%)
  starting transfers between devices  23.4 us (34%)
  Pallas kernels  9.77 us (14%)
  other arithmetic  2.06 us (3%)
  local copies, waits for them, and re-layouts  1.6 us (2%)
  between operations  0.77 us (1%)
    all_to_all x1, waiting for transfers between devices, body(): total = lax.all_to_all(total, ('xh', 'y', 'xl', 'zl'), 0, 0, tiled=True)  16.1 us
    all_to_all x1, starting transfers between devices, body(): total = lax.all_to_all(total, ('xh', 'y', 'xl', 'zl'), 0, 0, tiled=True)  13.1 us
    pallas_call x5, Pallas kernels, call(): pl.pallas_call(kernel, out_shape=[jax.ShapeDtypeStruct(s, d) for s, d in...  9.77 us
    ppermute x6, waiting for transfers between devices, shift(): return lax.ppermute(piece, ALL, pairs)  8.74 us
    ppermute x6, starting transfers between devices, shift(): return lax.ppermute(piece, ALL, pairs)  7.36 us
    ppermute x2, waiting for transfers between devices, body(): lax.ppermute(gone, 'zh', [(i, i ^ bit) for i in range(4)])  5.06 us
    ppermute x2, starting transfers between devices, body(): lax.ppermute(gone, 'zh', [(i, i ^ bit) for i in range(4)])  2.89 us
    unnamed x2, local copies, waits for them, and re-layouts  1.59 us
  transfers between devices with their start and end apart: 10, of which 7 were waited for; matrix products, arithmetic and copies ran while one was open for 0% of the time, Pallas kernels for 4%

profile of v2, /device:TPU:32, one launch (start us, length us, event | category | flops | bytes accessed | tf_op | source)
XLA Modules:
  0.0 68.5 jit_solution(7621149774483924384)
XLA Ops:
  0.6 1.2 %shard_map.58 = (bf16[2,3,6,4,512]{4,3,2,1,0:T(4,128)(2,1)S(1)}, bf16[2,3,6,4,512]{4,3,2,1,0:T(4,128)(2,1)S(1)}, bf16[2,3,6,4,512]{4,3,2,1,0:T(4,128)(2,1)S(1)}, bf16[2,3,6,4,512]{4,3,2,1,0:T(4,128)(2,1)S(1)}) custom-call(bf16[6,12,4,512]{3,2,1,0:T(4,128)(2,1)} %bitcast.18, bf16[6,12,4,512]{3,2,1,0:T(4,128)(2,1)} %bitcast.19), custom_call_target="tpu_custom_call" | custom-call | tf_op jit(solution)/shard_map/pallas_call | solution.py:34
  1.9 0.6 collective-permute-start
  2.4 5.2 %collective-permute-start.1 = (bf16[2,3,6,4,512]{4,3,2,1,0:T(4,128)(2,1)S(1)}, bf16[2,3,6,4,512]{4,3,2,1,0:T(4,128)(2,1)S(1)}, u32[]{:S(2)}, u32[]{:S(2)}) collective-permute-start(bf16[2,3,6,4,512]{4,3,2,1,0:T(4,128)(2,1)S(1)} %get-tuple-element.33), channel_id=1, source_target_pairs={{32,0},{225,1},{226,2},{35,3},{36,4},{229,5},{230,6},{39,7},{40,8}... | collective-permute-start | bytes 442376 | tf_op jit(solution)/shard_map/ppermute | solution.py:226
  7.6 0.0 collective-permute-start.2
  7.6 0.0 copy-start
  7.6 1.6 %copy-done = bf16[2048,512]{1,0:T(8,128)(2,1)S(1)} copy-done((bf16[2048,512]{1,0:T(8,128)(2,1)S(1)}, bf16[2048,512]{1,0:T(8,128)(2,1)}, u32[]{:S(2)}) %copy-start) | copy-done | bytes 2097176
  9.2 0.3 shard_map.59
  9.5 0.0 collective-permute-done.p1
  9.5 2.2 %collective-permute-done.1.p2 = bf16[2,3,6,4,512]{4,3,2,1,0:T(4,128)(2,1)S(1)} collective-permute-done((bf16[2,3,6,4,512]{4,3,2,1,0:T(4,128)(2,1)S(1)}, bf16[2,3,6,4,512]{4,3,2,1,0:T(4,128)(2,1)S(1)}, u32[]{:S(2)}, u32[]{:S(2)}) %collective-permute-start.1) | collective-permute-done | bytes 147488 | tf_op jit(solution)/shard_map/ppermute | solution.py:226
  11.7 0.5 collective-permute-done.2.p3
  12.2 5.8 %shard_map.60 = (bf16[288,512]{1,0:T(8,128)(2,1)S(1)}, bf16[288,512]{1,0:T(8,128)(2,1)S(1)}, bf16[2,512,144]{2,1,0:T(8,128)(2,1)S(1)}, bf16[2,512,144]{2,1,0:T(8...) custom-call(bf16[2,3,6,4,512]{4,3,2,1,0:T(4,128)(2,1)S(1)} %get-tupl, ...), custom_call_target="tpu_custom_call" | custom-call | tf_op jit(solution)/shard_map/pallas_call | solution.py:34
  18.0 0.1 collective-permute-start.3
  18.1 1.6 %shard_map.61 = (bf16[2,3,6,4,512]{4,3,2,1,0:T(4,128)(2,1)S(1)}, bf16[2,3,6,4,512]{4,3,2,1,0:T(4,128)(2,1)S(1)}, bf16[2,3,6,4,512]{4,3,2,1,0:T(4,128)(2,1)S(1)}, bf16[2,3,6,4,512]{4,3,2,1,0:T(4,128)(2,1)S(1)}) custom-call(bf16[288,512]{1,0:T(8,128)(2,1)S(1)} %get-tuple-element.38.x_ref, bf16[288,512]{1,0:T(8,128)(2,1)S(1)} %get-tuple-element.39.g_ref, ...), custom_call_target="tpu_custom_call" | custom-call | tf_op jit(solution)/shard_map/pallas_call | solution.py:34
  19.7 1.1 %collective-permute-done.3 = bf16[1024,512]{1,0:T(8,128)(2,1)S(1)} collective-permute-done((bf16[1024,512]{1,0:T(8,128)(2,1)S(1)}, bf16[1024,512]{1,0:T(8,128)(2,1)S(1)}, u32[]{:S(2)}, u32[]{:S(2)}) %collective-permute-start.3) | collective-permute-done | bytes 1048608 | tf_op jit(solution)/shard_map/ppermute | solution.py:255
  20.8 1.3 %add_convert_fusion = bf16[1024,512]{1,0:T(8,128)(2,1)} fusion(bf16[1024,512]{1,0:T(8,128)(2,1)S(1)} %collective-permute-done.3, bf16[1024,512]{1,0:T(8,128)(2,1)S(1)} %get-tuple-element.49), kind=kLoop, calls=%fused_computation.1 | loop fusion | flops 2097152 | bytes 3145728 | tf_op jit(solution)/shard_map/convert_element_type | solution.py:264
  22.0 13.1 %all-to-all-start = ((bf16[32,32,512]{2,1,0:T(8,128)(2,1)}), bf16[32,32,512]{2,1,0:T(8,128)(2,1)S(1)}, u32[]{:S(2)}, u32[]{:S(2)}) async-start(bf16[32,32,512]{2,1,0:T(8,128)(2,1)} %bitcast.2), calls=%async_computation | async-start | bytes 2097152 | tf_op jit(solution)/shard_map/all_to_all | solution.py:265
  35.1 0.1 collective-permute-start.4
  35.2 1.5 %collective-permute-start.5 = (bf16[2,3,6,4,512]{4,3,2,1,0:T(4,128)(2,1)S(1)}, bf16[2,3,6,4,512]{4,3,2,1,0:T(4,128)(2,1)S(1)}, u32[]{:S(2)}, u32[]{:S(2)}) collective-permute-start(bf16[2,3,6,4,512]{4,3,2,1,0:T(4,128)(2,1)S(1)} %get-tuple-element.52), channel_id=1, source_target_pairs={{0,32},{1,225},{2,226},{3,35},{4,36},{5,229},{6,230},{7,39},{8,40}... | collective-permute-start | bytes 442376 | tf_op jit(solution)/shard_map/ppermute | solution.py:226
  36.8 16.1 %all-to-all-done = bf16[32,32,512]{2,1,0:T(8,128)(2,1)S(1)} async-done(((bf16[32,32,512]{2,1,0:T(8,128)(2,1)}), bf16[32,32,512]{2,1,0:T(8,128)(2,1)S(1)}, u32[]{:S(2)}, u32[]{:S(2)}) %all-to-all-start) | async-done | bytes 1048608 | tf_op jit(solution)/shard_map/all_to_all | solution.py:265
  52.8 0.2 convert_reduce_fusion
  53.0 0.0 collective-permute-done.4.p1
  53.0 2.3 %collective-permute-done.5.p2 = bf16[2,3,6,4,512]{4,3,2,1,0:T(4,128)(2,1)S(1)} collective-permute-done((bf16[2,3,6,4,512]{4,3,2,1,0:T(4,128)(2,1)S(1)}, bf16[2,3,6,4,512]{4,3,2,1,0:T(4,128)(2,1)S(1)}, u32[]{:S(2)}, u32[]{:S(2)}) %collective-permute-start.5) | collective-permute-done | bytes 147488 | tf_op jit(solution)/shard_map/ppermute | solution.py:226
  55.3 2.8 %collective-permute-start.7 = (f32[16,512]{1,0:T(8,128)S(1)}, f32[16,512]{1,0:T(8,128)S(1)}, u32[]{:S(2)}, u32[]{:S(2)}) collective-permute-start(f32[16,512]{1,0:T(8,128)S(1)} %dynamic-slice_bitcast_fusion), channel_id=1, source_target_pairs={{0,16},{8,24},{16,0},{24,8},{1,17},{9,25},{17,1},{25,9},{2,18},{10... | collective-permute-start | bytes 98312 | tf_op jit(solution)/shard_map/ppermute | solution.py:275
  58.1 0.0 collective-permute-start.6
  58.1 5.1 %collective-permute-done.7 = f32[16,512]{1,0:T(8,128)S(1)} collective-permute-done((f32[16,512]{1,0:T(8,128)S(1)}, f32[16,512]{1,0:T(8,128)S(1)}, u32[]{:S(2)}, u32[]{:S(2)}) %collective-permute-start.7) | collective-permute-done | bytes 32800 | tf_op jit(solution)/shard_map/ppermute | solution.py:275
  63.1 0.1 collective-permute-start.8
  63.3 3.8 %collective-permute-done.6.p3 = bf16[2,3,6,4,512]{4,3,2,1,0:T(4,128)(2,1)S(1)} collective-permute-done((bf16[2,3,6,4,512]{4,3,2,1,0:T(4,128)(2,1)S(1)}, bf16[2,3,6,4,512]{4,3,2,1,0:T(4,128)(2,1)S(1)}, u32[]{:S(2)}, u32[]{:S(2)}) %collective-permute-start.6) | collective-permute-done | bytes 147488 | tf_op jit(solution)/shard_map/ppermute | solution.py:226
  67.0 0.9 %shard_map.62 = (bf16[6,12,4,512]{3,2,1,0:T(4,128)(2,1)}, bf16[6,12,4,512]{3,2,1,0:T(4,128)(2,1)}) custom-call(bf16[2,3,6,4,512]{4,3,2,1,0:T(4,128)(2,1)S(1)} %get-tuple-element.48.p0, bf16[2,3,6,4,512]{4,3,2,1,0:T(4,128)(2,1)S(1)} %collective-permute-done.4.p1, bf16[2,3,6,4,512]{4,3,2,1,0:T(4,128)(2,1)S(1)} %collective-permute-done.5.p2, ...), custom_call_target="tpu_custom_call" | custom-call | tf_op jit(solution)/shard_map/pallas_call | solution.py:34
  67.9 0.0 collective-permute-done.8
  67.9 0.6 bitcast_add_fusion.1
  (3 shorter events, 0.0 us)
Async XLA Ops:
  1.9 7.6 %collective-permute-start = (bf16[2,3,6,4,512]{4,3,2,1,0:T(4,128)(2,1)S(1)}, bf16[2,3,6,4,512]{4,3,2,1,0:T(4,128)(2,1)S(1)}, u32[]{:S(2)}, u32[]{:S(2)}) collective-permute-start(bf16[2,3,6,4,512]{4,3,2,1,0:T(4,128)(2,1)S(1)} %get-tuple-element.32), channel_id=1, source_target_pairs={{1,0},{2,1},{3,2},{4,3},{5,4},{6,5},{7,6},{8,7},{9,8},{10,9},{11,1... | collective-permute-start | bytes 442376 | tf_op jit(solution)/shard_map/ppermute | solution.py:226
  2.4 9.3 %collective-permute-start.1 = (bf16[2,3,6,4,512]{4,3,2,1,0:T(4,128)(2,1)S(1)}, bf16[2,3,6,4,512]{4,3,2,1,0:T(4,128)(2,1)S(1)}, u32[]{:S(2)}, u32[]{:S(2)}) collective-permute-start(bf16[2,3,6,4,512]{4,3,2,1,0:T(4,128)(2,1)S(1)} %get-tuple-element.33), channel_id=1, source_target_pairs={{32,0},{225,1},{226,2},{35,3},{36,4},{229,5},{230,6},{39,7},{40,8}... | collective-permute-start | bytes 442376 | tf_op jit(solution)/shard_map/ppermute | solution.py:226
  7.6 4.6 %collective-permute-start.2 = (bf16[2,3,6,4,512]{4,3,2,1,0:T(4,128)(2,1)S(1)}, bf16[2,3,6,4,512]{4,3,2,1,0:T(4,128)(2,1)S(1)}, u32[]{:S(2)}, u32[]{:S(2)}) collective-permute-start(bf16[2,3,6,4,512]{4,3,2,1,0:T(4,128)(2,1)S(1)} %get-tuple-element.34), channel_id=1, source_target_pairs={{33,0},{226,1},{227,2},{36,3},{37,4},{230,5},{231,6},{40,7},{41,8}... | collective-permute-start | bytes 442376 | tf_op jit(solution)/shard_map/ppermute | solution.py:226
  7.6 1.6 %copy-start = (bf16[2048,512]{1,0:T(8,128)(2,1)S(1)}, bf16[2048,512]{1,0:T(8,128)(2,1)}, u32[]{:S(2)}) copy-start(bf16[2048,512]{1,0:T(8,128)(2,1)} %w_ref.1) | copy-start | bytes 6291460
  18.0 2.7 %collective-permute-start.3 = (bf16[1024,512]{1,0:T(8,128)(2,1)S(1)}, bf16[1024,512]{1,0:T(8,128)(2,1)S(1)}, u32[]{:S(2)}, u32[]{:S(2)}) collective-permute-start(bf16[1024,512]{1,0:T(8,128)(2,1)S(1)} %get-tuple-element.37), channel_id=1, source_target_pairs={{0,1},{1,0},{2,3},{3,2},{4,5},{5,4},{6,7},{7,6},{8,9},{9,8},{10,11... | collective-permute-start | bytes 3145736 | tf_op jit(solution)/shard_map/ppermute | solution.py:255
  22.0 30.8 %all-to-all-start = ((bf16[32,32,512]{2,1,0:T(8,128)(2,1)}), bf16[32,32,512]{2,1,0:T(8,128)(2,1)S(1)}, u32[]{:S(2)}, u32[]{:S(2)}) async-start(bf16[32,32,512]{2,1,0:T(8,128)(2,1)} %bitcast.2), calls=%async_computation | async-start | bytes 2097152 | tf_op jit(solution)/shard_map/all_to_all | solution.py:265
  35.1 17.9 %collective-permute-start.4 = (bf16[2,3,6,4,512]{4,3,2,1,0:T(4,128)(2,1)S(1)}, bf16[2,3,6,4,512]{4,3,2,1,0:T(4,128)(2,1)S(1)}, u32[]{:S(2)}, u32[]{:S(2)}) collective-permute-start(bf16[2,3,6,4,512]{4,3,2,1,0:T(4,128)(2,1)S(1)} %get-tuple-element.51), channel_id=1, source_target_pairs={{0,1},{1,2},{2,3},{3,4},{4,5},{5,6},{6,7},{7,8},{8,9},{9,10},{10,1... | collective-permute-start | bytes 442376 | tf_op jit(solution)/shard_map/ppermute | solution.py:226
  35.2 20.1 %collective-permute-start.5 = (bf16[2,3,6,4,512]{4,3,2,1,0:T(4,128)(2,1)S(1)}, bf16[2,3,6,4,512]{4,3,2,1,0:T(4,128)(2,1)S(1)}, u32[]{:S(2)}, u32[]{:S(2)}) collective-permute-start(bf16[2,3,6,4,512]{4,3,2,1,0:T(4,128)(2,1)S(1)} %get-tuple-element.52), channel_id=1, source_target_pairs={{0,32},{1,225},{2,226},{3,35},{4,36},{5,229},{6,230},{7,39},{8,40}... | collective-permute-start | bytes 442376 | tf_op jit(solution)/shard_map/ppermute | solution.py:226
  55.3 7.9 %collective-permute-start.7 = (f32[16,512]{1,0:T(8,128)S(1)}, f32[16,512]{1,0:T(8,128)S(1)}, u32[]{:S(2)}, u32[]{:S(2)}) collective-permute-start(f32[16,512]{1,0:T(8,128)S(1)} %dynamic-slice_bitcast_fusion), channel_id=1, source_target_pairs={{0,16},{8,24},{16,0},{24,8},{1,17},{9,25},{17,1},{25,9},{2,18},{10... | collective-permute-start | bytes 98312 | tf_op jit(solution)/shard_map/ppermute | solution.py:275
  58.1 9.0 %collective-permute-start.6 = (bf16[2,3,6,4,512]{4,3,2,1,0:T(4,128)(2,1)S(1)}, bf16[2,3,6,4,512]{4,3,2,1,0:T(4,128)(2,1)S(1)}, u32[]{:S(2)}, u32[]{:S(2)}) collective-permute-start(bf16[2,3,6,4,512]{4,3,2,1,0:T(4,128)(2,1)S(1)} %get-tuple-element.55), channel_id=1, source_target_pairs={{0,33},{1,226},{2,227},{3,36},{4,37},{5,230},{6,231},{7,40},{8,41}... | collective-permute-start | bytes 442376 | tf_op jit(solution)/shard_map/ppermute | solution.py:226
  63.1 4.8 %collective-permute-start.8 = (f32[8,512]{1,0:T(8,128)S(1)}, f32[8,512]{1,0:T(8,128)S(1)}, u32[]{:S(2)}, u32[]{:S(2)}) collective-permute-start(f32[8,512]{1,0:T(8,128)S(1)} %dynamic-slice_bitcast_fusion.1), channel_id=1, source_target_pairs={{0,8},{8,0},{16,24},{24,16},{1,9},{9,1},{17,25},{25,17},{2,10},{10... | collective-permute-start | bytes 49160 | tf_op jit(solution)/shard_map/ppermute | solution.py:275

commit v3 on v2

--- a/solution.py
+++ b/solution.py
@@ -82,8 +82,9 @@
         copy.wait()
 
 
-def stage_kernel(w_ref, held_ref, turned_ref):
+def stage_kernel(w_ref, held_ref, turned_ref, order_ref):
     held_ref[...] = w_ref[...]
+    order_ref[...] = order_matrix(0)
     turned_ref[...] = w_ref[3 * FEAT :, :].T
 
 
@@ -113,7 +114,7 @@
 
 
 def main_kernel(
-    p0, p1, p2, p3, w_ref, wot_ref,
+    p0, p1, p2, p3, w_ref, wot_ref, order_ref,
     x_ref, g_ref, dqt_ref, dkt_ref, dvt_ref, ctxt_ref, kept_ref, sent_ref,
     rows_ref, s_ref, dp_ref, pb_ref, ds_ref,
 ):
@@ -121,7 +122,7 @@
     last = lax.axis_size(LAT) - 1
     upper = core == lax.axis_index("xl")
     seam = lax.axis_index("xh") * 4 + lax.axis_index("y") == jnp.where(upper, last, 0)
-    order = order_matrix(0)
+    order = order_ref[...]
     fields = []
     for i, ref in enumerate((x_ref, g_ref)):
         for q, piece in enumerate((p0, p1, p2, p3)):
@@ -139,46 +140,59 @@
     query = lax.broadcasted_iota(jnp.int32, (WIN, WIN), 1)
     apart = seam & ((key >= 72) != (query >= 72))
     levels = (key & 1) != (query & 1)
+    zero = jnp.zeros((HEAD, WIN), bf16)
     halves = []
-    zero = jnp.zeros((HEAD, WIN), bf16)
     for w in range(2):
-        rows = slice(w * WIN, (w + 1) * WIN)
-        nw = normed[rows]
+        nw = normed[w * WIN : (w + 1) * WIN]
         qkvt = nt(w_ref[: 3 * FEAT, :], nw).astype(bf16)
-        cgt = nt(wot_ref[...], grad[rows]).astype(bf16)
+        cgt = nt(wot_ref[...], grad[w * WIN : (w + 1) * WIN]).astype(bf16)
         qt, kt, vt = qkvt[:FEAT], qkvt[FEAT : 2 * FEAT], qkvt[2 * FEAT :]
-        halves.append((nw, qt, kt, vt, cgt))
         scaled_q = (qt.astype(f32) * 0.125).astype(bf16)
         scaled_c = (cgt.astype(f32) * 0.125).astype(bf16)
-        for h in range(HEADS):
-            pair = slice((h // 2) * 128, (h // 2) * 128 + 128)
-            value = slice(FEAT + (h // 2) * 128, FEAT + (h // 2) * 128 + 128)
-            mine = slice(h * HEAD, h * HEAD + HEAD)
-
-            def padded(half):
-                return jnp.concatenate([half, zero] if h % 2 == 0 else [zero, half], axis=0)
-
-            s_ref[w, h] = nn(kvn[rows, pair], padded(scaled_q[mine]))
-            dp_ref[w, h] = nn(kvn[rows, value], padded(scaled_c[mine]))
-    for w in range(2):
+        halves.append((nw, qt, kt, vt, cgt, scaled_q, scaled_c))
+
+    def scores(w, h):
+        rows = slice(w * WIN, (w + 1) * WIN)
+        pair = slice((h // 2) * 128, (h // 2) * 128 + 128)
+        value = slice(FEAT + (h // 2) * 128, FEAT + (h // 2) * 128 + 128)
+        mine = slice(h * HEAD, h * HEAD + HEAD)
+        scaled_q, scaled_c = halves[w][5:]
+
+        def padded(half):
+            return jnp.concatenate([half, zero] if h % 2 == 0 else [zero, half], axis=0)
+
+        s_ref[w, h] = nn(kvn[rows, pair], padded(scaled_q[mine]))
+        dp_ref[w, h] = nn(kvn[rows, value], padded(scaled_c[mine]))
+
+    def softmax(w, h):
         hidden = apart if w == 0 else apart | levels
-        for h in range(HEADS):
-            s = jnp.where(hidden, masked_score, s_ref[w, h] * LOG2E)
-            e = jnp.exp2(s - jnp.max(s, axis=0, keepdims=True))
-            p = e * (1.0 / jnp.sum(e, axis=0, keepdims=True))
-            dp = dp_ref[w, h]
-            pb_ref[w, h] = p.astype(bf16)
-            ds_ref[w, h] = (p * (dp - jnp.sum(dp * p, axis=0, keepdims=True))).astype(bf16)
-    for w in range(2):
-        nw, qt, kt, vt, cgt = halves[w]
-        for h in range(HEADS):
-            mine = slice(h * HEAD, h * HEAD + HEAD)
-            pb = pb_ref[w, h]
-            ds = ds_ref[w, h]
-            ctxt_ref[w, mine, :] = nn(vt[mine], pb).astype(bf16)
-            dvt_ref[w, mine, :] = nt(cgt[mine], pb).astype(bf16)
-            dqt_ref[w, mine, :] = nn(kt[mine], ds).astype(bf16)
-            dkt_ref[w, mine, :] = nt(qt[mine], ds).astype(bf16)
+        s = jnp.where(hidden, masked_score, s_ref[w, h] * LOG2E)
+        e = jnp.exp2(s - jnp.max(s, axis=0, keepdims=True))
+        p = e * (1.0 / jnp.sum(e, axis=0, keepdims=True))
+        dp = dp_ref[w, h]
+        pb_ref[w, h] = p.astype(bf16)
+        ds_ref[w, h] = (p * (dp - jnp.sum(dp * p, axis=0, keepdims=True))).astype(bf16)
+
+    def products(w, h):
+        qt, kt, vt, cgt = halves[w][1:5]
+        mine = slice(h * HEAD, h * HEAD + HEAD)
+        pb = pb_ref[w, h]
+        ds = ds_ref[w, h]
+        ctxt_ref[w, mine, :] = nn(vt[mine], pb).astype(bf16)
+        dvt_ref[w, mine, :] = nt(cgt[mine], pb).astype(bf16)
+        dqt_ref[w, mine, :] = nn(kt[mine], ds).astype(bf16)
+        dkt_ref[w, mine, :] = nt(qt[mine], ds).astype(bf16)
+
+    for h in range(HEADS):
+        scores(0, h)
+    for h in range(HEADS):
+        scores(1, h)
+        softmax(0, h)
+    for h in range(HEADS):
+        products(0, h)
+        softmax(1, h)
+    for h in range(HEADS):
+        products(1, h)
     for part, ref in enumerate((dqt_ref, dkt_ref, dvt_ref)):
         block = nn(ref[0], halves[0][0]) + nn(ref[1], halves[1][0])
         put_rows(core, block, part, kept_ref, sent_ref)
@@ -237,7 +251,9 @@
     parts = call(pack_kernel, quads, sems, 4, sources, [HBM] * 2)
     parts = [parts[0]] + [shift(p, *m, False) for p, m in zip(parts[1:], moves)]
     wide = ((4 * FEAT, FEAT), bf16)
-    held, turned = call(stage_kernel, [wide, ((FEAT, FEAT), bf16)], [], 8, (weights,))
+    square = ((FEAT, FEAT), bf16)
+    turn = ((2 * WIN, 2 * WIN), bf16)
+    held, turned, order = call(stage_kernel, [wide, square, turn], [], 8, (weights,))
     rows = ((2 * WIN, FEAT), bf16)
     square = ((2, FEAT, WIN), bf16)
     half = ((2 * FEAT, FEAT), bf16)
@@ -250,7 +266,7 @@
         [rows] * 2 + [square] * 4 + [half] * 2,
         [pltpu.VMEM((2, 2 * WIN, FEAT), f32)] + [tiles(f32)] * 2 + [tiles(bf16)] * 2,
         20,
-        (*parts, held, turned),
+        (*parts, held, turned, order),
     )
     got = lax.ppermute(sent, "c", [(0, 1), (1, 0)])
     backs = call(
@@ -265,7 +281,7 @@
     total = lax.all_to_all(total, ("xh", "y", "xl", "zl"), 0, 0, tiled=True)
     backs = [backs[0]] + [shift(p, *m, True) for p, m in zip(backs[1:], moves)]
     total = jnp.sum(total.astype(f32), axis=0)
-    total, backs[1], backs[2] = lax.optimization_barrier((total, backs[1], backs[2]))
+    total, backs[2], backs[3] = lax.optimization_barrier((total, backs[2], backs[3]))
     at = lax.axis_index("zh")
     for bit in (2, 1):
         total = total.reshape(2, 8 * bit, FEAT)

time: 68.8 us -> 69.2 us (level)
  the two profiles are of different devices: /device:TPU:32 before, /device:TPU:1 now
where the time goes in v3:
time: 69.2 us; the launch traced here: 68.9 us
  starting transfers between devices  30.3 us (44%)
  waiting for transfers between devices  24.7 us (36%)
  Pallas kernels  9.48 us (14%)
  other arithmetic  2.04 us (3%)
  local copies, waits for them, and re-layouts  1.6 us (2%)
  between operations  0.76 us (1%)
    ppermute x6, starting transfers between devices, shift(): return lax.ppermute(piece, ALL, pairs)  19.7 us
    all_to_all x1, waiting for transfers between devices, body(): total = lax.all_to_all(total, ('xh', 'y', 'xl', 'zl'), 0, 0, tiled=True)  10.7 us
    pallas_call x5, Pallas kernels, call(): pl.pallas_call(kernel, out_shape=[jax.ShapeDtypeStruct(s, d) for s, d in...  9.48 us
    all_to_all x1, starting transfers between devices, body(): total = lax.all_to_all(total, ('xh', 'y', 'xl', 'zl'), 0, 0, tiled=True)  7.15 us
    ppermute x2, waiting for transfers between devices, body(): lax.ppermute(gone, 'zh', [(i, i ^ bit) for i in range(4)])  6.71 us
    ppermute x6, waiting for transfers between devices, shift(): return lax.ppermute(piece, ALL, pairs)  6.6 us
    ppermute x2, starting transfers between devices, body(): lax.ppermute(gone, 'zh', [(i, i ^ bit) for i in range(4)])  2.61 us
    unnamed x2, local copies, waits for them, and re-layouts  1.59 us
  transfers between devices with their start and end apart: 10, of which 6 were waited for; matrix products, arithmetic and copies ran while one was open for 0% of the time, Pallas kernels for 4%

profile of v3, /device:TPU:1, one launch (start us, length us, event | category | flops | bytes accessed | tf_op | source)
XLA Modules:
  0.0 68.9 jit_solution(2602917106474039281)
XLA Ops:
  0.6 1.2 %shard_map.58 = (bf16[2,3,6,4,512]{4,3,2,1,0:T(4,128)(2,1)S(1)}, bf16[2,3,6,4,512]{4,3,2,1,0:T(4,128)(2,1)S(1)}, bf16[2,3,6,4,512]{4,3,2,1,0:T(4,128)(2,1)S(1)}, bf16[2,3,6,4,512]{4,3,2,1,0:T(4,128)(2,1)S(1)}) custom-call(bf16[6,12,4,512]{3,2,1,0:T(4,128)(2,1)} %bitcast.18, bf16[6,12,4,512]{3,2,1,0:T(4,128)(2,1)} %bitcast.19), custom_call_target="tpu_custom_call" | custom-call | tf_op jit(solution)/shard_map/pallas_call | solution.py:34
  1.9 3.3 %collective-permute-start = (bf16[2,3,6,4,512]{4,3,2,1,0:T(4,128)(2,1)S(1)}, bf16[2,3,6,4,512]{4,3,2,1,0:T(4,128)(2,1)S(1)}, u32[]{:S(2)}, u32[]{:S(2)}) collective-permute-start(bf16[2,3,6,4,512]{4,3,2,1,0:T(4,128)(2,1)S(1)} %get-tuple-element.33), channel_id=1, source_target_pairs={{1,0},{2,1},{3,2},{4,3},{5,4},{6,5},{7,6},{8,7},{9,8},{10,9},{11,1... | collective-permute-start | bytes 442376 | tf_op jit(solution)/shard_map/ppermute | solution.py:240
  5.2 0.0 collective-permute-start.1
  5.2 10.0 %collective-permute-start.2 = (bf16[2,3,6,4,512]{4,3,2,1,0:T(4,128)(2,1)S(1)}, bf16[2,3,6,4,512]{4,3,2,1,0:T(4,128)(2,1)S(1)}, u32[]{:S(2)}, u32[]{:S(2)}) collective-permute-start(bf16[2,3,6,4,512]{4,3,2,1,0:T(4,128)(2,1)S(1)} %get-tuple-element.35), channel_id=1, source_target_pairs={{33,0},{226,1},{227,2},{36,3},{37,4},{230,5},{231,6},{40,7},{41,8}... | collective-permute-start | bytes 442376 | tf_op jit(solution)/shard_map/ppermute | solution.py:240
  15.2 0.0 copy-start
  15.2 1.6 %copy-done = bf16[2048,512]{1,0:T(8,128)(2,1)S(1)} copy-done((bf16[2048,512]{1,0:T(8,128)(2,1)S(1)}, bf16[2048,512]{1,0:T(8,128)(2,1)}, u32[]{:S(2)}) %copy-start) | copy-done | bytes 2097176
  16.8 0.3 shard_map.59
  17.1 0.0 collective-permute-done.p1
  17.1 0.0 collective-permute-done.1.p2
  17.1 1.6 %collective-permute-done.2.p3 = bf16[2,3,6,4,512]{4,3,2,1,0:T(4,128)(2,1)S(1)} collective-permute-done((bf16[2,3,6,4,512]{4,3,2,1,0:T(4,128)(2,1)S(1)}, bf16[2,3,6,4,512]{4,3,2,1,0:T(4,128)(2,1)S(1)}, u32[]{:S(2)}, u32[]{:S(2)}) %collective-permute-start.2) | collective-permute-done | bytes 147488 | tf_op jit(solution)/shard_map/ppermute | solution.py:240
  18.7 5.5 %shard_map.60 = (bf16[288,512]{1,0:T(8,128)(2,1)S(1)}, bf16[288,512]{1,0:T(8,128)(2,1)S(1)}, bf16[2,512,144]{2,1,0:T(8,128)(2,1)S(1)}, bf16[2,512,144]{2,1,0:T(8...) custom-call(bf16[2,3,6,4,512]{4,3,2,1,0:T(4,128)(2,1)S(1)} %get-tupl, ...), custom_call_target="tpu_custom_call" | custom-call | tf_op jit(solution)/shard_map/pallas_call | solution.py:34
  24.2 0.8 %collective-permute-start.3 = (bf16[1024,512]{1,0:T(8,128)(2,1)S(1)}, bf16[1024,512]{1,0:T(8,128)(2,1)S(1)}, u32[]{:S(2)}, u32[]{:S(2)}) collective-permute-start(bf16[1024,512]{1,0:T(8,128)(2,1)S(1)} %get-tuple-element.39), channel_id=1, source_target_pairs={{0,1},{1,0},{2,3},{3,2},{4,5},{5,4},{6,7},{7,6},{8,9},{9,8},{10,11... | collective-permute-start | bytes 3145736 | tf_op jit(solution)/shard_map/ppermute | solution.py:271
  25.0 1.6 %shard_map.61 = (bf16[2,3,6,4,512]{4,3,2,1,0:T(4,128)(2,1)S(1)}, bf16[2,3,6,4,512]{4,3,2,1,0:T(4,128)(2,1)S(1)}, bf16[2,3,6,4,512]{4,3,2,1,0:T(4,128)(2,1)S(1)}, bf16[2,3,6,4,512]{4,3,2,1,0:T(4,128)(2,1)S(1)}) custom-call(bf16[288,512]{1,0:T(8,128)(2,1)S(1)} %get-tuple-element.40.x_ref, bf16[288,512]{1,0:T(8,128)(2,1)S(1)} %get-tuple-element.41.g_ref, ...), custom_call_target="tpu_custom_call" | custom-call | tf_op jit(solution)/shard_map/pallas_call | solution.py:34
  26.6 0.7 %collective-permute-done.3 = bf16[1024,512]{1,0:T(8,128)(2,1)S(1)} collective-permute-done((bf16[1024,512]{1,0:T(8,128)(2,1)S(1)}, bf16[1024,512]{1,0:T(8,128)(2,1)S(1)}, u32[]{:S(2)}, u32[]{:S(2)}) %collective-permute-start.3) | collective-permute-done | bytes 1048608 | tf_op jit(solution)/shard_map/ppermute | solution.py:271
  27.3 1.3 %add_convert_fusion = bf16[1024,512]{1,0:T(8,128)(2,1)} fusion(bf16[1024,512]{1,0:T(8,128)(2,1)S(1)} %collective-permute-done.3, bf16[1024,512]{1,0:T(8,128)(2,1)S(1)} %get-tuple-element.52), kind=kLoop, calls=%fused_computation.1 | loop fusion | flops 2097152 | bytes 3145728 | tf_op jit(solution)/shard_map/convert_element_type | solution.py:280
  28.5 7.2 %all-to-all-start = ((bf16[32,32,512]{2,1,0:T(8,128)(2,1)}), bf16[32,32,512]{2,1,0:T(8,128)(2,1)S(1)}, u32[]{:S(2)}, u32[]{:S(2)}) async-start(bf16[32,32,512]{2,1,0:T(8,128)(2,1)} %bitcast.2), calls=%async_computation | async-start | bytes 2097152 | tf_op jit(solution)/shard_map/all_to_all | solution.py:281
  35.7 5.0 %collective-permute-start.5 = (bf16[2,3,6,4,512]{4,3,2,1,0:T(4,128)(2,1)S(1)}, bf16[2,3,6,4,512]{4,3,2,1,0:T(4,128)(2,1)S(1)}, u32[]{:S(2)}, u32[]{:S(2)}) collective-permute-start(bf16[2,3,6,4,512]{4,3,2,1,0:T(4,128)(2,1)S(1)} %get-tuple-element.54), channel_id=1, source_target_pairs={{0,32},{1,225},{2,226},{3,35},{4,36},{5,229},{6,230},{7,39},{8,40}... | collective-permute-start | bytes 442376 | tf_op jit(solution)/shard_map/ppermute | solution.py:240
  40.7 1.4 %collective-permute-start.6 = (bf16[2,3,6,4,512]{4,3,2,1,0:T(4,128)(2,1)S(1)}, bf16[2,3,6,4,512]{4,3,2,1,0:T(4,128)(2,1)S(1)}, u32[]{:S(2)}, u32[]{:S(2)}) collective-permute-start(bf16[2,3,6,4,512]{4,3,2,1,0:T(4,128)(2,1)S(1)} %get-tuple-element.55), channel_id=1, source_target_pairs={{0,33},{1,226},{2,227},{3,36},{4,37},{5,230},{6,231},{7,40},{8,41}... | collective-permute-start | bytes 442376 | tf_op jit(solution)/shard_map/ppermute | solution.py:240
  42.1 10.7 %all-to-all-done = bf16[32,32,512]{2,1,0:T(8,128)(2,1)S(1)} async-done(((bf16[32,32,512]{2,1,0:T(8,128)(2,1)}), bf16[32,32,512]{2,1,0:T(8,128)(2,1)S(1)}, u32[]{:S(2)}, u32[]{:S(2)}) %all-to-all-start) | async-done | bytes 1048608 | tf_op jit(solution)/shard_map/all_to_all | solution.py:281
  52.8 0.2 convert_reduce_fusion
  53.0 0.0 collective-permute-done.5.p2
  53.0 5.0 %collective-permute-done.6.p3 = bf16[2,3,6,4,512]{4,3,2,1,0:T(4,128)(2,1)S(1)} collective-permute-done((bf16[2,3,6,4,512]{4,3,2,1,0:T(4,128)(2,1)S(1)}, bf16[2,3,6,4,512]{4,3,2,1,0:T(4,128)(2,1)S(1)}, u32[]{:S(2)}, u32[]{:S(2)}) %collective-permute-start.6) | collective-permute-done | bytes 147488 | tf_op jit(solution)/shard_map/ppermute | solution.py:240
  58.0 2.5 %collective-permute-start.7 = (f32[16,512]{1,0:T(8,128)S(1)}, f32[16,512]{1,0:T(8,128)S(1)}, u32[]{:S(2)}, u32[]{:S(2)}) collective-permute-start(f32[16,512]{1,0:T(8,128)S(1)} %dynamic-slice_bitcast_fusion), channel_id=1, source_target_pairs={{0,16},{8,24},{16,0},{24,8},{1,17},{9,25},{17,1},{25,9},{2,18},{10... | collective-permute-start | bytes 98312 | tf_op jit(solution)/shard_map/ppermute | solution.py:291
  60.5 0.0 collective-permute-start.4
  60.5 4.2 %collective-permute-done.7 = f32[16,512]{1,0:T(8,128)S(1)} collective-permute-done((f32[16,512]{1,0:T(8,128)S(1)}, f32[16,512]{1,0:T(8,128)S(1)}, u32[]{:S(2)}, u32[]{:S(2)}) %collective-permute-start.7) | collective-permute-done | bytes 32800 | tf_op jit(solution)/shard_map/ppermute | solution.py:291
  64.7 0.1 collective-permute-start.8
  64.8 0.0 collective-permute-done.4.p1
  64.8 0.9 %shard_map.62 = (bf16[6,12,4,512]{3,2,1,0:T(4,128)(2,1)}, bf16[6,12,4,512]{3,2,1,0:T(4,128)(2,1)}) custom-call(bf16[2,3,6,4,512]{4,3,2,1,0:T(4,128)(2,1)S(1)} %get-tuple-element.50.p0, bf16[2,3,6,4,512]{4,3,2,1,0:T(4,128)(2,1)S(1)} %collective-permute-done.4.p1, bf16[2,3,6,4,512]{4,3,2,1,0:T(4,128)(2,1)S(1)} %collective-permute-done.5.p2, ...), custom_call_target="tpu_custom_call" | custom-call | tf_op jit(solution)/shard_map/pallas_call | solution.py:34
  65.7 2.6 %collective-permute-done.8 = f32[8,512]{1,0:T(8,128)S(1)} collective-permute-done((f32[8,512]{1,0:T(8,128)S(1)}, f32[8,512]{1,0:T(8,128)S(1)}, u32[]{:S(2)}, u32[]{:S(2)}) %collective-permute-start.8) | collective-permute-done | bytes 16416 | tf_op jit(solution)/shard_map/ppermute | solution.py:291
  68.3 0.6 bitcast_add_fusion.1
  (3 shorter events, 0.0 us)
Async XLA Ops:
  1.9 15.3 %collective-permute-start = (bf16[2,3,6,4,512]{4,3,2,1,0:T(4,128)(2,1)S(1)}, bf16[2,3,6,4,512]{4,3,2,1,0:T(4,128)(2,1)S(1)}, u32[]{:S(2)}, u32[]{:S(2)}) collective-permute-start(bf16[2,3,6,4,512]{4,3,2,1,0:T(4,128)(2,1)S(1)} %get-tuple-element.33), channel_id=1, source_target_pairs={{1,0},{2,1},{3,2},{4,3},{5,4},{6,5},{7,6},{8,7},{9,8},{10,9},{11,1... | collective-permute-start | bytes 442376 | tf_op jit(solution)/shard_map/ppermute | solution.py:240
  5.2 11.9 %collective-permute-start.1 = (bf16[2,3,6,4,512]{4,3,2,1,0:T(4,128)(2,1)S(1)}, bf16[2,3,6,4,512]{4,3,2,1,0:T(4,128)(2,1)S(1)}, u32[]{:S(2)}, u32[]{:S(2)}) collective-permute-start(bf16[2,3,6,4,512]{4,3,2,1,0:T(4,128)(2,1)S(1)} %get-tuple-element.34), channel_id=1, source_target_pairs={{32,0},{225,1},{226,2},{35,3},{36,4},{229,5},{230,6},{39,7},{40,8}... | collective-permute-start | bytes 442376 | tf_op jit(solution)/shard_map/ppermute | solution.py:240
  5.2 13.5 %collective-permute-start.2 = (bf16[2,3,6,4,512]{4,3,2,1,0:T(4,128)(2,1)S(1)}, bf16[2,3,6,4,512]{4,3,2,1,0:T(4,128)(2,1)S(1)}, u32[]{:S(2)}, u32[]{:S(2)}) collective-permute-start(bf16[2,3,6,4,512]{4,3,2,1,0:T(4,128)(2,1)S(1)} %get-tuple-element.35), channel_id=1, source_target_pairs={{33,0},{226,1},{227,2},{36,3},{37,4},{230,5},{231,6},{40,7},{41,8}... | collective-permute-start | bytes 442376 | tf_op jit(solution)/shard_map/ppermute | solution.py:240
  15.2 1.6 %copy-start = (bf16[2048,512]{1,0:T(8,128)(2,1)S(1)}, bf16[2048,512]{1,0:T(8,128)(2,1)}, u32[]{:S(2)}) copy-start(bf16[2048,512]{1,0:T(8,128)(2,1)} %w_ref.1) | copy-start | bytes 6291460
  24.2 3.1 %collective-permute-start.3 = (bf16[1024,512]{1,0:T(8,128)(2,1)S(1)}, bf16[1024,512]{1,0:T(8,128)(2,1)S(1)}, u32[]{:S(2)}, u32[]{:S(2)}) collective-permute-start(bf16[1024,512]{1,0:T(8,128)(2,1)S(1)} %get-tuple-element.39), channel_id=1, source_target_pairs={{0,1},{1,0},{2,3},{3,2},{4,5},{5,4},{6,7},{7,6},{8,9},{9,8},{10,11... | collective-permute-start | bytes 3145736 | tf_op jit(solution)/shard_map/ppermute | solution.py:271
  28.5 24.3 %all-to-all-start = ((bf16[32,32,512]{2,1,0:T(8,128)(2,1)}), bf16[32,32,512]{2,1,0:T(8,128)(2,1)S(1)}, u32[]{:S(2)}, u32[]{:S(2)}) async-start(bf16[32,32,512]{2,1,0:T(8,128)(2,1)} %bitcast.2), calls=%async_computation | async-start | bytes 2097152 | tf_op jit(solution)/shard_map/all_to_all | solution.py:281
  35.7 17.3 %collective-permute-start.5 = (bf16[2,3,6,4,512]{4,3,2,1,0:T(4,128)(2,1)S(1)}, bf16[2,3,6,4,512]{4,3,2,1,0:T(4,128)(2,1)S(1)}, u32[]{:S(2)}, u32[]{:S(2)}) collective-permute-start(bf16[2,3,6,4,512]{4,3,2,1,0:T(4,128)(2,1)S(1)} %get-tuple-element.54), channel_id=1, source_target_pairs={{0,32},{1,225},{2,226},{3,35},{4,36},{5,229},{6,230},{7,39},{8,40}... | collective-permute-start | bytes 442376 | tf_op jit(solution)/shard_map/ppermute | solution.py:240
  40.7 17.3 %collective-permute-start.6 = (bf16[2,3,6,4,512]{4,3,2,1,0:T(4,128)(2,1)S(1)}, bf16[2,3,6,4,512]{4,3,2,1,0:T(4,128)(2,1)S(1)}, u32[]{:S(2)}, u32[]{:S(2)}) collective-permute-start(bf16[2,3,6,4,512]{4,3,2,1,0:T(4,128)(2,1)S(1)} %get-tuple-element.55), channel_id=1, source_target_pairs={{0,33},{1,226},{2,227},{3,36},{4,37},{5,230},{6,231},{7,40},{8,41}... | collective-permute-start | bytes 442376 | tf_op jit(solution)/shard_map/ppermute | solution.py:240
  58.0 6.7 %collective-permute-start.7 = (f32[16,512]{1,0:T(8,128)S(1)}, f32[16,512]{1,0:T(8,128)S(1)}, u32[]{:S(2)}, u32[]{:S(2)}) collective-permute-start(f32[16,512]{1,0:T(8,128)S(1)} %dynamic-slice_bitcast_fusion), channel_id=1, source_target_pairs={{0,16},{8,24},{16,0},{24,8},{1,17},{9,25},{17,1},{25,9},{2,18},{10... | collective-permute-start | bytes 98312 | tf_op jit(solution)/shard_map/ppermute | solution.py:291
  60.5 4.3 %collective-permute-start.4 = (bf16[2,3,6,4,512]{4,3,2,1,0:T(4,128)(2,1)S(1)}, bf16[2,3,6,4,512]{4,3,2,1,0:T(4,128)(2,1)S(1)}, u32[]{:S(2)}, u32[]{:S(2)}) collective-permute-start(bf16[2,3,6,4,512]{4,3,2,1,0:T(4,128)(2,1)S(1)} %get-tuple-element.51), channel_id=1, source_target_pairs={{0,1},{1,2},{2,3},{3,4},{4,5},{5,6},{6,7},{7,8},{8,9},{9,10},{10,1... | collective-permute-start | bytes 442376 | tf_op jit(solution)/shard_map/ppermute | solution.py:240
  64.7 3.6 %collective-permute-start.8 = (f32[8,512]{1,0:T(8,128)S(1)}, f32[8,512]{1,0:T(8,128)S(1)}, u32[]{:S(2)}, u32[]{:S(2)}) collective-permute-start(f32[8,512]{1,0:T(8,128)S(1)} %dynamic-slice_bitcast_fusion.1), channel_id=1, source_target_pairs={{0,8},{8,0},{16,24},{24,16},{1,9},{9,1},{17,25},{25,17},{2,10},{10... | collective-permute-start | bytes 49160 | tf_op jit(solution)/shard_map/ppermute | solution.py:291

commit v4 on v3

--- a/solution.py
+++ b/solution.py
@@ -114,7 +114,7 @@
 
 
 def main_kernel(
-    p0, p1, p2, p3, w_ref, wot_ref, order_ref,
+    p2, p3, p1, p0, w_ref, wot_ref, order_ref,
     x_ref, g_ref, dqt_ref, dkt_ref, dvt_ref, ctxt_ref, kept_ref, sent_ref,
     rows_ref, s_ref, dp_ref, pb_ref, ds_ref,
 ):
@@ -243,13 +243,14 @@
 def body(tokens, weights, out_grad):
     quads = [(QUAD, bf16)] * 4
     sems = [pltpu.SemaphoreType.DMA((4, 2))]
-    moves = ((0, 1), (1, 0), (1, 1))
+    moves = ((0, 0), (0, 1), (1, 0), (1, 1))
     sources = [
         pltpu.with_memory_space_constraint(a.transpose(1, 2, 0, 3), pltpu.HBM)
         for a in (tokens, out_grad)
     ]
-    parts = call(pack_kernel, quads, sems, 4, sources, [HBM] * 2)
-    parts = [parts[0]] + [shift(p, *m, False) for p, m in zip(parts[1:], moves)]
+    parts = list(call(pack_kernel, quads, sems, 4, sources, [HBM] * 2))
+    for q in (2, 3, 1):
+        parts[q] = shift(parts[q], *moves[q], False)
     wide = ((4 * FEAT, FEAT), bf16)
     square = ((FEAT, FEAT), bf16)
     turn = ((2 * WIN, 2 * WIN), bf16)
@@ -266,7 +267,7 @@
         [rows] * 2 + [square] * 4 + [half] * 2,
         [pltpu.VMEM((2, 2 * WIN, FEAT), f32)] + [tiles(f32)] * 2 + [tiles(bf16)] * 2,
         20,
-        (*parts, held, turned, order),
+        (parts[2], parts[3], parts[1], parts[0], held, turned, order),
     )
     got = lax.ppermute(sent, "c", [(0, 1), (1, 0)])
     backs = call(
@@ -276,20 +277,20 @@
         12,
         (x, grad, held, dqt, dkt, dvt, ctxt),
     )
-    got, backs = lax.optimization_barrier((got, backs))
+    got, backs = lax.optimization_barrier((got, list(backs)))
     total = (kept.astype(f32) + got.astype(f32)).astype(bf16).reshape(32, 32, FEAT)
     total = lax.all_to_all(total, ("xh", "y", "xl", "zl"), 0, 0, tiled=True)
-    backs = [backs[0]] + [shift(p, *m, True) for p, m in zip(backs[1:], moves)]
+    for q in (2, 3, 1):
+        backs[q] = shift(backs[q], *moves[q], True)
     total = jnp.sum(total.astype(f32), axis=0)
     total, backs[2], backs[3] = lax.optimization_barrier((total, backs[2], backs[3]))
+    total = total.reshape(4, 8, FEAT)
     at = lax.axis_index("zh")
-    for bit in (2, 1):
-        total = total.reshape(2, 8 * bit, FEAT)
-        mine = (at // bit) % 2
-        gone = lax.dynamic_index_in_dim(total, 1 - mine, 0, keepdims=False)
-        held_back = lax.dynamic_index_in_dim(total, mine, 0, keepdims=False)
-        total = held_back + lax.ppermute(gone, "zh", [(i, i ^ bit) for i in range(4)])
-    weight_grads = total
+    chunks = [lax.dynamic_index_in_dim(total, (at + d) % 4, 0, keepdims=False) for d in range(4)]
+    for d in (2, 1, 3):
+        pairs = [(i, (i + d) % 4) for i in range(4)]
+        chunks[d] = lax.ppermute(chunks[d], "zh", pairs)
+    weight_grads = chunks[0] + chunks[2] + (chunks[1] + chunks[3])
     field = ((6, 12, 4, FEAT), bf16)
     results = call(unpack_kernel, [field] * 2, sems, 4, backs, [ANY] * 4, HBM)
     mixed, token_grads = (r.transpose(2, 0, 1, 3) for r in results)

time: 69.2 us -> 68.2 us (0.986)
  waiting for transfers between devices: 24.7 us -> 18.7 us
  starting transfers between devices: 30.3 us -> 35.3 us
    ppermute x2 -> x3, waiting for transfers between devices: 6.71 us -> 0.23 us  [body(): chunks[d] = lax.ppermute(chunks[d], 'zh', pairs)]
    ppermute x2 -> x3, starting transfers between devices: 2.61 us -> 8.83 us  [body(): chunks[d] = lax.ppermute(chunks[d], 'zh', pairs)]
    all_to_all x1, starting transfers between devices: 7.15 us -> 5.49 us  [body(): total = lax.all_to_all(total, ('xh', 'y', 'xl', 'zl'), 0, 0, tiled=True)]
    ppermute x1, starting transfers between devices: 0.81 us -> 2.38 us  [body(): got = lax.ppermute(sent, 'c', [(0, 1), (1, 0)])]
    ppermute x6, starting transfers between devices: 19.7 us -> 18.7 us  [shift(): return lax.ppermute(piece, ALL, pairs)]
  transfers between devices with their start and end apart: 10 -> 11, of which waited for: 6 -> 4; matrix products, arithmetic and copies ran while one was open for 0% -> 0% of each run, Pallas kernels for 4% -> 4%
where the time goes in v4:
time: 68.2 us; the launch traced here: 67.9 us
  starting transfers between devices  35.3 us (52%)
  waiting for transfers between devices  18.7 us (27%)
  Pallas kernels  9.47 us (14%)
  other arithmetic  2.03 us (3%)
  local copies, waits for them, and re-layouts  1.6 us (2%)
  between operations  0.77 us (1%)
    ppermute x6, starting transfers between devices, shift(): return lax.ppermute(piece, ALL, pairs)  18.7 us
    all_to_all x1, waiting for transfers between devices, body(): total = lax.all_to_all(total, ('xh', 'y', 'xl', 'zl'), 0, 0, tiled=True)  11 us
    pallas_call x5, Pallas kernels, call(): pl.pallas_call(kernel, out_shape=[jax.ShapeDtypeStruct(s, d) for s, d in...  9.47 us
    ppermute x3, starting transfers between devices, body(): chunks[d] = lax.ppermute(chunks[d], 'zh', pairs)  8.83 us
    ppermute x6, waiting for transfers between devices, shift(): return lax.ppermute(piece, ALL, pairs)  6.83 us
    all_to_all x1, starting transfers between devices, body(): total = lax.all_to_all(total, ('xh', 'y', 'xl', 'zl'), 0, 0, tiled=True)  5.49 us
    ppermute x1, starting transfers between devices, body(): got = lax.ppermute(sent, 'c', [(0, 1), (1, 0)])  2.38 us
    unnamed x2, local copies, waits for them, and re-layouts  1.59 us
  transfers between devices with their start and end apart: 11, of which 4 were waited for; matrix products, arithmetic and copies ran while one was open for 0% of the time, Pallas kernels for 4%

profile of v4, /device:TPU:1, one launch (start us, length us, event | category | flops | bytes accessed | tf_op | source)
XLA Modules:
  0.0 67.9 jit_solution(16437786279199694968)
XLA Ops:
  0.6 1.2 %shard_map.58 = (bf16[2,3,6,4,512]{4,3,2,1,0:T(4,128)(2,1)S(1)}, bf16[2,3,6,4,512]{4,3,2,1,0:T(4,128)(2,1)S(1)}, bf16[2,3,6,4,512]{4,3,2,1,0:T(4,128)(2,1)S(1)}, bf16[2,3,6,4,512]{4,3,2,1,0:T(4,128)(2,1)S(1)}) custom-call(bf16[6,12,4,512]{3,2,1,0:T(4,128)(2,1)} %bitcast.16, bf16[6,12,4,512]{3,2,1,0:T(4,128)(2,1)} %bitcast.17), custom_call_target="tpu_custom_call" | custom-call | tf_op jit(solution)/shard_map/pallas_call | solution.py:34
  1.9 2.2 %collective-permute-start = (bf16[2,3,6,4,512]{4,3,2,1,0:T(4,128)(2,1)S(1)}, bf16[2,3,6,4,512]{4,3,2,1,0:T(4,128)(2,1)S(1)}, u32[]{:S(2)}, u32[]{:S(2)}) collective-permute-start(bf16[2,3,6,4,512]{4,3,2,1,0:T(4,128)(2,1)S(1)} %get-tuple-element.32), channel_id=1, source_target_pairs={{32,0},{225,1},{226,2},{35,3},{36,4},{229,5},{230,6},{39,7},{40,8}... | collective-permute-start | bytes 442376 | tf_op jit(solution)/shard_map/ppermute | solution.py:240
  4.1 5.2 %collective-permute-start.1 = (bf16[2,3,6,4,512]{4,3,2,1,0:T(4,128)(2,1)S(1)}, bf16[2,3,6,4,512]{4,3,2,1,0:T(4,128)(2,1)S(1)}, u32[]{:S(2)}, u32[]{:S(2)}) collective-permute-start(bf16[2,3,6,4,512]{4,3,2,1,0:T(4,128)(2,1)S(1)} %get-tuple-element.33), channel_id=1, source_target_pairs={{33,0},{226,1},{227,2},{36,3},{37,4},{230,5},{231,6},{40,7},{41,8}... | collective-permute-start | bytes 442376 | tf_op jit(solution)/shard_map/ppermute | solution.py:240
  9.3 4.6 %collective-permute-start.2 = (bf16[2,3,6,4,512]{4,3,2,1,0:T(4,128)(2,1)S(1)}, bf16[2,3,6,4,512]{4,3,2,1,0:T(4,128)(2,1)S(1)}, u32[]{:S(2)}, u32[]{:S(2)}) collective-permute-start(bf16[2,3,6,4,512]{4,3,2,1,0:T(4,128)(2,1)S(1)} %get-tuple-element.34), channel_id=1, source_target_pairs={{1,0},{2,1},{3,2},{4,3},{5,4},{6,5},{7,6},{8,7},{9,8},{10,9},{11,1... | collective-permute-start | bytes 442376 | tf_op jit(solution)/shard_map/ppermute | solution.py:240
  13.8 0.0 copy-start
  13.8 1.6 %copy-done = bf16[2048,512]{1,0:T(8,128)(2,1)S(1)} copy-done((bf16[2048,512]{1,0:T(8,128)(2,1)S(1)}, bf16[2048,512]{1,0:T(8,128)(2,1)}, u32[]{:S(2)}) %copy-start) | copy-done | bytes 2097176
  15.4 0.3 shard_map.59
  15.8 0.0 collective-permute-done.p2
  15.8 0.0 collective-permute-done.1.p3
  15.8 0.0 collective-permute-done.2.p1
  15.8 5.5 %shard_map.60 = (bf16[288,512]{1,0:T(8,128)(2,1)S(1)}, bf16[288,512]{1,0:T(8,128)(2,1)S(1)}, bf16[2,512,144]{2,1,0:T(8,128)(2,1)S(1)}, bf16[2,512,144]{2,1,0:T(8...) custom-call(bf16[2,3,6,4,512]{4,3,2,1,0:T(4,128)(2,1)S(1)} %collecti, ...), custom_call_target="tpu_custom_call" | custom-call | tf_op jit(solution)/shard_map/pallas_call | solution.py:34
  21.3 2.4 %collective-permute-start.3 = (bf16[1024,512]{1,0:T(8,128)(2,1)S(1)}, bf16[1024,512]{1,0:T(8,128)(2,1)S(1)}, u32[]{:S(2)}, u32[]{:S(2)}) collective-permute-start(bf16[1024,512]{1,0:T(8,128)(2,1)S(1)} %get-tuple-element.39), channel_id=1, source_target_pairs={{0,1},{1,0},{2,3},{3,2},{4,5},{5,4},{6,7},{7,6},{8,9},{9,8},{10,11... | collective-permute-start | bytes 3145736 | tf_op jit(solution)/shard_map/ppermute | solution.py:272
  23.7 1.6 %shard_map.61 = (bf16[2,3,6,4,512]{4,3,2,1,0:T(4,128)(2,1)S(1)}, bf16[2,3,6,4,512]{4,3,2,1,0:T(4,128)(2,1)S(1)}, bf16[2,3,6,4,512]{4,3,2,1,0:T(4,128)(2,1)S(1)}, bf16[2,3,6,4,512]{4,3,2,1,0:T(4,128)(2,1)S(1)}) custom-call(bf16[288,512]{1,0:T(8,128)(2,1)S(1)} %get-tuple-element.40.x_ref, bf16[288,512]{1,0:T(8,128)(2,1)S(1)} %get-tuple-element.41.g_ref, ...), custom_call_target="tpu_custom_call" | custom-call | tf_op jit(solution)/shard_map/pallas_call | solution.py:34
  25.2 0.7 %collective-permute-done.3 = bf16[1024,512]{1,0:T(8,128)(2,1)S(1)} collective-permute-done((bf16[1024,512]{1,0:T(8,128)(2,1)S(1)}, bf16[1024,512]{1,0:T(8,128)(2,1)S(1)}, u32[]{:S(2)}, u32[]{:S(2)}) %collective-permute-start.3) | collective-permute-done | bytes 1048608 | tf_op jit(solution)/shard_map/ppermute | solution.py:272
  25.9 1.3 %add_convert_fusion = bf16[1024,512]{1,0:T(8,128)(2,1)} fusion(bf16[1024,512]{1,0:T(8,128)(2,1)S(1)} %collective-permute-done.3, bf16[1024,512]{1,0:T(8,128)(2,1)S(1)} %get-tuple-element.52), kind=kLoop, calls=%fused_computation.1 | loop fusion | flops 2097152 | bytes 3145728 | tf_op jit(solution)/shard_map/convert_element_type | solution.py:281
  27.2 5.5 %all-to-all-start = ((bf16[32,32,512]{2,1,0:T(8,128)(2,1)}), bf16[32,32,512]{2,1,0:T(8,128)(2,1)S(1)}, u32[]{:S(2)}, u32[]{:S(2)}) async-start(bf16[32,32,512]{2,1,0:T(8,128)(2,1)} %bitcast.2), calls=%async_computation | async-start | bytes 2097152 | tf_op jit(solution)/shard_map/all_to_all | solution.py:282
  32.7 5.0 %collective-permute-start.5 = (bf16[2,3,6,4,512]{4,3,2,1,0:T(4,128)(2,1)S(1)}, bf16[2,3,6,4,512]{4,3,2,1,0:T(4,128)(2,1)S(1)}, u32[]{:S(2)}, u32[]{:S(2)}) collective-permute-start(bf16[2,3,6,4,512]{4,3,2,1,0:T(4,128)(2,1)S(1)} %get-tuple-element.54), channel_id=1, source_target_pairs={{0,32},{1,225},{2,226},{3,35},{4,36},{5,229},{6,230},{7,39},{8,40}... | collective-permute-start | bytes 442376 | tf_op jit(solution)/shard_map/ppermute | solution.py:240
  37.7 1.4 %collective-permute-start.6 = (bf16[2,3,6,4,512]{4,3,2,1,0:T(4,128)(2,1)S(1)}, bf16[2,3,6,4,512]{4,3,2,1,0:T(4,128)(2,1)S(1)}, u32[]{:S(2)}, u32[]{:S(2)}) collective-permute-start(bf16[2,3,6,4,512]{4,3,2,1,0:T(4,128)(2,1)S(1)} %get-tuple-element.55), channel_id=1, source_target_pairs={{0,33},{1,226},{2,227},{3,36},{4,37},{5,230},{6,231},{7,40},{8,41}... | collective-permute-start | bytes 442376 | tf_op jit(solution)/shard_map/ppermute | solution.py:240
  39.1 0.3 collective-permute-start.4
  39.4 11.0 %all-to-all-done = bf16[32,32,512]{2,1,0:T(8,128)(2,1)S(1)} async-done(((bf16[32,32,512]{2,1,0:T(8,128)(2,1)}), bf16[32,32,512]{2,1,0:T(8,128)(2,1)S(1)}, u32[]{:S(2)}, u32[]{:S(2)}) %all-to-all-start) | async-done | bytes 1048608 | tf_op jit(solution)/shard_map/all_to_all | solution.py:282
  50.4 0.2 convert_reduce_fusion
  50.5 0.0 collective-permute-done.5.p2
  50.5 6.8 %collective-permute-done.6.p3 = bf16[2,3,6,4,512]{4,3,2,1,0:T(4,128)(2,1)S(1)} collective-permute-done((bf16[2,3,6,4,512]{4,3,2,1,0:T(4,128)(2,1)S(1)}, bf16[2,3,6,4,512]{4,3,2,1,0:T(4,128)(2,1)S(1)}, u32[]{:S(2)}, u32[]{:S(2)}) %collective-permute-start.6) | collective-permute-done | bytes 147488 | tf_op jit(solution)/shard_map/ppermute | solution.py:240
  57.4 5.3 %collective-permute-start.7 = (f32[8,512]{1,0:T(8,128)S(1)}, f32[8,512]{1,0:T(8,128)S(1)}, u32[]{:S(2)}, u32[]{:S(2)}) collective-permute-start(f32[8,512]{1,0:T(8,128)S(1)} %get-tuple-element.63), channel_id=1, source_target_pairs={{0,16},{8,24},{16,0},{24,8},{1,17},{9,25},{17,1},{25,9},{2,18},{10... | collective-permute-start | bytes 49160 | tf_op jit(solution)/shard_map/ppermute | solution.py:292
  62.6 0.9 %collective-permute-start.8 = (f32[8,512]{1,0:T(8,128)S(1)}, f32[8,512]{1,0:T(8,128)S(1)}, u32[]{:S(2)}, u32[]{:S(2)}) collective-permute-start(f32[8,512]{1,0:T(8,128)S(1)} %get-tuple-element.62), channel_id=1, source_target_pairs={{0,8},{8,16},{16,24},{24,0},{1,9},{9,17},{17,25},{25,1},{2,10},{10... | collective-permute-start | bytes 49160 | tf_op jit(solution)/shard_map/ppermute | solution.py:292
  63.5 2.7 %collective-permute-start.9 = (f32[8,512]{1,0:T(8,128)S(1)}, f32[8,512]{1,0:T(8,128)S(1)}, u32[]{:S(2)}, u32[]{:S(2)}) collective-permute-start(f32[8,512]{1,0:T(8,128)S(1)} %get-tuple-element.61), channel_id=1, source_target_pairs={{0,24},{8,0},{16,8},{24,16},{1,25},{9,1},{17,9},{25,17},{2,26},{10... | collective-permute-start | bytes 49160 | tf_op jit(solution)/shard_map/ppermute | solution.py:292
  66.2 0.0 collective-permute-done.4.p1
  66.2 0.9 %shard_map.62 = (bf16[6,12,4,512]{3,2,1,0:T(4,128)(2,1)}, bf16[6,12,4,512]{3,2,1,0:T(4,128)(2,1)}) custom-call(bf16[2,3,6,4,512]{4,3,2,1,0:T(4,128)(2,1)S(1)} %get-tuple-element.50.p0, bf16[2,3,6,4,512]{4,3,2,1,0:T(4,128)(2,1)S(1)} %collective-permute-done.4.p1, bf16[2,3,6,4,512]{4,3,2,1,0:T(4,128)(2,1)S(1)} %collective-permute-done.5.p2, ...), custom_call_target="tpu_custom_call" | custom-call | tf_op jit(solution)/shard_map/pallas_call | solution.py:34
  67.1 0.0 collective-permute-done.7
  67.1 0.2 collective-permute-done.8
  67.3 0.0 collective-permute-done.9
  67.3 0.6 fusion
  (1 shorter events, 0.0 us)
Async XLA Ops:
  1.9 13.9 %collective-permute-start = (bf16[2,3,6,4,512]{4,3,2,1,0:T(4,128)(2,1)S(1)}, bf16[2,3,6,4,512]{4,3,2,1,0:T(4,128)(2,1)S(1)}, u32[]{:S(2)}, u32[]{:S(2)}) collective-permute-start(bf16[2,3,6,4,512]{4,3,2,1,0:T(4,128)(2,1)S(1)} %get-tuple-element.32), channel_id=1, source_target_pairs={{32,0},{225,1},{226,2},{35,3},{36,4},{229,5},{230,6},{39,7},{40,8}... | collective-permute-start | bytes 442376 | tf_op jit(solution)/shard_map/ppermute | solution.py:240
  4.1 11.7 %collective-permute-start.1 = (bf16[2,3,6,4,512]{4,3,2,1,0:T(4,128)(2,1)S(1)}, bf16[2,3,6,4,512]{4,3,2,1,0:T(4,128)(2,1)S(1)}, u32[]{:S(2)}, u32[]{:S(2)}) collective-permute-start(bf16[2,3,6,4,512]{4,3,2,1,0:T(4,128)(2,1)S(1)} %get-tuple-element.33), channel_id=1, source_target_pairs={{33,0},{226,1},{227,2},{36,3},{37,4},{230,5},{231,6},{40,7},{41,8}... | collective-permute-start | bytes 442376 | tf_op jit(solution)/shard_map/ppermute | solution.py:240
  9.3 6.5 %collective-permute-start.2 = (bf16[2,3,6,4,512]{4,3,2,1,0:T(4,128)(2,1)S(1)}, bf16[2,3,6,4,512]{4,3,2,1,0:T(4,128)(2,1)S(1)}, u32[]{:S(2)}, u32[]{:S(2)}) collective-permute-start(bf16[2,3,6,4,512]{4,3,2,1,0:T(4,128)(2,1)S(1)} %get-tuple-element.34), channel_id=1, source_target_pairs={{1,0},{2,1},{3,2},{4,3},{5,4},{6,5},{7,6},{8,7},{9,8},{10,9},{11,1... | collective-permute-start | bytes 442376 | tf_op jit(solution)/shard_map/ppermute | solution.py:240
  13.8 1.6 %copy-start = (bf16[2048,512]{1,0:T(8,128)(2,1)S(1)}, bf16[2048,512]{1,0:T(8,128)(2,1)}, u32[]{:S(2)}) copy-start(bf16[2048,512]{1,0:T(8,128)(2,1)} %w_ref.1) | copy-start | bytes 6291460
  21.3 4.7 %collective-permute-start.3 = (bf16[1024,512]{1,0:T(8,128)(2,1)S(1)}, bf16[1024,512]{1,0:T(8,128)(2,1)S(1)}, u32[]{:S(2)}, u32[]{:S(2)}) collective-permute-start(bf16[1024,512]{1,0:T(8,128)(2,1)S(1)} %get-tuple-element.39), channel_id=1, source_target_pairs={{0,1},{1,0},{2,3},{3,2},{4,5},{5,4},{6,7},{7,6},{8,9},{9,8},{10,11... | collective-permute-start | bytes 3145736 | tf_op jit(solution)/shard_map/ppermute | solution.py:272
  27.2 23.2 %all-to-all-start = ((bf16[32,32,512]{2,1,0:T(8,128)(2,1)}), bf16[32,32,512]{2,1,0:T(8,128)(2,1)S(1)}, u32[]{:S(2)}, u32[]{:S(2)}) async-start(bf16[32,32,512]{2,1,0:T(8,128)(2,1)} %bitcast.2), calls=%async_computation | async-start | bytes 2097152 | tf_op jit(solution)/shard_map/all_to_all | solution.py:282
  32.7 17.8 %collective-permute-start.5 = (bf16[2,3,6,4,512]{4,3,2,1,0:T(4,128)(2,1)S(1)}, bf16[2,3,6,4,512]{4,3,2,1,0:T(4,128)(2,1)S(1)}, u32[]{:S(2)}, u32[]{:S(2)}) collective-permute-start(bf16[2,3,6,4,512]{4,3,2,1,0:T(4,128)(2,1)S(1)} %get-tuple-element.54), channel_id=1, source_target_pairs={{0,32},{1,225},{2,226},{3,35},{4,36},{5,229},{6,230},{7,39},{8,40}... | collective-permute-start | bytes 442376 | tf_op jit(solution)/shard_map/ppermute | solution.py:240
  37.7 19.6 %collective-permute-start.6 = (bf16[2,3,6,4,512]{4,3,2,1,0:T(4,128)(2,1)S(1)}, bf16[2,3,6,4,512]{4,3,2,1,0:T(4,128)(2,1)S(1)}, u32[]{:S(2)}, u32[]{:S(2)}) collective-permute-start(bf16[2,3,6,4,512]{4,3,2,1,0:T(4,128)(2,1)S(1)} %get-tuple-element.55), channel_id=1, source_target_pairs={{0,33},{1,226},{2,227},{3,36},{4,37},{5,230},{6,231},{7,40},{8,41}... | collective-permute-start | bytes 442376 | tf_op jit(solution)/shard_map/ppermute | solution.py:240
  39.1 27.1 %collective-permute-start.4 = (bf16[2,3,6,4,512]{4,3,2,1,0:T(4,128)(2,1)S(1)}, bf16[2,3,6,4,512]{4,3,2,1,0:T(4,128)(2,1)S(1)}, u32[]{:S(2)}, u32[]{:S(2)}) collective-permute-start(bf16[2,3,6,4,512]{4,3,2,1,0:T(4,128)(2,1)S(1)} %get-tuple-element.51), channel_id=1, source_target_pairs={{0,1},{1,2},{2,3},{3,4},{4,5},{5,6},{6,7},{7,8},{8,9},{9,10},{10,1... | collective-permute-start | bytes 442376 | tf_op jit(solution)/shard_map/ppermute | solution.py:240
  57.4 9.7 %collective-permute-start.7 = (f32[8,512]{1,0:T(8,128)S(1)}, f32[8,512]{1,0:T(8,128)S(1)}, u32[]{:S(2)}, u32[]{:S(2)}) collective-permute-start(f32[8,512]{1,0:T(8,128)S(1)} %get-tuple-element.63), channel_id=1, source_target_pairs={{0,16},{8,24},{16,0},{24,8},{1,17},{9,25},{17,1},{25,9},{2,18},{10... | collective-permute-start | bytes 49160 | tf_op jit(solution)/shard_map/ppermute | solution.py:292
  62.6 4.7 %collective-permute-start.8 = (f32[8,512]{1,0:T(8,128)S(1)}, f32[8,512]{1,0:T(8,128)S(1)}, u32[]{:S(2)}, u32[]{:S(2)}) collective-permute-start(f32[8,512]{1,0:T(8,128)S(1)} %get-tuple-element.62), channel_id=1, source_target_pairs={{0,8},{8,16},{16,24},{24,0},{1,9},{9,17},{17,25},{25,1},{2,10},{10... | collective-permute-start | bytes 49160 | tf_op jit(solution)/shard_map/ppermute | solution.py:292
  63.5 3.8 %collective-permute-start.9 = (f32[8,512]{1,0:T(8,128)S(1)}, f32[8,512]{1,0:T(8,128)S(1)}, u32[]{:S(2)}, u32[]{:S(2)}) collective-permute-start(f32[8,512]{1,0:T(8,128)S(1)} %get-tuple-element.61), channel_id=1, source_target_pairs={{0,24},{8,0},{16,8},{24,16},{1,25},{9,1},{17,9},{25,17},{2,26},{10... | collective-permute-start | bytes 49160 | tf_op jit(solution)/shard_map/ppermute | solution.py:292

commit v5 on v4

--- a/solution.py
+++ b/solution.py
@@ -283,16 +283,16 @@
     for q in (2, 3, 1):
         backs[q] = shift(backs[q], *moves[q], True)
     total = jnp.sum(total.astype(f32), axis=0)
-    total, backs[2], backs[3] = lax.optimization_barrier((total, backs[2], backs[3]))
     total = total.reshape(4, 8, FEAT)
     at = lax.axis_index("zh")
     chunks = [lax.dynamic_index_in_dim(total, (at + d) % 4, 0, keepdims=False) for d in range(4)]
     for d in (2, 1, 3):
         pairs = [(i, (i + d) % 4) for i in range(4)]
         chunks[d] = lax.ppermute(chunks[d], "zh", pairs)
-    weight_grads = chunks[0] + chunks[2] + (chunks[1] + chunks[3])
     field = ((6, 12, 4, FEAT), bf16)
     results = call(unpack_kernel, [field] * 2, sems, 4, backs, [ANY] * 4, HBM)
+    chunks, results = lax.optimization_barrier((chunks, results))
+    weight_grads = chunks[0] + chunks[2] + (chunks[1] + chunks[3])
     mixed, token_grads = (r.transpose(2, 0, 1, 3) for r in results)
     return mixed, token_grads, weight_grads
 

time: 68.2 us -> 64.7 us (0.949)
  the two profiles are of different devices: /device:TPU:1 before, /device:TPU:2 now
where the time goes in v5:
time: 64.7 us; the launch traced here: 64.4 us
  starting transfers between devices  33.5 us (52%)
  waiting for transfers between devices  17 us (26%)
  Pallas kernels  9.47 us (15%)
  other arithmetic  2.03 us (3%)
  local copies, waits for them, and re-layouts  1.6 us (2%)
  between operations  0.77 us (1%)
    ppermute x6, starting transfers between devices, shift(): return lax.ppermute(piece, ALL, pairs)  13.2 us
    all_to_all x1, waiting for transfers between devices, body(): total = lax.all_to_all(total, ('xh', 'y', 'xl', 'zl'), 0, 0, tiled=True)  12.8 us
    ppermute x3, starting transfers between devices, body(): chunks[d] = lax.ppermute(chunks[d], 'zh', pairs)  10.5 us
    pallas_call x5, Pallas kernels, call(): pl.pallas_call(kernel, out_shape=[jax.ShapeDtypeStruct(s, d) for s, d in...  9.47 us
    all_to_all x1, starting transfers between devices, body(): total = lax.all_to_all(total, ('xh', 'y', 'xl', 'zl'), 0, 0, tiled=True)  9.1 us
    ppermute x6, waiting for transfers between devices, shift(): return lax.ppermute(piece, ALL, pairs)  2.95 us
    unnamed x2, local copies, waits for them, and re-layouts  1.59 us
  transfers between devices with their start and end apart: 11, of which 5 were waited for; matrix products, arithmetic and copies ran while one was open for 0% of the time, Pallas kernels for 4%

profile of v5, /device:TPU:2, one launch (start us, length us, event | category | flops | bytes accessed | tf_op | source)
XLA Modules:
  0.0 64.4 jit_solution(17212361179373959891)
XLA Ops:
  0.6 1.2 %shard_map.58 = (bf16[2,3,6,4,512]{4,3,2,1,0:T(4,128)(2,1)S(1)}, bf16[2,3,6,4,512]{4,3,2,1,0:T(4,128)(2,1)S(1)}, bf16[2,3,6,4,512]{4,3,2,1,0:T(4,128)(2,1)S(1)}, bf16[2,3,6,4,512]{4,3,2,1,0:T(4,128)(2,1)S(1)}) custom-call(bf16[6,12,4,512]{3,2,1,0:T(4,128)(2,1)} %bitcast.14, bf16[6,12,4,512]{3,2,1,0:T(4,128)(2,1)} %bitcast.15), custom_call_target="tpu_custom_call" | custom-call | tf_op jit(solution)/shard_map/pallas_call | solution.py:34
  1.9 1.7 %collective-permute-start = (bf16[2,3,6,4,512]{4,3,2,1,0:T(4,128)(2,1)S(1)}, bf16[2,3,6,4,512]{4,3,2,1,0:T(4,128)(2,1)S(1)}, u32[]{:S(2)}, u32[]{:S(2)}) collective-permute-start(bf16[2,3,6,4,512]{4,3,2,1,0:T(4,128)(2,1)S(1)} %get-tuple-element.35), channel_id=1, source_target_pairs={{32,0},{225,1},{226,2},{35,3},{36,4},{229,5},{230,6},{39,7},{40,8}... | collective-permute-start | bytes 442376 | tf_op jit(solution)/shard_map/ppermute | solution.py:240
  3.5 0.7 %collective-permute-start.1 = (bf16[2,3,6,4,512]{4,3,2,1,0:T(4,128)(2,1)S(1)}, bf16[2,3,6,4,512]{4,3,2,1,0:T(4,128)(2,1)S(1)}, u32[]{:S(2)}, u32[]{:S(2)}) collective-permute-start(bf16[2,3,6,4,512]{4,3,2,1,0:T(4,128)(2,1)S(1)} %get-tuple-element.36), channel_id=1, source_target_pairs={{33,0},{226,1},{227,2},{36,3},{37,4},{230,5},{231,6},{40,7},{41,8}... | collective-permute-start | bytes 442376 | tf_op jit(solution)/shard_map/ppermute | solution.py:240
  4.2 4.2 %collective-permute-start.2 = (bf16[2,3,6,4,512]{4,3,2,1,0:T(4,128)(2,1)S(1)}, bf16[2,3,6,4,512]{4,3,2,1,0:T(4,128)(2,1)S(1)}, u32[]{:S(2)}, u32[]{:S(2)}) collective-permute-start(bf16[2,3,6,4,512]{4,3,2,1,0:T(4,128)(2,1)S(1)} %get-tuple-element.37), channel_id=1, source_target_pairs={{1,0},{2,1},{3,2},{4,3},{5,4},{6,5},{7,6},{8,7},{9,8},{10,9},{11,1... | collective-permute-start | bytes 442376 | tf_op jit(solution)/shard_map/ppermute | solution.py:240
  8.4 0.0 copy-start
  8.4 1.6 %copy-done = bf16[2048,512]{1,0:T(8,128)(2,1)S(1)} copy-done((bf16[2048,512]{1,0:T(8,128)(2,1)S(1)}, bf16[2048,512]{1,0:T(8,128)(2,1)}, u32[]{:S(2)}) %copy-start) | copy-done | bytes 2097176
  10.0 0.3 shard_map.59
  10.3 0.9 %collective-permute-done.p2 = bf16[2,3,6,4,512]{4,3,2,1,0:T(4,128)(2,1)S(1)} collective-permute-done((bf16[2,3,6,4,512]{4,3,2,1,0:T(4,128)(2,1)S(1)}, bf16[2,3,6,4,512]{4,3,2,1,0:T(4,128)(2,1)S(1)}, u32[]{:S(2)}, u32[]{:S(2)}) %collective-permute-start) | collective-permute-done | bytes 147488 | tf_op jit(solution)/shard_map/ppermute | solution.py:240
  11.3 2.0 %collective-permute-done.1.p3 = bf16[2,3,6,4,512]{4,3,2,1,0:T(4,128)(2,1)S(1)} collective-permute-done((bf16[2,3,6,4,512]{4,3,2,1,0:T(4,128)(2,1)S(1)}, bf16[2,3,6,4,512]{4,3,2,1,0:T(4,128)(2,1)S(1)}, u32[]{:S(2)}, u32[]{:S(2)}) %collective-permute-start.1) | collective-permute-done | bytes 147488 | tf_op jit(solution)/shard_map/ppermute | solution.py:240
  13.3 0.0 collective-permute-done.2.p1
  13.3 5.5 %shard_map.60 = (bf16[288,512]{1,0:T(8,128)(2,1)S(1)}, bf16[288,512]{1,0:T(8,128)(2,1)S(1)}, bf16[2,512,144]{2,1,0:T(8,128)(2,1)S(1)}, bf16[2,512,144]{2,1,0:T(8...) custom-call(bf16[2,3,6,4,512]{4,3,2,1,0:T(4,128)(2,1)S(1)} %collecti, ...), custom_call_target="tpu_custom_call" | custom-call | tf_op jit(solution)/shard_map/pallas_call | solution.py:34
  18.8 0.7 %collective-permute-start.3 = (bf16[1024,512]{1,0:T(8,128)(2,1)S(1)}, bf16[1024,512]{1,0:T(8,128)(2,1)S(1)}, u32[]{:S(2)}, u32[]{:S(2)}) collective-permute-start(bf16[1024,512]{1,0:T(8,128)(2,1)S(1)} %get-tuple-element.43), channel_id=1, source_target_pairs={{0,1},{1,0},{2,3},{3,2},{4,5},{5,4},{6,7},{7,6},{8,9},{9,8},{10,11... | collective-permute-start | bytes 3145736 | tf_op jit(solution)/shard_map/ppermute | solution.py:272
  19.5 1.6 %shard_map.61 = (bf16[2,3,6,4,512]{4,3,2,1,0:T(4,128)(2,1)S(1)}, bf16[2,3,6,4,512]{4,3,2,1,0:T(4,128)(2,1)S(1)}, bf16[2,3,6,4,512]{4,3,2,1,0:T(4,128)(2,1)S(1)}, bf16[2,3,6,4,512]{4,3,2,1,0:T(4,128)(2,1)S(1)}) custom-call(bf16[288,512]{1,0:T(8,128)(2,1)S(1)} %get-tuple-element.44.x_ref, bf16[288,512]{1,0:T(8,128)(2,1)S(1)} %get-tuple-element.45.g_ref, ...), custom_call_target="tpu_custom_call" | custom-call | tf_op jit(solution)/shard_map/pallas_call | solution.py:34
  21.1 0.7 %collective-permute-done.3 = bf16[1024,512]{1,0:T(8,128)(2,1)S(1)} collective-permute-done((bf16[1024,512]{1,0:T(8,128)(2,1)S(1)}, bf16[1024,512]{1,0:T(8,128)(2,1)S(1)}, u32[]{:S(2)}, u32[]{:S(2)}) %collective-permute-start.3) | collective-permute-done | bytes 1048608 | tf_op jit(solution)/shard_map/ppermute | solution.py:272
  21.8 1.3 %add_convert_fusion = bf16[1024,512]{1,0:T(8,128)(2,1)} fusion(bf16[1024,512]{1,0:T(8,128)(2,1)S(1)} %collective-permute-done.3, bf16[1024,512]{1,0:T(8,128)(2,1)S(1)} %get-tuple-element.42), kind=kLoop, calls=%fused_computation.1 | loop fusion | flops 2097152 | bytes 3145728 | tf_op jit(solution)/shard_map/convert_element_type | solution.py:281
  23.0 9.1 %all-to-all-start = ((bf16[32,32,512]{2,1,0:T(8,128)(2,1)}), bf16[32,32,512]{2,1,0:T(8,128)(2,1)S(1)}, u32[]{:S(2)}, u32[]{:S(2)}) async-start(bf16[32,32,512]{2,1,0:T(8,128)(2,1)} %bitcast.2), calls=%async_computation | async-start | bytes 2097152 | tf_op jit(solution)/shard_map/all_to_all | solution.py:282
  32.2 0.1 collective-permute-start.7
  32.3 4.3 %collective-permute-start.8 = (bf16[2,3,6,4,512]{4,3,2,1,0:T(4,128)(2,1)S(1)}, bf16[2,3,6,4,512]{4,3,2,1,0:T(4,128)(2,1)S(1)}, u32[]{:S(2)}, u32[]{:S(2)}) collective-permute-start(bf16[2,3,6,4,512]{4,3,2,1,0:T(4,128)(2,1)S(1)} %get-tuple-element.57), channel_id=1, source_target_pairs={{0,32},{1,225},{2,226},{3,35},{4,36},{5,229},{6,230},{7,39},{8,40}... | collective-permute-start | bytes 442376 | tf_op jit(solution)/shard_map/ppermute | solution.py:240
  36.6 2.2 %collective-permute-start.9 = (bf16[2,3,6,4,512]{4,3,2,1,0:T(4,128)(2,1)S(1)}, bf16[2,3,6,4,512]{4,3,2,1,0:T(4,128)(2,1)S(1)}, u32[]{:S(2)}, u32[]{:S(2)}) collective-permute-start(bf16[2,3,6,4,512]{4,3,2,1,0:T(4,128)(2,1)S(1)} %get-tuple-element.58), channel_id=1, source_target_pairs={{0,33},{1,226},{2,227},{3,36},{4,37},{5,230},{6,231},{7,40},{8,41}... | collective-permute-start | bytes 442376 | tf_op jit(solution)/shard_map/ppermute | solution.py:240
  38.8 12.8 %all-to-all-done = bf16[32,32,512]{2,1,0:T(8,128)(2,1)S(1)} async-done(((bf16[32,32,512]{2,1,0:T(8,128)(2,1)}), bf16[32,32,512]{2,1,0:T(8,128)(2,1)S(1)}, u32[]{:S(2)}, u32[]{:S(2)}) %all-to-all-start) | async-done | bytes 1048608 | tf_op jit(solution)/shard_map/all_to_all | solution.py:282
  51.6 0.2 convert_reduce_fusion
  51.8 2.1 %collective-permute-start.4 = (f32[8,512]{1,0:T(8,128)S(1)}, f32[8,512]{1,0:T(8,128)S(1)}, u32[]{:S(2)}, u32[]{:S(2)}) collective-permute-start(f32[8,512]{1,0:T(8,128)S(1)} %get-tuple-element.69), channel_id=1, source_target_pairs={{0,8},{8,16},{16,24},{24,0},{1,9},{9,17},{17,25},{25,1},{2,10},{10... | collective-permute-start | bytes 49160 | tf_op jit(solution)/shard_map/ppermute | solution.py:291
  53.9 5.2 %collective-permute-start.5 = (f32[8,512]{1,0:T(8,128)S(1)}, f32[8,512]{1,0:T(8,128)S(1)}, u32[]{:S(2)}, u32[]{:S(2)}) collective-permute-start(f32[8,512]{1,0:T(8,128)S(1)} %get-tuple-element.68), channel_id=1, source_target_pairs={{0,16},{8,24},{16,0},{24,8},{1,17},{9,25},{17,1},{25,9},{2,18},{10... | collective-permute-start | bytes 49160 | tf_op jit(solution)/shard_map/ppermute | solution.py:291
  59.2 0.0 collective-permute-done.7.p1
  59.2 3.1 %collective-permute-start.6 = (f32[8,512]{1,0:T(8,128)S(1)}, f32[8,512]{1,0:T(8,128)S(1)}, u32[]{:S(2)}, u32[]{:S(2)}) collective-permute-start(f32[8,512]{1,0:T(8,128)S(1)} %get-tuple-element.67), channel_id=1, source_target_pairs={{0,24},{8,0},{16,8},{24,16},{1,25},{9,1},{17,9},{25,17},{2,26},{10... | collective-permute-start | bytes 49160 | tf_op jit(solution)/shard_map/ppermute | solution.py:291
  62.3 0.0 collective-permute-done.8.p2
  62.3 0.0 collective-permute-done.9.p3
  62.3 0.9 %shard_map.62 = (bf16[6,12,4,512]{3,2,1,0:T(4,128)(2,1)}, bf16[6,12,4,512]{3,2,1,0:T(4,128)(2,1)}) custom-call(bf16[2,3,6,4,512]{4,3,2,1,0:T(4,128)(2,1)S(1)} %get-tuple-element.55.p0, bf16[2,3,6,4,512]{4,3,2,1,0:T(4,128)(2,1)S(1)} %collective-permute-done.7.p1, bf16[2,3,6,4,512]{4,3,2,1,0:T(4,128)(2,1)S(1)} %collective-permute-done.8.p2, ...), custom_call_target="tpu_custom_call" | custom-call | tf_op jit(solution)/shard_map/pallas_call | solution.py:34
  63.2 0.0 collective-permute-done.4
  63.2 0.0 collective-permute-done.5
  63.2 0.6 collective-permute-done.6
  63.8 0.6 add_add_fusion
  (1 shorter events, 0.0 us)
Async XLA Ops:
  1.9 9.4 %collective-permute-start = (bf16[2,3,6,4,512]{4,3,2,1,0:T(4,128)(2,1)S(1)}, bf16[2,3,6,4,512]{4,3,2,1,0:T(4,128)(2,1)S(1)}, u32[]{:S(2)}, u32[]{:S(2)}) collective-permute-start(bf16[2,3,6,4,512]{4,3,2,1,0:T(4,128)(2,1)S(1)} %get-tuple-element.35), channel_id=1, source_target_pairs={{32,0},{225,1},{226,2},{35,3},{36,4},{229,5},{230,6},{39,7},{40,8}... | collective-permute-start | bytes 442376 | tf_op jit(solution)/shard_map/ppermute | solution.py:240
  3.5 9.8 %collective-permute-start.1 = (bf16[2,3,6,4,512]{4,3,2,1,0:T(4,128)(2,1)S(1)}, bf16[2,3,6,4,512]{4,3,2,1,0:T(4,128)(2,1)S(1)}, u32[]{:S(2)}, u32[]{:S(2)}) collective-permute-start(bf16[2,3,6,4,512]{4,3,2,1,0:T(4,128)(2,1)S(1)} %get-tuple-element.36), channel_id=1, source_target_pairs={{33,0},{226,1},{227,2},{36,3},{37,4},{230,5},{231,6},{40,7},{41,8}... | collective-permute-start | bytes 442376 | tf_op jit(solution)/shard_map/ppermute | solution.py:240
  4.2 9.1 %collective-permute-start.2 = (bf16[2,3,6,4,512]{4,3,2,1,0:T(4,128)(2,1)S(1)}, bf16[2,3,6,4,512]{4,3,2,1,0:T(4,128)(2,1)S(1)}, u32[]{:S(2)}, u32[]{:S(2)}) collective-permute-start(bf16[2,3,6,4,512]{4,3,2,1,0:T(4,128)(2,1)S(1)} %get-tuple-element.37), channel_id=1, source_target_pairs={{1,0},{2,1},{3,2},{4,3},{5,4},{6,5},{7,6},{8,7},{9,8},{10,9},{11,1... | collective-permute-start | bytes 442376 | tf_op jit(solution)/shard_map/ppermute | solution.py:240
  8.4 1.6 %copy-start = (bf16[2048,512]{1,0:T(8,128)(2,1)S(1)}, bf16[2048,512]{1,0:T(8,128)(2,1)}, u32[]{:S(2)}) copy-start(bf16[2048,512]{1,0:T(8,128)(2,1)} %w_ref.1) | copy-start | bytes 6291460
  18.8 3.0 %collective-permute-start.3 = (bf16[1024,512]{1,0:T(8,128)(2,1)S(1)}, bf16[1024,512]{1,0:T(8,128)(2,1)S(1)}, u32[]{:S(2)}, u32[]{:S(2)}) collective-permute-start(bf16[1024,512]{1,0:T(8,128)(2,1)S(1)} %get-tuple-element.43), channel_id=1, source_target_pairs={{0,1},{1,0},{2,3},{3,2},{4,5},{5,4},{6,7},{7,6},{8,9},{9,8},{10,11... | collective-permute-start | bytes 3145736 | tf_op jit(solution)/shard_map/ppermute | solution.py:272
  23.0 28.6 %all-to-all-start = ((bf16[32,32,512]{2,1,0:T(8,128)(2,1)}), bf16[32,32,512]{2,1,0:T(8,128)(2,1)S(1)}, u32[]{:S(2)}, u32[]{:S(2)}) async-start(bf16[32,32,512]{2,1,0:T(8,128)(2,1)} %bitcast.2), calls=%async_computation | async-start | bytes 2097152 | tf_op jit(solution)/shard_map/all_to_all | solution.py:282
  32.2 27.0 %collective-permute-start.7 = (bf16[2,3,6,4,512]{4,3,2,1,0:T(4,128)(2,1)S(1)}, bf16[2,3,6,4,512]{4,3,2,1,0:T(4,128)(2,1)S(1)}, u32[]{:S(2)}, u32[]{:S(2)}) collective-permute-start(bf16[2,3,6,4,512]{4,3,2,1,0:T(4,128)(2,1)S(1)} %get-tuple-element.56), channel_id=1, source_target_pairs={{0,1},{1,2},{2,3},{3,4},{4,5},{5,6},{6,7},{7,8},{8,9},{9,10},{10,1... | collective-permute-start | bytes 442376 | tf_op jit(solution)/shard_map/ppermute | solution.py:240
  32.3 30.0 %collective-permute-start.8 = (bf16[2,3,6,4,512]{4,3,2,1,0:T(4,128)(2,1)S(1)}, bf16[2,3,6,4,512]{4,3,2,1,0:T(4,128)(2,1)S(1)}, u32[]{:S(2)}, u32[]{:S(2)}) collective-permute-start(bf16[2,3,6,4,512]{4,3,2,1,0:T(4,128)(2,1)S(1)} %get-tuple-element.57), channel_id=1, source_target_pairs={{0,32},{1,225},{2,226},{3,35},{4,36},{5,229},{6,230},{7,39},{8,40}... | collective-permute-start | bytes 442376 | tf_op jit(solution)/shard_map/ppermute | solution.py:240
  36.6 25.6 %collective-permute-start.9 = (bf16[2,3,6,4,512]{4,3,2,1,0:T(4,128)(2,1)S(1)}, bf16[2,3,6,4,512]{4,3,2,1,0:T(4,128)(2,1)S(1)}, u32[]{:S(2)}, u32[]{:S(2)}) collective-permute-start(bf16[2,3,6,4,512]{4,3,2,1,0:T(4,128)(2,1)S(1)} %get-tuple-element.58), channel_id=1, source_target_pairs={{0,33},{1,226},{2,227},{3,36},{4,37},{5,230},{6,231},{7,40},{8,41}... | collective-permute-start | bytes 442376 | tf_op jit(solution)/shard_map/ppermute | solution.py:240
  51.8 11.4 %collective-permute-start.4 = (f32[8,512]{1,0:T(8,128)S(1)}, f32[8,512]{1,0:T(8,128)S(1)}, u32[]{:S(2)}, u32[]{:S(2)}) collective-permute-start(f32[8,512]{1,0:T(8,128)S(1)} %get-tuple-element.69), channel_id=1, source_target_pairs={{0,8},{8,16},{16,24},{24,0},{1,9},{9,17},{17,25},{25,1},{2,10},{10... | collective-permute-start | bytes 49160 | tf_op jit(solution)/shard_map/ppermute | solution.py:291
  53.9 9.3 %collective-permute-start.5 = (f32[8,512]{1,0:T(8,128)S(1)}, f32[8,512]{1,0:T(8,128)S(1)}, u32[]{:S(2)}, u32[]{:S(2)}) collective-permute-start(f32[8,512]{1,0:T(8,128)S(1)} %get-tuple-element.68), channel_id=1, source_target_pairs={{0,16},{8,24},{16,0},{24,8},{1,17},{9,25},{17,1},{25,9},{2,18},{10... | collective-permute-start | bytes 49160 | tf_op jit(solution)/shard_map/ppermute | solution.py:291
  59.2 4.6 %collective-permute-start.6 = (f32[8,512]{1,0:T(8,128)S(1)}, f32[8,512]{1,0:T(8,128)S(1)}, u32[]{:S(2)}, u32[]{:S(2)}) collective-permute-start(f32[8,512]{1,0:T(8,128)S(1)} %get-tuple-element.67), channel_id=1, source_target_pairs={{0,24},{8,0},{16,8},{24,16},{1,25},{9,1},{17,9},{25,17},{2,26},{10... | collective-permute-start | bytes 49160 | tf_op jit(solution)/shard_map/ppermute | solution.py:291

commit v6 on v5

--- a/solution.py
+++ b/solution.py
@@ -107,10 +107,10 @@
                 for c in range(2):
                     at = h * HEAD + zl * 32 + xl * 16 + c * 8
                     pair = [block[at : at + 8], block[at + HEAD : at + HEAD + 8]]
-                    two.append(jnp.concatenate(pair, axis=0))
+                    two.append(jnp.concatenate(pair, axis=0).astype(bf16))
                 at = (part * 2 + h // 4) * 128 + xl * 64 + zl * 32 + (h % 4) * 8
-                kept_ref[at : at + 16, :] = jnp.where(core == 0, two[0], two[1]).astype(bf16)
-                sent_ref[at : at + 16, :] = jnp.where(core == 0, two[1], two[0]).astype(bf16)
+                kept_ref[at : at + 16, :] = jnp.where(core == 0, two[0], two[1])
+                sent_ref[at : at + 16, :] = jnp.where(core == 0, two[1], two[0])
 
 
 def main_kernel(
@@ -126,10 +126,8 @@
     fields = []
     for i, ref in enumerate((x_ref, g_ref)):
         for q, piece in enumerate((p0, p1, p2, p3)):
-            for a in range(3):
-                for b in range(6):
-                    at = ((q * 3 + a) * 6 + b) * 4
-                    rows_ref[i, at : at + 4, :] = piece[i, a, b].astype(f32)
+            at = q * (WIN // 2)
+            rows_ref[i, at : at + WIN // 2, :] = piece[i].astype(f32).reshape(WIN // 2, FEAT)
         field = nn(order, rows_ref[i].astype(bf16))
         fields.append(field)
         ref[...] = field.astype(bf16)

time: 64.7 us -> 64.6 us (level)
  no operation moved by 1% of the time
where the time goes in v6:
time: 64.6 us; the launch traced here: 64.4 us
  starting transfers between devices  33.5 us (52%)
  waiting for transfers between devices  17 us (26%)
  Pallas kernels  9.43 us (15%)
  other arithmetic  2.03 us (3%)
  local copies, waits for them, and re-layouts  1.6 us (2%)
  between operations  0.78 us (1%)
    ppermute x6, starting transfers between devices, shift(): return lax.ppermute(piece, ALL, pairs)  13.2 us
    all_to_all x1, waiting for transfers between devices, body(): total = lax.all_to_all(total, ('xh', 'y', 'xl', 'zl'), 0, 0, tiled=True)  12.8 us
    ppermute x3, starting transfers between devices, body(): chunks[d] = lax.ppermute(chunks[d], 'zh', pairs)  10.5 us
    pallas_call x5, Pallas kernels, call(): pl.pallas_call(kernel, out_shape=[jax.ShapeDtypeStruct(s, d) for s, d in...  9.43 us
    all_to_all x1, starting transfers between devices, body(): total = lax.all_to_all(total, ('xh', 'y', 'xl', 'zl'), 0, 0, tiled=True)  9.11 us
    ppermute x6, waiting for transfers between devices, shift(): return lax.ppermute(piece, ALL, pairs)  2.95 us
    unnamed x2, local copies, waits for them, and re-layouts  1.59 us
  transfers between devices with their start and end apart: 11, of which 5 were waited for; matrix products, arithmetic and copies ran while one was open for 0% of the time, Pallas kernels for 4%

profile of v6, /device:TPU:2, one launch (start us, length us, event | category | flops | bytes accessed | tf_op | source)
XLA Modules:
  0.0 64.4 jit_solution(3501764150410158684)
XLA Ops:
  0.6 1.2 %shard_map.58 = (bf16[2,3,6,4,512]{4,3,2,1,0:T(4,128)(2,1)S(1)}, bf16[2,3,6,4,512]{4,3,2,1,0:T(4,128)(2,1)S(1)}, bf16[2,3,6,4,512]{4,3,2,1,0:T(4,128)(2,1)S(1)}, bf16[2,3,6,4,512]{4,3,2,1,0:T(4,128)(2,1)S(1)}) custom-call(bf16[6,12,4,512]{3,2,1,0:T(4,128)(2,1)} %bitcast.14, bf16[6,12,4,512]{3,2,1,0:T(4,128)(2,1)} %bitcast.15), custom_call_target="tpu_custom_call" | custom-call | tf_op jit(solution)/shard_map/pallas_call | solution.py:34
  1.9 1.7 %collective-permute-start = (bf16[2,3,6,4,512]{4,3,2,1,0:T(4,128)(2,1)S(1)}, bf16[2,3,6,4,512]{4,3,2,1,0:T(4,128)(2,1)S(1)}, u32[]{:S(2)}, u32[]{:S(2)}) collective-permute-start(bf16[2,3,6,4,512]{4,3,2,1,0:T(4,128)(2,1)S(1)} %get-tuple-element.35), channel_id=1, source_target_pairs={{32,0},{225,1},{226,2},{35,3},{36,4},{229,5},{230,6},{39,7},{40,8}... | collective-permute-start | bytes 442376 | tf_op jit(solution)/shard_map/ppermute | solution.py:238
  3.5 0.7 %collective-permute-start.1 = (bf16[2,3,6,4,512]{4,3,2,1,0:T(4,128)(2,1)S(1)}, bf16[2,3,6,4,512]{4,3,2,1,0:T(4,128)(2,1)S(1)}, u32[]{:S(2)}, u32[]{:S(2)}) collective-permute-start(bf16[2,3,6,4,512]{4,3,2,1,0:T(4,128)(2,1)S(1)} %get-tuple-element.36), channel_id=1, source_target_pairs={{33,0},{226,1},{227,2},{36,3},{37,4},{230,5},{231,6},{40,7},{41,8}... | collective-permute-start | bytes 442376 | tf_op jit(solution)/shard_map/ppermute | solution.py:238
  4.2 4.2 %collective-permute-start.2 = (bf16[2,3,6,4,512]{4,3,2,1,0:T(4,128)(2,1)S(1)}, bf16[2,3,6,4,512]{4,3,2,1,0:T(4,128)(2,1)S(1)}, u32[]{:S(2)}, u32[]{:S(2)}) collective-permute-start(bf16[2,3,6,4,512]{4,3,2,1,0:T(4,128)(2,1)S(1)} %get-tuple-element.37), channel_id=1, source_target_pairs={{1,0},{2,1},{3,2},{4,3},{5,4},{6,5},{7,6},{8,7},{9,8},{10,9},{11,1... | collective-permute-start | bytes 442376 | tf_op jit(solution)/shard_map/ppermute | solution.py:238
  8.4 0.0 copy-start
  8.4 1.6 %copy-done = bf16[2048,512]{1,0:T(8,128)(2,1)S(1)} copy-done((bf16[2048,512]{1,0:T(8,128)(2,1)S(1)}, bf16[2048,512]{1,0:T(8,128)(2,1)}, u32[]{:S(2)}) %copy-start) | copy-done | bytes 2097176
  10.0 0.3 shard_map.59
  10.3 0.9 %collective-permute-done.p2 = bf16[2,3,6,4,512]{4,3,2,1,0:T(4,128)(2,1)S(1)} collective-permute-done((bf16[2,3,6,4,512]{4,3,2,1,0:T(4,128)(2,1)S(1)}, bf16[2,3,6,4,512]{4,3,2,1,0:T(4,128)(2,1)S(1)}, u32[]{:S(2)}, u32[]{:S(2)}) %collective-permute-start) | collective-permute-done | bytes 147488 | tf_op jit(solution)/shard_map/ppermute | solution.py:238
  11.3 2.0 %collective-permute-done.1.p3 = bf16[2,3,6,4,512]{4,3,2,1,0:T(4,128)(2,1)S(1)} collective-permute-done((bf16[2,3,6,4,512]{4,3,2,1,0:T(4,128)(2,1)S(1)}, bf16[2,3,6,4,512]{4,3,2,1,0:T(4,128)(2,1)S(1)}, u32[]{:S(2)}, u32[]{:S(2)}) %collective-permute-start.1) | collective-permute-done | bytes 147488 | tf_op jit(solution)/shard_map/ppermute | solution.py:238
  13.3 0.0 collective-permute-done.2.p1
  13.3 5.4 %shard_map.60 = (bf16[288,512]{1,0:T(8,128)(2,1)S(1)}, bf16[288,512]{1,0:T(8,128)(2,1)S(1)}, bf16[2,512,144]{2,1,0:T(8,128)(2,1)S(1)}, bf16[2,512,144]{2,1,0:T(8...) custom-call(bf16[2,3,6,4,512]{4,3,2,1,0:T(4,128)(2,1)S(1)} %collecti, ...), custom_call_target="tpu_custom_call" | custom-call | tf_op jit(solution)/shard_map/pallas_call | solution.py:34
  18.7 0.7 %collective-permute-start.3 = (bf16[1024,512]{1,0:T(8,128)(2,1)S(1)}, bf16[1024,512]{1,0:T(8,128)(2,1)S(1)}, u32[]{:S(2)}, u32[]{:S(2)}) collective-permute-start(bf16[1024,512]{1,0:T(8,128)(2,1)S(1)} %get-tuple-element.43), channel_id=1, source_target_pairs={{0,1},{1,0},{2,3},{3,2},{4,5},{5,4},{6,7},{7,6},{8,9},{9,8},{10,11... | collective-permute-start | bytes 3145736 | tf_op jit(solution)/shard_map/ppermute | solution.py:270
  19.4 1.6 %shard_map.61 = (bf16[2,3,6,4,512]{4,3,2,1,0:T(4,128)(2,1)S(1)}, bf16[2,3,6,4,512]{4,3,2,1,0:T(4,128)(2,1)S(1)}, bf16[2,3,6,4,512]{4,3,2,1,0:T(4,128)(2,1)S(1)}, bf16[2,3,6,4,512]{4,3,2,1,0:T(4,128)(2,1)S(1)}) custom-call(bf16[288,512]{1,0:T(8,128)(2,1)S(1)} %get-tuple-element.44.x_ref, bf16[288,512]{1,0:T(8,128)(2,1)S(1)} %get-tuple-element.45.g_ref, ...), custom_call_target="tpu_custom_call" | custom-call | tf_op jit(solution)/shard_map/pallas_call | solution.py:34
  21.0 0.7 %collective-permute-done.3 = bf16[1024,512]{1,0:T(8,128)(2,1)S(1)} collective-permute-done((bf16[1024,512]{1,0:T(8,128)(2,1)S(1)}, bf16[1024,512]{1,0:T(8,128)(2,1)S(1)}, u32[]{:S(2)}, u32[]{:S(2)}) %collective-permute-start.3) | collective-permute-done | bytes 1048608 | tf_op jit(solution)/shard_map/ppermute | solution.py:270
  21.7 1.3 %add_convert_fusion = bf16[1024,512]{1,0:T(8,128)(2,1)} fusion(bf16[1024,512]{1,0:T(8,128)(2,1)S(1)} %collective-permute-done.3, bf16[1024,512]{1,0:T(8,128)(2,1)S(1)} %get-tuple-element.42), kind=kLoop, calls=%fused_computation.1 | loop fusion | flops 2097152 | bytes 3145728 | tf_op jit(solution)/shard_map/convert_element_type | solution.py:279
  23.0 9.1 %all-to-all-start = ((bf16[32,32,512]{2,1,0:T(8,128)(2,1)}), bf16[32,32,512]{2,1,0:T(8,128)(2,1)S(1)}, u32[]{:S(2)}, u32[]{:S(2)}) async-start(bf16[32,32,512]{2,1,0:T(8,128)(2,1)} %bitcast.2), calls=%async_computation | async-start | bytes 2097152 | tf_op jit(solution)/shard_map/all_to_all | solution.py:280
  32.2 0.1 collective-permute-start.7
  32.2 4.3 %collective-permute-start.8 = (bf16[2,3,6,4,512]{4,3,2,1,0:T(4,128)(2,1)S(1)}, bf16[2,3,6,4,512]{4,3,2,1,0:T(4,128)(2,1)S(1)}, u32[]{:S(2)}, u32[]{:S(2)}) collective-permute-start(bf16[2,3,6,4,512]{4,3,2,1,0:T(4,128)(2,1)S(1)} %get-tuple-element.57), channel_id=1, source_target_pairs={{0,32},{1,225},{2,226},{3,35},{4,36},{5,229},{6,230},{7,39},{8,40}... | collective-permute-start | bytes 442376 | tf_op jit(solution)/shard_map/ppermute | solution.py:238
  36.6 2.2 %collective-permute-start.9 = (bf16[2,3,6,4,512]{4,3,2,1,0:T(4,128)(2,1)S(1)}, bf16[2,3,6,4,512]{4,3,2,1,0:T(4,128)(2,1)S(1)}, u32[]{:S(2)}, u32[]{:S(2)}) collective-permute-start(bf16[2,3,6,4,512]{4,3,2,1,0:T(4,128)(2,1)S(1)} %get-tuple-element.58), channel_id=1, source_target_pairs={{0,33},{1,226},{2,227},{3,36},{4,37},{5,230},{6,231},{7,40},{8,41}... | collective-permute-start | bytes 442376 | tf_op jit(solution)/shard_map/ppermute | solution.py:238
  38.8 12.8 %all-to-all-done = bf16[32,32,512]{2,1,0:T(8,128)(2,1)S(1)} async-done(((bf16[32,32,512]{2,1,0:T(8,128)(2,1)}), bf16[32,32,512]{2,1,0:T(8,128)(2,1)S(1)}, u32[]{:S(2)}, u32[]{:S(2)}) %all-to-all-start) | async-done | bytes 1048608 | tf_op jit(solution)/shard_map/all_to_all | solution.py:280
  51.6 0.2 convert_reduce_fusion
  51.7 2.1 %collective-permute-start.4 = (f32[8,512]{1,0:T(8,128)S(1)}, f32[8,512]{1,0:T(8,128)S(1)}, u32[]{:S(2)}, u32[]{:S(2)}) collective-permute-start(f32[8,512]{1,0:T(8,128)S(1)} %get-tuple-element.69), channel_id=1, source_target_pairs={{0,8},{8,16},{16,24},{24,0},{1,9},{9,17},{17,25},{25,1},{2,10},{10... | collective-permute-start | bytes 49160 | tf_op jit(solution)/shard_map/ppermute | solution.py:289
  53.9 5.2 %collective-permute-start.5 = (f32[8,512]{1,0:T(8,128)S(1)}, f32[8,512]{1,0:T(8,128)S(1)}, u32[]{:S(2)}, u32[]{:S(2)}) collective-permute-start(f32[8,512]{1,0:T(8,128)S(1)} %get-tuple-element.68), channel_id=1, source_target_pairs={{0,16},{8,24},{16,0},{24,8},{1,17},{9,25},{17,1},{25,9},{2,18},{10... | collective-permute-start | bytes 49160 | tf_op jit(solution)/shard_map/ppermute | solution.py:289
  59.1 0.0 collective-permute-done.7.p1
  59.1 3.1 %collective-permute-start.6 = (f32[8,512]{1,0:T(8,128)S(1)}, f32[8,512]{1,0:T(8,128)S(1)}, u32[]{:S(2)}, u32[]{:S(2)}) collective-permute-start(f32[8,512]{1,0:T(8,128)S(1)} %get-tuple-element.67), channel_id=1, source_target_pairs={{0,24},{8,0},{16,8},{24,16},{1,25},{9,1},{17,9},{25,17},{2,26},{10... | collective-permute-start | bytes 49160 | tf_op jit(solution)/shard_map/ppermute | solution.py:289
  62.2 0.0 collective-permute-done.8.p2
  62.2 0.0 collective-permute-done.9.p3
  62.2 0.9 %shard_map.62 = (bf16[6,12,4,512]{3,2,1,0:T(4,128)(2,1)}, bf16[6,12,4,512]{3,2,1,0:T(4,128)(2,1)}) custom-call(bf16[2,3,6,4,512]{4,3,2,1,0:T(4,128)(2,1)S(1)} %get-tuple-element.55.p0, bf16[2,3,6,4,512]{4,3,2,1,0:T(4,128)(2,1)S(1)} %collective-permute-done.7.p1, bf16[2,3,6,4,512]{4,3,2,1,0:T(4,128)(2,1)S(1)} %collective-permute-done.8.p2, ...), custom_call_target="tpu_custom_call" | custom-call | tf_op jit(solution)/shard_map/pallas_call | solution.py:34
  63.1 0.0 collective-permute-done.4
  63.1 0.0 collective-permute-done.5
  63.1 0.6 collective-permute-done.6
  63.8 0.6 add_add_fusion
  (1 shorter events, 0.0 us)
Async XLA Ops:
  1.9 9.4 %collective-permute-start = (bf16[2,3,6,4,512]{4,3,2,1,0:T(4,128)(2,1)S(1)}, bf16[2,3,6,4,512]{4,3,2,1,0:T(4,128)(2,1)S(1)}, u32[]{:S(2)}, u32[]{:S(2)}) collective-permute-start(bf16[2,3,6,4,512]{4,3,2,1,0:T(4,128)(2,1)S(1)} %get-tuple-element.35), channel_id=1, source_target_pairs={{32,0},{225,1},{226,2},{35,3},{36,4},{229,5},{230,6},{39,7},{40,8}... | collective-permute-start | bytes 442376 | tf_op jit(solution)/shard_map/ppermute | solution.py:238
  3.5 9.8 %collective-permute-start.1 = (bf16[2,3,6,4,512]{4,3,2,1,0:T(4,128)(2,1)S(1)}, bf16[2,3,6,4,512]{4,3,2,1,0:T(4,128)(2,1)S(1)}, u32[]{:S(2)}, u32[]{:S(2)}) collective-permute-start(bf16[2,3,6,4,512]{4,3,2,1,0:T(4,128)(2,1)S(1)} %get-tuple-element.36), channel_id=1, source_target_pairs={{33,0},{226,1},{227,2},{36,3},{37,4},{230,5},{231,6},{40,7},{41,8}... | collective-permute-start | bytes 442376 | tf_op jit(solution)/shard_map/ppermute | solution.py:238
  4.2 9.1 %collective-permute-start.2 = (bf16[2,3,6,4,512]{4,3,2,1,0:T(4,128)(2,1)S(1)}, bf16[2,3,6,4,512]{4,3,2,1,0:T(4,128)(2,1)S(1)}, u32[]{:S(2)}, u32[]{:S(2)}) collective-permute-start(bf16[2,3,6,4,512]{4,3,2,1,0:T(4,128)(2,1)S(1)} %get-tuple-element.37), channel_id=1, source_target_pairs={{1,0},{2,1},{3,2},{4,3},{5,4},{6,5},{7,6},{8,7},{9,8},{10,9},{11,1... | collective-permute-start | bytes 442376 | tf_op jit(solution)/shard_map/ppermute | solution.py:238
  8.4 1.6 %copy-start = (bf16[2048,512]{1,0:T(8,128)(2,1)S(1)}, bf16[2048,512]{1,0:T(8,128)(2,1)}, u32[]{:S(2)}) copy-start(bf16[2048,512]{1,0:T(8,128)(2,1)} %w_ref.1) | copy-start | bytes 6291460
  18.7 3.0 %collective-permute-start.3 = (bf16[1024,512]{1,0:T(8,128)(2,1)S(1)}, bf16[1024,512]{1,0:T(8,128)(2,1)S(1)}, u32[]{:S(2)}, u32[]{:S(2)}) collective-permute-start(bf16[1024,512]{1,0:T(8,128)(2,1)S(1)} %get-tuple-element.43), channel_id=1, source_target_pairs={{0,1},{1,0},{2,3},{3,2},{4,5},{5,4},{6,7},{7,6},{8,9},{9,8},{10,11... | collective-permute-start | bytes 3145736 | tf_op jit(solution)/shard_map/ppermute | solution.py:270
  23.0 28.6 %all-to-all-start = ((bf16[32,32,512]{2,1,0:T(8,128)(2,1)}), bf16[32,32,512]{2,1,0:T(8,128)(2,1)S(1)}, u32[]{:S(2)}, u32[]{:S(2)}) async-start(bf16[32,32,512]{2,1,0:T(8,128)(2,1)} %bitcast.2), calls=%async_computation | async-start | bytes 2097152 | tf_op jit(solution)/shard_map/all_to_all | solution.py:280
  32.2 27.0 %collective-permute-start.7 = (bf16[2,3,6,4,512]{4,3,2,1,0:T(4,128)(2,1)S(1)}, bf16[2,3,6,4,512]{4,3,2,1,0:T(4,128)(2,1)S(1)}, u32[]{:S(2)}, u32[]{:S(2)}) collective-permute-start(bf16[2,3,6,4,512]{4,3,2,1,0:T(4,128)(2,1)S(1)} %get-tuple-element.56), channel_id=1, source_target_pairs={{0,1},{1,2},{2,3},{3,4},{4,5},{5,6},{6,7},{7,8},{8,9},{9,10},{10,1... | collective-permute-start | bytes 442376 | tf_op jit(solution)/shard_map/ppermute | solution.py:238
  32.2 30.0 %collective-permute-start.8 = (bf16[2,3,6,4,512]{4,3,2,1,0:T(4,128)(2,1)S(1)}, bf16[2,3,6,4,512]{4,3,2,1,0:T(4,128)(2,1)S(1)}, u32[]{:S(2)}, u32[]{:S(2)}) collective-permute-start(bf16[2,3,6,4,512]{4,3,2,1,0:T(4,128)(2,1)S(1)} %get-tuple-element.57), channel_id=1, source_target_pairs={{0,32},{1,225},{2,226},{3,35},{4,36},{5,229},{6,230},{7,39},{8,40}... | collective-permute-start | bytes 442376 | tf_op jit(solution)/shard_map/ppermute | solution.py:238
  36.6 25.7 %collective-permute-start.9 = (bf16[2,3,6,4,512]{4,3,2,1,0:T(4,128)(2,1)S(1)}, bf16[2,3,6,4,512]{4,3,2,1,0:T(4,128)(2,1)S(1)}, u32[]{:S(2)}, u32[]{:S(2)}) collective-permute-start(bf16[2,3,6,4,512]{4,3,2,1,0:T(4,128)(2,1)S(1)} %get-tuple-element.58), channel_id=1, source_target_pairs={{0,33},{1,226},{2,227},{3,36},{4,37},{5,230},{6,231},{7,40},{8,41}... | collective-permute-start | bytes 442376 | tf_op jit(solution)/shard_map/ppermute | solution.py:238
  51.7 11.4 %collective-permute-start.4 = (f32[8,512]{1,0:T(8,128)S(1)}, f32[8,512]{1,0:T(8,128)S(1)}, u32[]{:S(2)}, u32[]{:S(2)}) collective-permute-start(f32[8,512]{1,0:T(8,128)S(1)} %get-tuple-element.69), channel_id=1, source_target_pairs={{0,8},{8,16},{16,24},{24,0},{1,9},{9,17},{17,25},{25,1},{2,10},{10... | collective-permute-start | bytes 49160 | tf_op jit(solution)/shard_map/ppermute | solution.py:289
  53.9 9.3 %collective-permute-start.5 = (f32[8,512]{1,0:T(8,128)S(1)}, f32[8,512]{1,0:T(8,128)S(1)}, u32[]{:S(2)}, u32[]{:S(2)}) collective-permute-start(f32[8,512]{1,0:T(8,128)S(1)} %get-tuple-element.68), channel_id=1, source_target_pairs={{0,16},{8,24},{16,0},{24,8},{1,17},{9,25},{17,1},{25,9},{2,18},{10... | collective-permute-start | bytes 49160 | tf_op jit(solution)/shard_map/ppermute | solution.py:289
  59.1 4.6 %collective-permute-start.6 = (f32[8,512]{1,0:T(8,128)S(1)}, f32[8,512]{1,0:T(8,128)S(1)}, u32[]{:S(2)}, u32[]{:S(2)}) collective-permute-start(f32[8,512]{1,0:T(8,128)S(1)} %get-tuple-element.67), channel_id=1, source_target_pairs={{0,24},{8,0},{16,8},{24,16},{1,25},{9,1},{17,9},{25,17},{2,26},{10... | collective-permute-start | bytes 49160 | tf_op jit(solution)/shard_map/ppermute | solution.py:289

commit v7 on v5

--- a/solution.py
+++ b/solution.py
@@ -108,7 +108,8 @@
                     at = h * HEAD + zl * 32 + xl * 16 + c * 8
                     pair = [block[at : at + 8], block[at + HEAD : at + HEAD + 8]]
                     two.append(jnp.concatenate(pair, axis=0))
-                at = (part * 2 + h // 4) * 128 + xl * 64 + zl * 32 + (h % 4) * 8
+                y = (part % 2) * 2 + h // 4
+                at = zl * 512 + xl * 256 + y * 64 + (part // 2) * 32 + (h % 4) * 8
                 kept_ref[at : at + 16, :] = jnp.where(core == 0, two[0], two[1]).astype(bf16)
                 sent_ref[at : at + 16, :] = jnp.where(core == 0, two[1], two[0]).astype(bf16)
 
@@ -279,7 +280,7 @@
     )
     got, backs = lax.optimization_barrier((got, list(backs)))
     total = (kept.astype(f32) + got.astype(f32)).astype(bf16).reshape(32, 32, FEAT)
-    total = lax.all_to_all(total, ("xh", "y", "xl", "zl"), 0, 0, tiled=True)
+    total = lax.all_to_all(total, ("zl", "xl", "y", "xh"), 0, 0, tiled=True)
     for q in (2, 3, 1):
         backs[q] = shift(backs[q], *moves[q], True)
     total = jnp.sum(total.astype(f32), axis=0)

time: 64.7 us -> 63.4 us (0.980)
  waiting for transfers between devices: 17 us -> 15.3 us
    all_to_all x1, waiting for transfers between devices: 12.8 us -> 11 us  [body(): total = lax.all_to_all(total, ('zl', 'xl', 'y', 'xh'), 0, 0, tiled=True)]
where the time goes in v7:
time: 63.4 us; the launch traced here: 62.6 us
  starting transfers between devices  33.5 us (53%)
  waiting for transfers between devices  15.3 us (24%)
  Pallas kernels  9.47 us (15%)
  other arithmetic  2.03 us (3%)
  local copies, waits for them, and re-layouts  1.6 us (3%)
  between operations  0.77 us (1%)
    ppermute x6, starting transfers between devices, shift(): return lax.ppermute(piece, ALL, pairs)  13.2 us
    all_to_all x1, waiting for transfers between devices, body(): total = lax.all_to_all(total, ('zl', 'xl', 'y', 'xh'), 0, 0, tiled=True)  11 us
    ppermute x3, starting transfers between devices, body(): chunks[d] = lax.ppermute(chunks[d], 'zh', pairs)  10.5 us
    pallas_call x5, Pallas kernels, call(): pl.pallas_call(kernel, out_shape=[jax.ShapeDtypeStruct(s, d) for s, d in...  9.47 us
    all_to_all x1, starting transfers between devices, body(): total = lax.all_to_all(total, ('zl', 'xl', 'y', 'xh'), 0, 0, tiled=True)  9.1 us
    ppermute x6, waiting for transfers between devices, shift(): return lax.ppermute(piece, ALL, pairs)  2.95 us
    unnamed x2, local copies, waits for them, and re-layouts  1.59 us
  transfers between devices with their start and end apart: 11, of which 5 were waited for; matrix products, arithmetic and copies ran while one was open for 0% of the time, Pallas kernels for 4%

profile of v7, /device:TPU:2, one launch (start us, length us, event | category | flops | bytes accessed | tf_op | source)
XLA Modules:
  0.0 62.6 jit_solution(7262515354337911634)
XLA Ops:
  0.6 1.2 %shard_map.58 = (bf16[2,3,6,4,512]{4,3,2,1,0:T(4,128)(2,1)S(1)}, bf16[2,3,6,4,512]{4,3,2,1,0:T(4,128)(2,1)S(1)}, bf16[2,3,6,4,512]{4,3,2,1,0:T(4,128)(2,1)S(1)}, bf16[2,3,6,4,512]{4,3,2,1,0:T(4,128)(2,1)S(1)}) custom-call(bf16[6,12,4,512]{3,2,1,0:T(4,128)(2,1)} %bitcast.14, bf16[6,12,4,512]{3,2,1,0:T(4,128)(2,1)} %bitcast.15), custom_call_target="tpu_custom_call" | custom-call | tf_op jit(solution)/shard_map/pallas_call | solution.py:34
  1.9 1.7 %collective-permute-start = (bf16[2,3,6,4,512]{4,3,2,1,0:T(4,128)(2,1)S(1)}, bf16[2,3,6,4,512]{4,3,2,1,0:T(4,128)(2,1)S(1)}, u32[]{:S(2)}, u32[]{:S(2)}) collective-permute-start(bf16[2,3,6,4,512]{4,3,2,1,0:T(4,128)(2,1)S(1)} %get-tuple-element.35), channel_id=1, source_target_pairs={{32,0},{225,1},{226,2},{35,3},{36,4},{229,5},{230,6},{39,7},{40,8}... | collective-permute-start | bytes 442376 | tf_op jit(solution)/shard_map/ppermute | solution.py:241
  3.5 0.7 %collective-permute-start.1 = (bf16[2,3,6,4,512]{4,3,2,1,0:T(4,128)(2,1)S(1)}, bf16[2,3,6,4,512]{4,3,2,1,0:T(4,128)(2,1)S(1)}, u32[]{:S(2)}, u32[]{:S(2)}) collective-permute-start(bf16[2,3,6,4,512]{4,3,2,1,0:T(4,128)(2,1)S(1)} %get-tuple-element.36), channel_id=1, source_target_pairs={{33,0},{226,1},{227,2},{36,3},{37,4},{230,5},{231,6},{40,7},{41,8}... | collective-permute-start | bytes 442376 | tf_op jit(solution)/shard_map/ppermute | solution.py:241
  4.2 4.2 %collective-permute-start.2 = (bf16[2,3,6,4,512]{4,3,2,1,0:T(4,128)(2,1)S(1)}, bf16[2,3,6,4,512]{4,3,2,1,0:T(4,128)(2,1)S(1)}, u32[]{:S(2)}, u32[]{:S(2)}) collective-permute-start(bf16[2,3,6,4,512]{4,3,2,1,0:T(4,128)(2,1)S(1)} %get-tuple-element.37), channel_id=1, source_target_pairs={{1,0},{2,1},{3,2},{4,3},{5,4},{6,5},{7,6},{8,7},{9,8},{10,9},{11,1... | collective-permute-start | bytes 442376 | tf_op jit(solution)/shard_map/ppermute | solution.py:241
  8.4 0.0 copy-start
  8.4 1.6 %copy-done = bf16[2048,512]{1,0:T(8,128)(2,1)S(1)} copy-done((bf16[2048,512]{1,0:T(8,128)(2,1)S(1)}, bf16[2048,512]{1,0:T(8,128)(2,1)}, u32[]{:S(2)}) %copy-start) | copy-done | bytes 2097176
  10.0 0.3 shard_map.59
  10.3 0.9 %collective-permute-done.p2 = bf16[2,3,6,4,512]{4,3,2,1,0:T(4,128)(2,1)S(1)} collective-permute-done((bf16[2,3,6,4,512]{4,3,2,1,0:T(4,128)(2,1)S(1)}, bf16[2,3,6,4,512]{4,3,2,1,0:T(4,128)(2,1)S(1)}, u32[]{:S(2)}, u32[]{:S(2)}) %collective-permute-start) | collective-permute-done | bytes 147488 | tf_op jit(solution)/shard_map/ppermute | solution.py:241
  11.3 2.0 %collective-permute-done.1.p3 = bf16[2,3,6,4,512]{4,3,2,1,0:T(4,128)(2,1)S(1)} collective-permute-done((bf16[2,3,6,4,512]{4,3,2,1,0:T(4,128)(2,1)S(1)}, bf16[2,3,6,4,512]{4,3,2,1,0:T(4,128)(2,1)S(1)}, u32[]{:S(2)}, u32[]{:S(2)}) %collective-permute-start.1) | collective-permute-done | bytes 147488 | tf_op jit(solution)/shard_map/ppermute | solution.py:241
  13.3 0.0 collective-permute-done.2.p1
  13.3 5.5 %shard_map.60 = (bf16[288,512]{1,0:T(8,128)(2,1)S(1)}, bf16[288,512]{1,0:T(8,128)(2,1)S(1)}, bf16[2,512,144]{2,1,0:T(8,128)(2,1)S(1)}, bf16[2,512,144]{2,1,0:T(8...) custom-call(bf16[2,3,6,4,512]{4,3,2,1,0:T(4,128)(2,1)S(1)} %collecti, ...), custom_call_target="tpu_custom_call" | custom-call | tf_op jit(solution)/shard_map/pallas_call | solution.py:34
  18.8 0.7 %collective-permute-start.3 = (bf16[1024,512]{1,0:T(8,128)(2,1)S(1)}, bf16[1024,512]{1,0:T(8,128)(2,1)S(1)}, u32[]{:S(2)}, u32[]{:S(2)}) collective-permute-start(bf16[1024,512]{1,0:T(8,128)(2,1)S(1)} %get-tuple-element.43), channel_id=1, source_target_pairs={{0,1},{1,0},{2,3},{3,2},{4,5},{5,4},{6,7},{7,6},{8,9},{9,8},{10,11... | collective-permute-start | bytes 3145736 | tf_op jit(solution)/shard_map/ppermute | solution.py:273
  19.5 1.6 %shard_map.61 = (bf16[2,3,6,4,512]{4,3,2,1,0:T(4,128)(2,1)S(1)}, bf16[2,3,6,4,512]{4,3,2,1,0:T(4,128)(2,1)S(1)}, bf16[2,3,6,4,512]{4,3,2,1,0:T(4,128)(2,1)S(1)}, bf16[2,3,6,4,512]{4,3,2,1,0:T(4,128)(2,1)S(1)}) custom-call(bf16[288,512]{1,0:T(8,128)(2,1)S(1)} %get-tuple-element.44.x_ref, bf16[288,512]{1,0:T(8,128)(2,1)S(1)} %get-tuple-element.45.g_ref, ...), custom_call_target="tpu_custom_call" | custom-call | tf_op jit(solution)/shard_map/pallas_call | solution.py:34
  21.1 0.7 %collective-permute-done.3 = bf16[1024,512]{1,0:T(8,128)(2,1)S(1)} collective-permute-done((bf16[1024,512]{1,0:T(8,128)(2,1)S(1)}, bf16[1024,512]{1,0:T(8,128)(2,1)S(1)}, u32[]{:S(2)}, u32[]{:S(2)}) %collective-permute-start.3) | collective-permute-done | bytes 1048608 | tf_op jit(solution)/shard_map/ppermute | solution.py:273
  21.8 1.3 %add_convert_fusion = bf16[1024,512]{1,0:T(8,128)(2,1)} fusion(bf16[1024,512]{1,0:T(8,128)(2,1)S(1)} %collective-permute-done.3, bf16[1024,512]{1,0:T(8,128)(2,1)S(1)} %get-tuple-element.42), kind=kLoop, calls=%fused_computation.1 | loop fusion | flops 2097152 | bytes 3145728 | tf_op jit(solution)/shard_map/convert_element_type | solution.py:282
  23.0 9.1 %all-to-all-start = ((bf16[32,32,512]{2,1,0:T(8,128)(2,1)}), bf16[32,32,512]{2,1,0:T(8,128)(2,1)S(1)}, u32[]{:S(2)}, u32[]{:S(2)}) async-start(bf16[32,32,512]{2,1,0:T(8,128)(2,1)} %bitcast.2), calls=%async_computation | async-start | bytes 2097152 | tf_op jit(solution)/shard_map/all_to_all | solution.py:283
  32.2 0.1 collective-permute-start.7
  32.3 4.3 %collective-permute-start.8 = (bf16[2,3,6,4,512]{4,3,2,1,0:T(4,128)(2,1)S(1)}, bf16[2,3,6,4,512]{4,3,2,1,0:T(4,128)(2,1)S(1)}, u32[]{:S(2)}, u32[]{:S(2)}) collective-permute-start(bf16[2,3,6,4,512]{4,3,2,1,0:T(4,128)(2,1)S(1)} %get-tuple-element.57), channel_id=1, source_target_pairs={{0,32},{1,225},{2,226},{3,35},{4,36},{5,229},{6,230},{7,39},{8,40}... | collective-permute-start | bytes 442376 | tf_op jit(solution)/shard_map/ppermute | solution.py:241
  36.6 2.3 %collective-permute-start.9 = (bf16[2,3,6,4,512]{4,3,2,1,0:T(4,128)(2,1)S(1)}, bf16[2,3,6,4,512]{4,3,2,1,0:T(4,128)(2,1)S(1)}, u32[]{:S(2)}, u32[]{:S(2)}) collective-permute-start(bf16[2,3,6,4,512]{4,3,2,1,0:T(4,128)(2,1)S(1)} %get-tuple-element.58), channel_id=1, source_target_pairs={{0,33},{1,226},{2,227},{3,36},{4,37},{5,230},{6,231},{7,40},{8,41}... | collective-permute-start | bytes 442376 | tf_op jit(solution)/shard_map/ppermute | solution.py:241
  38.8 11.0 %all-to-all-done = bf16[32,32,512]{2,1,0:T(8,128)(2,1)S(1)} async-done(((bf16[32,32,512]{2,1,0:T(8,128)(2,1)}), bf16[32,32,512]{2,1,0:T(8,128)(2,1)S(1)}, u32[]{:S(2)}, u32[]{:S(2)}) %all-to-all-start) | async-done | bytes 1048608 | tf_op jit(solution)/shard_map/all_to_all | solution.py:283
  49.8 0.2 convert_reduce_fusion
  50.0 2.0 %collective-permute-start.4 = (f32[8,512]{1,0:T(8,128)S(1)}, f32[8,512]{1,0:T(8,128)S(1)}, u32[]{:S(2)}, u32[]{:S(2)}) collective-permute-start(f32[8,512]{1,0:T(8,128)S(1)} %get-tuple-element.69), channel_id=1, source_target_pairs={{0,8},{8,16},{16,24},{24,0},{1,9},{9,17},{17,25},{25,1},{2,10},{10... | collective-permute-start | bytes 49160 | tf_op jit(solution)/shard_map/ppermute | solution.py:292
  52.0 5.4 %collective-permute-start.5 = (f32[8,512]{1,0:T(8,128)S(1)}, f32[8,512]{1,0:T(8,128)S(1)}, u32[]{:S(2)}, u32[]{:S(2)}) collective-permute-start(f32[8,512]{1,0:T(8,128)S(1)} %get-tuple-element.68), channel_id=1, source_target_pairs={{0,16},{8,24},{16,0},{24,8},{1,17},{9,25},{17,1},{25,9},{2,18},{10... | collective-permute-start | bytes 49160 | tf_op jit(solution)/shard_map/ppermute | solution.py:292
  57.4 0.0 collective-permute-done.7.p1
  57.4 3.1 %collective-permute-start.6 = (f32[8,512]{1,0:T(8,128)S(1)}, f32[8,512]{1,0:T(8,128)S(1)}, u32[]{:S(2)}, u32[]{:S(2)}) collective-permute-start(f32[8,512]{1,0:T(8,128)S(1)} %get-tuple-element.67), channel_id=1, source_target_pairs={{0,24},{8,0},{16,8},{24,16},{1,25},{9,1},{17,9},{25,17},{2,26},{10... | collective-permute-start | bytes 49160 | tf_op jit(solution)/shard_map/ppermute | solution.py:292
  60.5 0.0 collective-permute-done.8.p2
  60.5 0.0 collective-permute-done.9.p3
  60.5 0.9 %shard_map.62 = (bf16[6,12,4,512]{3,2,1,0:T(4,128)(2,1)}, bf16[6,12,4,512]{3,2,1,0:T(4,128)(2,1)}) custom-call(bf16[2,3,6,4,512]{4,3,2,1,0:T(4,128)(2,1)S(1)} %get-tuple-element.55.p0, bf16[2,3,6,4,512]{4,3,2,1,0:T(4,128)(2,1)S(1)} %collective-permute-done.7.p1, bf16[2,3,6,4,512]{4,3,2,1,0:T(4,128)(2,1)S(1)} %collective-permute-done.8.p2, ...), custom_call_target="tpu_custom_call" | custom-call | tf_op jit(solution)/shard_map/pallas_call | solution.py:34
  61.4 0.0 collective-permute-done.4
  61.4 0.0 collective-permute-done.5
  61.4 0.6 collective-permute-done.6
  62.0 0.6 add_add_fusion
  (1 shorter events, 0.0 us)
Async XLA Ops:
  1.9 9.4 %collective-permute-start = (bf16[2,3,6,4,512]{4,3,2,1,0:T(4,128)(2,1)S(1)}, bf16[2,3,6,4,512]{4,3,2,1,0:T(4,128)(2,1)S(1)}, u32[]{:S(2)}, u32[]{:S(2)}) collective-permute-start(bf16[2,3,6,4,512]{4,3,2,1,0:T(4,128)(2,1)S(1)} %get-tuple-element.35), channel_id=1, source_target_pairs={{32,0},{225,1},{226,2},{35,3},{36,4},{229,5},{230,6},{39,7},{40,8}... | collective-permute-start | bytes 442376 | tf_op jit(solution)/shard_map/ppermute | solution.py:241
  3.5 9.8 %collective-permute-start.1 = (bf16[2,3,6,4,512]{4,3,2,1,0:T(4,128)(2,1)S(1)}, bf16[2,3,6,4,512]{4,3,2,1,0:T(4,128)(2,1)S(1)}, u32[]{:S(2)}, u32[]{:S(2)}) collective-permute-start(bf16[2,3,6,4,512]{4,3,2,1,0:T(4,128)(2,1)S(1)} %get-tuple-element.36), channel_id=1, source_target_pairs={{33,0},{226,1},{227,2},{36,3},{37,4},{230,5},{231,6},{40,7},{41,8}... | collective-permute-start | bytes 442376 | tf_op jit(solution)/shard_map/ppermute | solution.py:241
  4.2 9.1 %collective-permute-start.2 = (bf16[2,3,6,4,512]{4,3,2,1,0:T(4,128)(2,1)S(1)}, bf16[2,3,6,4,512]{4,3,2,1,0:T(4,128)(2,1)S(1)}, u32[]{:S(2)}, u32[]{:S(2)}) collective-permute-start(bf16[2,3,6,4,512]{4,3,2,1,0:T(4,128)(2,1)S(1)} %get-tuple-element.37), channel_id=1, source_target_pairs={{1,0},{2,1},{3,2},{4,3},{5,4},{6,5},{7,6},{8,7},{9,8},{10,9},{11,1... | collective-permute-start | bytes 442376 | tf_op jit(solution)/shard_map/ppermute | solution.py:241
  8.4 1.6 %copy-start = (bf16[2048,512]{1,0:T(8,128)(2,1)S(1)}, bf16[2048,512]{1,0:T(8,128)(2,1)}, u32[]{:S(2)}) copy-start(bf16[2048,512]{1,0:T(8,128)(2,1)} %w_ref.1) | copy-start | bytes 6291460
  18.8 3.0 %collective-permute-start.3 = (bf16[1024,512]{1,0:T(8,128)(2,1)S(1)}, bf16[1024,512]{1,0:T(8,128)(2,1)S(1)}, u32[]{:S(2)}, u32[]{:S(2)}) collective-permute-start(bf16[1024,512]{1,0:T(8,128)(2,1)S(1)} %get-tuple-element.43), channel_id=1, source_target_pairs={{0,1},{1,0},{2,3},{3,2},{4,5},{5,4},{6,7},{7,6},{8,9},{9,8},{10,11... | collective-permute-start | bytes 3145736 | tf_op jit(solution)/shard_map/ppermute | solution.py:273
  23.0 26.8 %all-to-all-start = ((bf16[32,32,512]{2,1,0:T(8,128)(2,1)}), bf16[32,32,512]{2,1,0:T(8,128)(2,1)S(1)}, u32[]{:S(2)}, u32[]{:S(2)}) async-start(bf16[32,32,512]{2,1,0:T(8,128)(2,1)} %bitcast.2), calls=%async_computation | async-start | bytes 2097152 | tf_op jit(solution)/shard_map/all_to_all | solution.py:283
  32.2 25.2 %collective-permute-start.7 = (bf16[2,3,6,4,512]{4,3,2,1,0:T(4,128)(2,1)S(1)}, bf16[2,3,6,4,512]{4,3,2,1,0:T(4,128)(2,1)S(1)}, u32[]{:S(2)}, u32[]{:S(2)}) collective-permute-start(bf16[2,3,6,4,512]{4,3,2,1,0:T(4,128)(2,1)S(1)} %get-tuple-element.56), channel_id=1, source_target_pairs={{0,1},{1,2},{2,3},{3,4},{4,5},{5,6},{6,7},{7,8},{8,9},{9,10},{10,1... | collective-permute-start | bytes 442376 | tf_op jit(solution)/shard_map/ppermute | solution.py:241
  32.3 28.2 %collective-permute-start.8 = (bf16[2,3,6,4,512]{4,3,2,1,0:T(4,128)(2,1)S(1)}, bf16[2,3,6,4,512]{4,3,2,1,0:T(4,128)(2,1)S(1)}, u32[]{:S(2)}, u32[]{:S(2)}) collective-permute-start(bf16[2,3,6,4,512]{4,3,2,1,0:T(4,128)(2,1)S(1)} %get-tuple-element.57), channel_id=1, source_target_pairs={{0,32},{1,225},{2,226},{3,35},{4,36},{5,229},{6,230},{7,39},{8,40}... | collective-permute-start | bytes 442376 | tf_op jit(solution)/shard_map/ppermute | solution.py:241
  36.6 23.9 %collective-permute-start.9 = (bf16[2,3,6,4,512]{4,3,2,1,0:T(4,128)(2,1)S(1)}, bf16[2,3,6,4,512]{4,3,2,1,0:T(4,128)(2,1)S(1)}, u32[]{:S(2)}, u32[]{:S(2)}) collective-permute-start(bf16[2,3,6,4,512]{4,3,2,1,0:T(4,128)(2,1)S(1)} %get-tuple-element.58), channel_id=1, source_target_pairs={{0,33},{1,226},{2,227},{3,36},{4,37},{5,230},{6,231},{7,40},{8,41}... | collective-permute-start | bytes 442376 | tf_op jit(solution)/shard_map/ppermute | solution.py:241
  50.0 11.4 %collective-permute-start.4 = (f32[8,512]{1,0:T(8,128)S(1)}, f32[8,512]{1,0:T(8,128)S(1)}, u32[]{:S(2)}, u32[]{:S(2)}) collective-permute-start(f32[8,512]{1,0:T(8,128)S(1)} %get-tuple-element.69), channel_id=1, source_target_pairs={{0,8},{8,16},{16,24},{24,0},{1,9},{9,17},{17,25},{25,1},{2,10},{10... | collective-permute-start | bytes 49160 | tf_op jit(solution)/shard_map/ppermute | solution.py:292
  52.0 9.4 %collective-permute-start.5 = (f32[8,512]{1,0:T(8,128)S(1)}, f32[8,512]{1,0:T(8,128)S(1)}, u32[]{:S(2)}, u32[]{:S(2)}) collective-permute-start(f32[8,512]{1,0:T(8,128)S(1)} %get-tuple-element.68), channel_id=1, source_target_pairs={{0,16},{8,24},{16,0},{24,8},{1,17},{9,25},{17,1},{25,9},{2,18},{10... | collective-permute-start | bytes 49160 | tf_op jit(solution)/shard_map/ppermute | solution.py:292
  57.4 4.6 %collective-permute-start.6 = (f32[8,512]{1,0:T(8,128)S(1)}, f32[8,512]{1,0:T(8,128)S(1)}, u32[]{:S(2)}, u32[]{:S(2)}) collective-permute-start(f32[8,512]{1,0:T(8,128)S(1)} %get-tuple-element.67), channel_id=1, source_target_pairs={{0,24},{8,0},{16,8},{24,16},{1,25},{9,1},{17,9},{25,17},{2,26},{10... | collective-permute-start | bytes 49160 | tf_op jit(solution)/shard_map/ppermute | solution.py:292

commit v8 on v7

--- a/solution.py
+++ b/solution.py
@@ -284,16 +284,21 @@
     for q in (2, 3, 1):
         backs[q] = shift(backs[q], *moves[q], True)
     total = jnp.sum(total.astype(f32), axis=0)
-    total = total.reshape(4, 8, FEAT)
     at = lax.axis_index("zh")
-    chunks = [lax.dynamic_index_in_dim(total, (at + d) % 4, 0, keepdims=False) for d in range(4)]
-    for d in (2, 1, 3):
-        pairs = [(i, (i + d) % 4) for i in range(4)]
-        chunks[d] = lax.ppermute(chunks[d], "zh", pairs)
+
+    def halves(rows, bit):
+        rows = rows.reshape(2, 8 * bit, FEAT)
+        mine = (at // bit) % 2
+        stays = lax.dynamic_index_in_dim(rows, mine, 0, keepdims=False)
+        gone = lax.dynamic_index_in_dim(rows, 1 - mine, 0, keepdims=False)
+        return stays, lax.ppermute(gone, "zh", [(i, i ^ bit) for i in range(4)])
+
+    stays, came = halves(total, 2)
     field = ((6, 12, 4, FEAT), bf16)
     results = call(unpack_kernel, [field] * 2, sems, 4, backs, [ANY] * 4, HBM)
-    chunks, results = lax.optimization_barrier((chunks, results))
-    weight_grads = chunks[0] + chunks[2] + (chunks[1] + chunks[3])
+    came, results = lax.optimization_barrier((came, results))
+    stays, came = halves(stays + came, 1)
+    weight_grads = stays + came
     mixed, token_grads = (r.transpose(2, 0, 1, 3) for r in results)
     return mixed, token_grads, weight_grads
 

time: 63.4 us -> 64.5 us (1.017)
  waiting for transfers between devices: 15.3 us -> 19.2 us
  starting transfers between devices: 33.5 us -> 30.8 us
    ppermute x3 -> x2, waiting for transfers between devices: 0.62 us -> 4.51 us  [halves(): return (stays, lax.ppermute(gone, 'zh', [(i, i ^ bit) for i in range(4)]))]
    ppermute x3 -> x2, starting transfers between devices: 10.5 us -> 7.84 us  [halves(): return (stays, lax.ppermute(gone, 'zh', [(i, i ^ bit) for i in range(4)]))]
  transfers between devices with their start and end apart: 11 -> 10, of which waited for: 5 -> 6; matrix products, arithmetic and copies ran while one was open for 0% -> 0% of each run, Pallas kernels for 4% -> 4%
where the time goes in v8:
time: 64.5 us; the launch traced here: 63.9 us
  starting transfers between devices  30.8 us (48%)
  waiting for transfers between devices  19.2 us (30%)
  Pallas kernels  9.49 us (15%)
  other arithmetic  2.04 us (3%)
  local copies, waits for them, and re-layouts  1.6 us (2%)
  between operations  0.74 us (1%)
    ppermute x6, starting transfers between devices, shift(): return lax.ppermute(piece, ALL, pairs)  13.2 us
    all_to_all x1, waiting for transfers between devices, body(): total = lax.all_to_all(total, ('zl', 'xl', 'y', 'xh'), 0, 0, tiled=True)  11 us
    pallas_call x5, Pallas kernels, call(): pl.pallas_call(kernel, out_shape=[jax.ShapeDtypeStruct(s, d) for s, d in...  9.49 us
    all_to_all x1, starting transfers between devices, body(): total = lax.all_to_all(total, ('zl', 'xl', 'y', 'xh'), 0, 0, tiled=True)  9.1 us
    ppermute x2, starting transfers between devices, halves(): return (stays, lax.ppermute(gone, 'zh', [(i, i ^ bit) for i in range(4)]))  7.84 us
    ppermute x2, waiting for transfers between devices, halves(): return (stays, lax.ppermute(gone, 'zh', [(i, i ^ bit) for i in range(4)]))  4.51 us
    ppermute x6, waiting for transfers between devices, shift(): return lax.ppermute(piece, ALL, pairs)  2.95 us
    unnamed x2, local copies, waits for them, and re-layouts  1.59 us
  transfers between devices with their start and end apart: 10, of which 6 were waited for; matrix products, arithmetic and copies ran while one was open for 0% of the time, Pallas kernels for 4%

profile of v8, /device:TPU:2, one launch (start us, length us, event | category | flops | bytes accessed | tf_op | source)
XLA Modules:
  0.0 63.9 jit_solution(162708537468544750)
XLA Ops:
  0.6 1.2 %shard_map.58 = (bf16[2,3,6,4,512]{4,3,2,1,0:T(4,128)(2,1)S(1)}, bf16[2,3,6,4,512]{4,3,2,1,0:T(4,128)(2,1)S(1)}, bf16[2,3,6,4,512]{4,3,2,1,0:T(4,128)(2,1)S(1)}, bf16[2,3,6,4,512]{4,3,2,1,0:T(4,128)(2,1)S(1)}) custom-call(bf16[6,12,4,512]{3,2,1,0:T(4,128)(2,1)} %bitcast.18, bf16[6,12,4,512]{3,2,1,0:T(4,128)(2,1)} %bitcast.19), custom_call_target="tpu_custom_call" | custom-call | tf_op jit(solution)/shard_map/pallas_call | solution.py:34
  1.9 1.7 %collective-permute-start = (bf16[2,3,6,4,512]{4,3,2,1,0:T(4,128)(2,1)S(1)}, bf16[2,3,6,4,512]{4,3,2,1,0:T(4,128)(2,1)S(1)}, u32[]{:S(2)}, u32[]{:S(2)}) collective-permute-start(bf16[2,3,6,4,512]{4,3,2,1,0:T(4,128)(2,1)S(1)} %get-tuple-element.32), channel_id=1, source_target_pairs={{32,0},{225,1},{226,2},{35,3},{36,4},{229,5},{230,6},{39,7},{40,8}... | collective-permute-start | bytes 442376 | tf_op jit(solution)/shard_map/ppermute | solution.py:241
  3.5 0.7 %collective-permute-start.1 = (bf16[2,3,6,4,512]{4,3,2,1,0:T(4,128)(2,1)S(1)}, bf16[2,3,6,4,512]{4,3,2,1,0:T(4,128)(2,1)S(1)}, u32[]{:S(2)}, u32[]{:S(2)}) collective-permute-start(bf16[2,3,6,4,512]{4,3,2,1,0:T(4,128)(2,1)S(1)} %get-tuple-element.33), channel_id=1, source_target_pairs={{33,0},{226,1},{227,2},{36,3},{37,4},{230,5},{231,6},{40,7},{41,8}... | collective-permute-start | bytes 442376 | tf_op jit(solution)/shard_map/ppermute | solution.py:241
  4.2 4.2 %collective-permute-start.2 = (bf16[2,3,6,4,512]{4,3,2,1,0:T(4,128)(2,1)S(1)}, bf16[2,3,6,4,512]{4,3,2,1,0:T(4,128)(2,1)S(1)}, u32[]{:S(2)}, u32[]{:S(2)}) collective-permute-start(bf16[2,3,6,4,512]{4,3,2,1,0:T(4,128)(2,1)S(1)} %get-tuple-element.34), channel_id=1, source_target_pairs={{1,0},{2,1},{3,2},{4,3},{5,4},{6,5},{7,6},{8,7},{9,8},{10,9},{11,1... | collective-permute-start | bytes 442376 | tf_op jit(solution)/shard_map/ppermute | solution.py:241
  8.4 0.0 copy-start
  8.4 1.6 %copy-done = bf16[2048,512]{1,0:T(8,128)(2,1)S(1)} copy-done((bf16[2048,512]{1,0:T(8,128)(2,1)S(1)}, bf16[2048,512]{1,0:T(8,128)(2,1)}, u32[]{:S(2)}) %copy-start) | copy-done | bytes 2097176
  10.0 0.3 shard_map.59
  10.3 0.9 %collective-permute-done.p2 = bf16[2,3,6,4,512]{4,3,2,1,0:T(4,128)(2,1)S(1)} collective-permute-done((bf16[2,3,6,4,512]{4,3,2,1,0:T(4,128)(2,1)S(1)}, bf16[2,3,6,4,512]{4,3,2,1,0:T(4,128)(2,1)S(1)}, u32[]{:S(2)}, u32[]{:S(2)}) %collective-permute-start) | collective-permute-done | bytes 147488 | tf_op jit(solution)/shard_map/ppermute | solution.py:241
  11.3 2.0 %collective-permute-done.1.p3 = bf16[2,3,6,4,512]{4,3,2,1,0:T(4,128)(2,1)S(1)} collective-permute-done((bf16[2,3,6,4,512]{4,3,2,1,0:T(4,128)(2,1)S(1)}, bf16[2,3,6,4,512]{4,3,2,1,0:T(4,128)(2,1)S(1)}, u32[]{:S(2)}, u32[]{:S(2)}) %collective-permute-start.1) | collective-permute-done | bytes 147488 | tf_op jit(solution)/shard_map/ppermute | solution.py:241
  13.3 0.0 collective-permute-done.2.p1
  13.3 5.5 %shard_map.60 = (bf16[288,512]{1,0:T(8,128)(2,1)S(1)}, bf16[288,512]{1,0:T(8,128)(2,1)S(1)}, bf16[2,512,144]{2,1,0:T(8,128)(2,1)S(1)}, bf16[2,512,144]{2,1,0:T(8...) custom-call(bf16[2,3,6,4,512]{4,3,2,1,0:T(4,128)(2,1)S(1)} %collecti, ...), custom_call_target="tpu_custom_call" | custom-call | tf_op jit(solution)/shard_map/pallas_call | solution.py:34
  18.8 0.7 %collective-permute-start.3 = (bf16[1024,512]{1,0:T(8,128)(2,1)S(1)}, bf16[1024,512]{1,0:T(8,128)(2,1)S(1)}, u32[]{:S(2)}, u32[]{:S(2)}) collective-permute-start(bf16[1024,512]{1,0:T(8,128)(2,1)S(1)} %get-tuple-element.40), channel_id=1, source_target_pairs={{0,1},{1,0},{2,3},{3,2},{4,5},{5,4},{6,7},{7,6},{8,9},{9,8},{10,11... | collective-permute-start | bytes 3145736 | tf_op jit(solution)/shard_map/ppermute | solution.py:273
  19.5 1.6 %shard_map.61 = (bf16[2,3,6,4,512]{4,3,2,1,0:T(4,128)(2,1)S(1)}, bf16[2,3,6,4,512]{4,3,2,1,0:T(4,128)(2,1)S(1)}, bf16[2,3,6,4,512]{4,3,2,1,0:T(4,128)(2,1)S(1)}, bf16[2,3,6,4,512]{4,3,2,1,0:T(4,128)(2,1)S(1)}) custom-call(bf16[288,512]{1,0:T(8,128)(2,1)S(1)} %get-tuple-element.41.x_ref, bf16[288,512]{1,0:T(8,128)(2,1)S(1)} %get-tuple-element.42.g_ref, ...), custom_call_target="tpu_custom_call" | custom-call | tf_op jit(solution)/shard_map/pallas_call | solution.py:34
  21.1 0.7 %collective-permute-done.3 = bf16[1024,512]{1,0:T(8,128)(2,1)S(1)} collective-permute-done((bf16[1024,512]{1,0:T(8,128)(2,1)S(1)}, bf16[1024,512]{1,0:T(8,128)(2,1)S(1)}, u32[]{:S(2)}, u32[]{:S(2)}) %collective-permute-start.3) | collective-permute-done | bytes 1048608 | tf_op jit(solution)/shard_map/ppermute | solution.py:273
  21.8 1.3 %add_convert_fusion = bf16[1024,512]{1,0:T(8,128)(2,1)} fusion(bf16[1024,512]{1,0:T(8,128)(2,1)S(1)} %collective-permute-done.3, bf16[1024,512]{1,0:T(8,128)(2,1)S(1)} %get-tuple-element.39), kind=kLoop, calls=%fused_computation.1 | loop fusion | flops 2097152 | bytes 3145728 | tf_op jit(solution)/shard_map/convert_element_type | solution.py:282
  23.0 9.1 %all-to-all-start = ((bf16[32,32,512]{2,1,0:T(8,128)(2,1)}), bf16[32,32,512]{2,1,0:T(8,128)(2,1)S(1)}, u32[]{:S(2)}, u32[]{:S(2)}) async-start(bf16[32,32,512]{2,1,0:T(8,128)(2,1)} %bitcast.2), calls=%async_computation | async-start | bytes 2097152 | tf_op jit(solution)/shard_map/all_to_all | solution.py:283
  32.2 0.1 collective-permute-start.5
  32.3 4.3 %collective-permute-start.6 = (bf16[2,3,6,4,512]{4,3,2,1,0:T(4,128)(2,1)S(1)}, bf16[2,3,6,4,512]{4,3,2,1,0:T(4,128)(2,1)S(1)}, u32[]{:S(2)}, u32[]{:S(2)}) collective-permute-start(bf16[2,3,6,4,512]{4,3,2,1,0:T(4,128)(2,1)S(1)} %get-tuple-element.54), channel_id=1, source_target_pairs={{0,32},{1,225},{2,226},{3,35},{4,36},{5,229},{6,230},{7,39},{8,40}... | collective-permute-start | bytes 442376 | tf_op jit(solution)/shard_map/ppermute | solution.py:241
  36.5 2.3 %collective-permute-start.7 = (bf16[2,3,6,4,512]{4,3,2,1,0:T(4,128)(2,1)S(1)}, bf16[2,3,6,4,512]{4,3,2,1,0:T(4,128)(2,1)S(1)}, u32[]{:S(2)}, u32[]{:S(2)}) collective-permute-start(bf16[2,3,6,4,512]{4,3,2,1,0:T(4,128)(2,1)S(1)} %get-tuple-element.55), channel_id=1, source_target_pairs={{0,33},{1,226},{2,227},{3,36},{4,37},{5,230},{6,231},{7,40},{8,41}... | collective-permute-start | bytes 442376 | tf_op jit(solution)/shard_map/ppermute | solution.py:241
  38.8 11.0 %all-to-all-done = bf16[32,32,512]{2,1,0:T(8,128)(2,1)S(1)} async-done(((bf16[32,32,512]{2,1,0:T(8,128)(2,1)}), bf16[32,32,512]{2,1,0:T(8,128)(2,1)S(1)}, u32[]{:S(2)}, u32[]{:S(2)}) %all-to-all-start) | async-done | bytes 1048608 | tf_op jit(solution)/shard_map/all_to_all | solution.py:283
  49.8 0.2 convert_reduce_fusion
  50.0 6.4 %collective-permute-start.4 = (f32[16,512]{1,0:T(8,128)S(1)}, f32[16,512]{1,0:T(8,128)S(1)}, u32[]{:S(2)}, u32[]{:S(2)}) collective-permute-start(f32[16,512]{1,0:T(8,128)S(1)} %dynamic-slice_bitcast_fusion), channel_id=1, source_target_pairs={{0,16},{8,24},{16,0},{24,8},{1,17},{9,25},{17,1},{25,9},{2,18},{10... | collective-permute-start | bytes 98312 | tf_op jit(solution)/shard_map/ppermute | solution.py:294
  56.4 0.0 collective-permute-done.5.p1
  56.4 0.0 collective-permute-done.6.p2
  56.4 0.0 collective-permute-done.7.p3
  56.4 0.9 %shard_map.62 = (bf16[6,12,4,512]{3,2,1,0:T(4,128)(2,1)}, bf16[6,12,4,512]{3,2,1,0:T(4,128)(2,1)}) custom-call(bf16[2,3,6,4,512]{4,3,2,1,0:T(4,128)(2,1)S(1)} %get-tuple-element.52.p0, bf16[2,3,6,4,512]{4,3,2,1,0:T(4,128)(2,1)S(1)} %collective-permute-done.5.p1, bf16[2,3,6,4,512]{4,3,2,1,0:T(4,128)(2,1)S(1)} %collective-permute-done.6.p2, ...), custom_call_target="tpu_custom_call" | custom-call | tf_op jit(solution)/shard_map/pallas_call | solution.py:34
  57.3 1.2 %collective-permute-done.4 = f32[16,512]{1,0:T(8,128)S(1)} collective-permute-done((f32[16,512]{1,0:T(8,128)S(1)}, f32[16,512]{1,0:T(8,128)S(1)}, u32[]{:S(2)}, u32[]{:S(2)}) %collective-permute-start.4) | collective-permute-done | bytes 32800 | tf_op jit(solution)/shard_map/ppermute | solution.py:294
  58.5 1.5 %collective-permute-start.8 = (f32[8,512]{1,0:T(8,128)S(1)}, f32[8,512]{1,0:T(8,128)S(1)}, u32[]{:S(2)}, u32[]{:S(2)}) collective-permute-start(f32[8,512]{1,0:T(8,128)S(1)} %dynamic-slice_bitcast_fusion.1), channel_id=1, source_target_pairs={{0,8},{8,0},{16,24},{24,16},{1,9},{9,1},{17,25},{25,17},{2,10},{10... | collective-permute-start | bytes 49160 | tf_op jit(solution)/shard_map/ppermute | solution.py:294
  60.0 3.3 %collective-permute-done.8 = f32[8,512]{1,0:T(8,128)S(1)} collective-permute-done((f32[8,512]{1,0:T(8,128)S(1)}, f32[8,512]{1,0:T(8,128)S(1)}, u32[]{:S(2)}, u32[]{:S(2)}) %collective-permute-start.8) | collective-permute-done | bytes 16416 | tf_op jit(solution)/shard_map/ppermute | solution.py:294
  63.3 0.6 bitcast_add_fusion.1
  (3 shorter events, 0.0 us)
Async XLA Ops:
  1.9 9.4 %collective-permute-start = (bf16[2,3,6,4,512]{4,3,2,1,0:T(4,128)(2,1)S(1)}, bf16[2,3,6,4,512]{4,3,2,1,0:T(4,128)(2,1)S(1)}, u32[]{:S(2)}, u32[]{:S(2)}) collective-permute-start(bf16[2,3,6,4,512]{4,3,2,1,0:T(4,128)(2,1)S(1)} %get-tuple-element.32), channel_id=1, source_target_pairs={{32,0},{225,1},{226,2},{35,3},{36,4},{229,5},{230,6},{39,7},{40,8}... | collective-permute-start | bytes 442376 | tf_op jit(solution)/shard_map/ppermute | solution.py:241
  3.5 9.8 %collective-permute-start.1 = (bf16[2,3,6,4,512]{4,3,2,1,0:T(4,128)(2,1)S(1)}, bf16[2,3,6,4,512]{4,3,2,1,0:T(4,128)(2,1)S(1)}, u32[]{:S(2)}, u32[]{:S(2)}) collective-permute-start(bf16[2,3,6,4,512]{4,3,2,1,0:T(4,128)(2,1)S(1)} %get-tuple-element.33), channel_id=1, source_target_pairs={{33,0},{226,1},{227,2},{36,3},{37,4},{230,5},{231,6},{40,7},{41,8}... | collective-permute-start | bytes 442376 | tf_op jit(solution)/shard_map/ppermute | solution.py:241
  4.2 9.1 %collective-permute-start.2 = (bf16[2,3,6,4,512]{4,3,2,1,0:T(4,128)(2,1)S(1)}, bf16[2,3,6,4,512]{4,3,2,1,0:T(4,128)(2,1)S(1)}, u32[]{:S(2)}, u32[]{:S(2)}) collective-permute-start(bf16[2,3,6,4,512]{4,3,2,1,0:T(4,128)(2,1)S(1)} %get-tuple-element.34), channel_id=1, source_target_pairs={{1,0},{2,1},{3,2},{4,3},{5,4},{6,5},{7,6},{8,7},{9,8},{10,9},{11,1... | collective-permute-start | bytes 442376 | tf_op jit(solution)/shard_map/ppermute | solution.py:241
  8.4 1.6 %copy-start = (bf16[2048,512]{1,0:T(8,128)(2,1)S(1)}, bf16[2048,512]{1,0:T(8,128)(2,1)}, u32[]{:S(2)}) copy-start(bf16[2048,512]{1,0:T(8,128)(2,1)} %w_ref.1) | copy-start | bytes 6291460
  18.8 3.0 %collective-permute-start.3 = (bf16[1024,512]{1,0:T(8,128)(2,1)S(1)}, bf16[1024,512]{1,0:T(8,128)(2,1)S(1)}, u32[]{:S(2)}, u32[]{:S(2)}) collective-permute-start(bf16[1024,512]{1,0:T(8,128)(2,1)S(1)} %get-tuple-element.40), channel_id=1, source_target_pairs={{0,1},{1,0},{2,3},{3,2},{4,5},{5,4},{6,7},{7,6},{8,9},{9,8},{10,11... | collective-permute-start | bytes 3145736 | tf_op jit(solution)/shard_map/ppermute | solution.py:273
  23.0 26.8 %all-to-all-start = ((bf16[32,32,512]{2,1,0:T(8,128)(2,1)}), bf16[32,32,512]{2,1,0:T(8,128)(2,1)S(1)}, u32[]{:S(2)}, u32[]{:S(2)}) async-start(bf16[32,32,512]{2,1,0:T(8,128)(2,1)} %bitcast.2), calls=%async_computation | async-start | bytes 2097152 | tf_op jit(solution)/shard_map/all_to_all | solution.py:283
  32.2 24.2 %collective-permute-start.5 = (bf16[2,3,6,4,512]{4,3,2,1,0:T(4,128)(2,1)S(1)}, bf16[2,3,6,4,512]{4,3,2,1,0:T(4,128)(2,1)S(1)}, u32[]{:S(2)}, u32[]{:S(2)}) collective-permute-start(bf16[2,3,6,4,512]{4,3,2,1,0:T(4,128)(2,1)S(1)} %get-tuple-element.53), channel_id=1, source_target_pairs={{0,1},{1,2},{2,3},{3,4},{4,5},{5,6},{6,7},{7,8},{8,9},{9,10},{10,1... | collective-permute-start | bytes 442376 | tf_op jit(solution)/shard_map/ppermute | solution.py:241
  32.3 24.1 %collective-permute-start.6 = (bf16[2,3,6,4,512]{4,3,2,1,0:T(4,128)(2,1)S(1)}, bf16[2,3,6,4,512]{4,3,2,1,0:T(4,128)(2,1)S(1)}, u32[]{:S(2)}, u32[]{:S(2)}) collective-permute-start(bf16[2,3,6,4,512]{4,3,2,1,0:T(4,128)(2,1)S(1)} %get-tuple-element.54), channel_id=1, source_target_pairs={{0,32},{1,225},{2,226},{3,35},{4,36},{5,229},{6,230},{7,39},{8,40}... | collective-permute-start | bytes 442376 | tf_op jit(solution)/shard_map/ppermute | solution.py:241
  36.5 19.8 %collective-permute-start.7 = (bf16[2,3,6,4,512]{4,3,2,1,0:T(4,128)(2,1)S(1)}, bf16[2,3,6,4,512]{4,3,2,1,0:T(4,128)(2,1)S(1)}, u32[]{:S(2)}, u32[]{:S(2)}) collective-permute-start(bf16[2,3,6,4,512]{4,3,2,1,0:T(4,128)(2,1)S(1)} %get-tuple-element.55), channel_id=1, source_target_pairs={{0,33},{1,226},{2,227},{3,36},{4,37},{5,230},{6,231},{7,40},{8,41}... | collective-permute-start | bytes 442376 | tf_op jit(solution)/shard_map/ppermute | solution.py:241
  50.0 8.5 %collective-permute-start.4 = (f32[16,512]{1,0:T(8,128)S(1)}, f32[16,512]{1,0:T(8,128)S(1)}, u32[]{:S(2)}, u32[]{:S(2)}) collective-permute-start(f32[16,512]{1,0:T(8,128)S(1)} %dynamic-slice_bitcast_fusion), channel_id=1, source_target_pairs={{0,16},{8,24},{16,0},{24,8},{1,17},{9,25},{17,1},{25,9},{2,18},{10... | collective-permute-start | bytes 98312 | tf_op jit(solution)/shard_map/ppermute | solution.py:294
  58.5 4.7 %collective-permute-start.8 = (f32[8,512]{1,0:T(8,128)S(1)}, f32[8,512]{1,0:T(8,128)S(1)}, u32[]{:S(2)}, u32[]{:S(2)}) collective-permute-start(f32[8,512]{1,0:T(8,128)S(1)} %dynamic-slice_bitcast_fusion.1), channel_id=1, source_target_pairs={{0,8},{8,0},{16,24},{24,16},{1,9},{9,1},{17,25},{25,17},{2,10},{10... | collective-permute-start | bytes 49160 | tf_op jit(solution)/shard_map/ppermute | solution.py:294
